TPU v7x, 512 devices: a whole 4x8x8 slice. The times are simulated.
512 devices in a mesh: heads: 8 (over z_lo, core), tokens: 64 (over x, y, z_hi).
Axes of the slice: x: 4, y: 8, z: 8 (z_hi: 2, z_lo: 4; z = z_hi * 4 + z_lo), core: 2. Of those that a mesh axis runs over, the one named last changes fastest.
Arguments:
- queries: bfloat16 [2, 8192, 2048], P(None, 'tokens', 'heads'), may hold values from -8.5 to 8.5, as said below
- keys: bfloat16 [2, 8192, 2048], P(None, 'tokens', 'heads'), may hold values from -6 to 6
- values: bfloat16 [2, 8192, 2048], P(None, 'tokens', 'heads'), may hold values from -6 to 6
- rates: float32 [2, 8, 8192], P(None, 'heads', 'tokens'), may hold values from 0.05 to 1
- fast_init: bfloat16 [8, 3, 256, 256], P('heads'), may hold values from -0.375 to 0.375
- out_gain: float32 [2048], P('heads'), may hold values from 0.25 to 1.75
Outputs:
- mixed: bfloat16 [2, 8192, 2048], P(None, 'tokens', 'heads')
- final_weights: bfloat16 [8, 3, 256, 256], P('heads')
Inputs may be any that keep to these rules, and one draw needn't show every extreme that they name: queries are real-valued and of order one.
All inputs are finite; a program needn't handle non-finite values.
Results may differ from a plain program's by a relative error of at most 0.0095.
Values may be sent and summed in bfloat16 or wider, within the bound.
No kernel may reach another device: no remote copies, remote signals or barrier semaphores. Data moves between devices by JAX's collectives and lax.ppermute only.
A program may use at most 64 MiB of HBM per device.

v0:
```python
import jax
import jax.numpy as jnp
from jax import lax
from jax.sharding import PartitionSpec as P

D = 2048
NS_STEPS = 2


coef_a = 3.4445
coef_b = -4.775
coef_c = 2.0315
step_size = 0.5


def cut_along(array, dim, peers):
    shape = array.shape
    parts = array.reshape(*shape[:dim], peers, shape[dim] // peers, *shape[dim + 1 :])
    return jnp.moveaxis(parts, dim, 0)


def sum_at_owner(array, axis, dim):
    peers = lax.axis_size(axis)
    parts = lax.all_to_all(cut_along(array, dim, peers), axis, 0, 0, tiled=True)
    return jnp.sum(parts, axis=0)


def from_everyone(array, axis):
    copies = jnp.broadcast_to(array, (lax.axis_size(axis), *array.shape))
    return lax.all_to_all(copies, axis, split_axis=0, concat_axis=0, tiled=True)


def taken_together(array, axis):
    return from_everyone(array, axis).sum(axis=0)


def joined_along(parts, dim):
    parts = jnp.moveaxis(parts, 0, dim)
    shape = parts.shape
    return parts.reshape(*shape[:dim], shape[dim] * shape[dim + 1], *shape[dim + 2 :])


def collect(array, axis, dim):
    parts = from_everyone(array, axis)
    return joined_along(parts, dim)


def newton(current):
    for step in range(NS_STEPS):
        gram = jnp.einsum(
            "hmij,hmkj->hmik", current, current, preferred_element_type=jnp.float32
        ).astype(jnp.bfloat16)
        square = jnp.einsum("hmij,hmjk->hmik", gram, gram, preferred_element_type=jnp.float32)
        mixer = (coef_b * gram.astype(jnp.float32) + coef_c * square).astype(jnp.bfloat16)
        product = jnp.einsum("hmij,hmjk->hmik", mixer, current, preferred_element_type=jnp.float32)
        current = (coef_a * current.astype(jnp.float32) + product).astype(jnp.bfloat16)
    return current


def apply_heads(query, weights):
    gate_q = jnp.einsum("nhd,hde->nhe", query, weights[:, 0], preferred_element_type=jnp.float32)
    up_q = jnp.einsum("nhd,hde->nhe", query, weights[:, 1], preferred_element_type=jnp.float32)
    hidden_q = (jax.nn.silu(gate_q) * up_q).astype(jnp.bfloat16)
    return jnp.einsum("nhd,hde->nhe", hidden_q, weights[:, 2], preferred_element_type=jnp.float32)


def local_grads(key_rows, value_rows, rate, weights):
    gate_k = jnp.einsum("nhd,hde->nhe", key_rows, weights[:, 0], preferred_element_type=jnp.float32)
    up_k = jnp.einsum("nhd,hde->nhe", key_rows, weights[:, 1], preferred_element_type=jnp.float32)
    sig = jax.nn.sigmoid(gate_k)
    hidden = (gate_k * sig * up_k).astype(jnp.bfloat16)
    scaled = (rate.T[:, :, None] * value_rows.astype(jnp.float32)).astype(jnp.bfloat16)
    back = jnp.einsum("nhe,hde->nhd", scaled, weights[:, 2], preferred_element_type=jnp.float32)
    grad_gate = (back * up_k * sig * (1.0 + gate_k * (1.0 - sig))).astype(jnp.bfloat16)
    grad_up = (back * gate_k * sig).astype(jnp.bfloat16)
    g_gate = jnp.einsum("nhd,nhe->hde", key_rows, grad_gate, preferred_element_type=jnp.float32)
    g_up = jnp.einsum("nhd,nhe->hde", key_rows, grad_up, preferred_element_type=jnp.float32)
    g_down = jnp.einsum("nhd,nhe->hde", hidden, scaled, preferred_element_type=jnp.float32)
    return jnp.stack([g_gate, g_up, g_down], axis=1)


def finish(joined, totals, out_gain):
    return (joined / jnp.sqrt(totals[:, None] / D + 1e-06) * out_gain[None, :]).astype(jnp.bfloat16)


def per_device(queries, keys, values, rates, fast_init, out_gain):
    heads_here = fast_init.shape[0]
    head_size = fast_init.shape[2]
    tok_rows = queries.shape[1]
    weights = fast_init
    outputs = []
    joined_all = []
    for block in range(queries.shape[0]):
        query = queries[block].reshape(tok_rows, heads_here, head_size)
        key_rows = keys[block].reshape(tok_rows, heads_here, head_size)
        value_rows = values[block].reshape(tok_rows, heads_here, head_size)
        joined = apply_heads(query, weights).reshape(tok_rows, heads_here * head_size)
        grads = local_grads(key_rows, value_rows, rates[block], weights)
        shares = sum_at_owner(grads, "tokens", 2)
        squares = taken_together(jnp.sum(shares * shares, axis=(2, 3)), "tokens")
        start_rows = (shares / (jnp.sqrt(squares)[:, :, None, None] + 1e-07)).astype(jnp.bfloat16)
        start = collect(start_rows, "tokens", 2)
        update = newton(start)
        weights = (weights.astype(jnp.float32) + step_size * update.astype(jnp.float32)).astype(
            jnp.bfloat16
        )
        joined_all.append(joined)
    stacked = jnp.stack(joined_all, axis=0)
    totals = taken_together(jnp.sum(stacked * stacked, axis=2), "heads")
    outputs = [
        finish(joined_all[index], totals[index], out_gain) for index in range(len(joined_all))
    ]
    return (jnp.stack(outputs, axis=0), weights)


def solution(mesh):
    in_specs = (
        P(None, "tokens", "heads"),
        P(None, "tokens", "heads"),
        P(None, "tokens", "heads"),
        P(None, "heads", "tokens"),
        P("heads", None, None, None),
        P("heads"),
    )
    out_specs = (P(None, "tokens", "heads"), P("heads", None, None, None))
    return jax.shard_map(
        per_device, mesh=mesh, in_specs=in_specs, out_specs=out_specs, check_vma=False
    )
```

profile of v0, /device:TPU:6, one launch (start us, length us, event | category | flops | bytes accessed | tf_op | source)
XLA Modules:
  0.0 187.1 jit_solution(15818449543463330043)
XLA Ops:
  0.6 1.2 convolution_bitcast_fusion.12
  1.9 1.2 multiply_convert_fusion.5
  3.1 0.2 convolution_bitcast_fusion.14
  3.3 0.2 convolution_bitcast_fusion.4
  3.6 0.2 convolution_bitcast_fusion.5
  4.1 0.2 convolution_bitcast_fusion.3
  4.4 0.5 copy.59
  4.9 44.8 %all_to_all.35 = f32[64,1,3,4,256]{4,3,2,1,0:T(4,128)S(1)} all-to-all(f32[64,1,3,4,256]{4,3,2,1,0:T(4,128)S(1)} %copy.59), channel_id=1, replica_groups=mesh['heads'=8,'tokens'=64] {'tokens'}, dimensions={0} | all-to-all | bytes 1572864 | tf_op jit(solution)/shard_map/all_to_all | solution.py:24
  49.8 0.2 reduce_sum.72
  50.1 19.7 %all_to_all.36 = f32[64,1,3]{2,1,0:T(1,128)S(1)} all-to-all(f32[64,1,3]{2,1,0:T(1,128)S(1)} %broadcast_in_dim.19), channel_id=1, replica_groups=mesh['heads'=8,'tokens'=64] {'tokens'}, dimensions={0} | all-to-all | bytes 1536 | tf_op jit(solution)/shard_map/all_to_all | solution.py:30
  69.9 0.1 broadcast_in_dim.20
  70.0 21.8 %all_to_all.37 = bf16[64,1,3,4,256]{4,3,2,1,0:T(4,128)(2,1)S(1)} all-to-all(bf16[64,1,3,4,256]{4,3,2,1,0:T(4,128)(2,1)S(1)} %broadcast_in_dim.20), channel_id=1, replica_groups=mesh['heads'=8,'tokens'=64] {'tokens'}, dimensions={0} | all-to-all | bytes 786432 | tf_op jit(solution)/shard_map/all_to_all | solution.py:30
  91.9 0.1 copy.61
  92.1 0.3 convolution_convert_fusion.3
  92.4 0.4 fusion.8
  92.8 0.3 convolution_convert_fusion.2
  93.1 0.4 fusion.14
  93.6 0.2 convolution_bitcast_fusion.6
  93.8 0.2 multiply_convert_fusion
  94.0 0.2 convolution_bitcast_fusion.8
  94.3 0.2 convolution_bitcast_fusion.1
  94.5 0.2 convolution_bitcast_fusion.2
  95.0 0.2 convolution_bitcast_fusion
  95.3 1.4 copy.67
  96.7 7.1 %all-to-all-start.4 = ((f32[64,1,3,4,256]{4,3,2,1,0:T(4,128)}), f32[64,1,3,4,256]{4,3,2,1,0:T(4,128)S(1)}, u32[]{:S(2)}, u32[]{:S(2)}) async-start(f32[64,1,3,4,256]{4,3,2,1,0:T(4,128)} %copy.67), calls=%async_computation.4 | async-start | bytes 1572864 | tf_op jit(solution)/shard_map/all_to_all | solution.py:24
  103.8 0.2 convolution_bitcast_fusion.17
  104.0 0.4 convolution_bitcast_fusion.15
  104.5 0.2 convolution_bitcast_fusion.11
  104.7 0.4 convolution_bitcast_fusion.9
  105.1 22.3 %all-to-all-done.4 = f32[64,1,3,4,256]{4,3,2,1,0:T(4,128)S(1)} async-done(((f32[64,1,3,4,256]{4,3,2,1,0:T(4,128)}), f32[64,1,3,4,256]{4,3,2,1,0:T(4,128)S(1)}, u32[]{:S(2)}, u32[]{:S(2)}) %all-to-all-start.4) | async-done | bytes 786464 | tf_op jit(solution)/shard_map/all_to_all | solution.py:24
  127.4 0.2 reduce_sum.77
  127.7 0.6 broadcast_in_dim.22
  128.3 7.7 %all-to-all-start.5 = ((f32[64,1,3]{2,1,0:T(1,128)}), f32[64,1,3]{2,1,0:T(1,128)S(1)}, u32[]{:S(2)}, u32[]{:S(2)}) async-start(f32[64,1,3]{2,1,0:T(1,128)} %broadcast_in_dim.22), calls=%async_computation.5 | async-start | bytes 65536 | tf_op jit(solution)/shard_map/all_to_all | solution.py:30
  136.0 0.1 fusion.44
  136.1 12.2 %all-to-all-done.5 = f32[64,1,3]{2,1,0:T(1,128)S(1)} async-done(((f32[64,1,3]{2,1,0:T(1,128)}), f32[64,1,3]{2,1,0:T(1,128)S(1)}, u32[]{:S(2)}, u32[]{:S(2)}) %all-to-all-start.5) | async-done | bytes 800 | tf_op jit(solution)/shard_map/all_to_all | solution.py:30
  148.3 0.6 broadcast_in_dim.21
  148.9 4.6 %all-to-all-start.3 = ((f32[8,2,128]{2,1,0:T(2,128)}), f32[8,2,128]{2,1,0:T(2,128)S(1)}, u32[]{:S(2)}, u32[]{:S(2)}) async-start(f32[8,2,128]{2,1,0:T(2,128)} %broadcast_in_dim.21), calls=%async_computation.3 | async-start | bytes 16384 | tf_op jit(solution)/shard_map/all_to_all | solution.py:30
  153.7 5.4 %all-to-all-done.3 = f32[8,2,128]{2,1,0:T(2,128)S(1)} async-done(((f32[8,2,128]{2,1,0:T(2,128)}), f32[8,2,128]{2,1,0:T(2,128)S(1)}, u32[]{:S(2)}, u32[]{:S(2)}) %all-to-all-start.3) | async-done | bytes 8224 | tf_op jit(solution)/shard_map/all_to_all | solution.py:30
  159.1 0.8 broadcast_in_dim.23
  159.9 6.5 %all-to-all-start.6 = ((bf16[64,1,3,4,256]{4,3,2,1,0:T(4,128)(2,1)}), bf16[64,1,3,4,256]{4,3,2,1,0:T(4,128)(2,1)S(1)}, u32[]{:S(2)}, u32[]{:S(2)}) async-start(bf16[64,1,3,4,256]{4,3,2,1,0:T(4,128)(2,1)} %broadcast_in_dim.23), calls=%async_computation.6 | async-start | bytes 786432 | tf_op jit(solution)/shard_map/all_to_all | solution.py:30
  166.5 0.7 copy-done.4
  167.3 0.7 pad_maximum_fusion
  168.0 16.6 %all-to-all-done.6 = bf16[64,1,3,4,256]{4,3,2,1,0:T(4,128)(2,1)S(1)} async-done(((bf16[64,1,3,4,256]{4,3,2,1,0:T(4,128)(2,1)}), bf16[64,1,3,4,256]{4,3,2,1,0:T(4,128)(2,1)S(1)}, u32[]{:S(2)}, u32[]{:S(2)}) %all-to-all-start.6) | async-done | bytes 393248 | tf_op jit(solution)/shard_map/all_to_all | solution.py:30
  184.6 0.1 copy.69
  184.9 0.3 convolution_convert_fusion.1
  185.2 0.4 fusion.15
  185.6 0.3 convolution_convert_fusion
  185.9 1.2 fusion.21
  (36 shorter events, 1.6 us)
Async XLA Ops:
  0.6 1.2 copy-start.2
  1.8 1.2 copy-start.5
  1.8 1.2 copy-start
  1.8 1.2 copy-start.1
  96.7 7.1 %copy-start.3 = (bf16[2,128,256]{2,1,0:T(8,128)(2,1)S(1)}, bf16[2,128,256]{2,1,0:T(8,128)(2,1)}, u32[]{:S(2)}) copy-start(bf16[2,128,256]{2,1,0:T(8,128)(2,1)} %param.6) | copy-start | bytes 393220
  96.7 30.7 %all-to-all-start.4 = ((f32[64,1,3,4,256]{4,3,2,1,0:T(4,128)}), f32[64,1,3,4,256]{4,3,2,1,0:T(4,128)S(1)}, u32[]{:S(2)}, u32[]{:S(2)}) async-start(f32[64,1,3,4,256]{4,3,2,1,0:T(4,128)} %copy.67), calls=%async_computation.4 | async-start | bytes 1572864 | tf_op jit(solution)/shard_map/all_to_all | solution.py:24
  128.3 20.0 %all-to-all-start.5 = ((f32[64,1,3]{2,1,0:T(1,128)}), f32[64,1,3]{2,1,0:T(1,128)S(1)}, u32[]{:S(2)}, u32[]{:S(2)}) async-start(f32[64,1,3]{2,1,0:T(1,128)} %broadcast_in_dim.22), calls=%async_computation.5 | async-start | bytes 65536 | tf_op jit(solution)/shard_map/all_to_all | solution.py:30
  148.9 10.2 %all-to-all-start.3 = ((f32[8,2,128]{2,1,0:T(2,128)}), f32[8,2,128]{2,1,0:T(2,128)S(1)}, u32[]{:S(2)}, u32[]{:S(2)}) async-start(f32[8,2,128]{2,1,0:T(2,128)} %broadcast_in_dim.21), calls=%async_computation.3 | async-start | bytes 16384 | tf_op jit(solution)/shard_map/all_to_all | solution.py:30
  159.9 24.7 %all-to-all-start.6 = ((bf16[64,1,3,4,256]{4,3,2,1,0:T(4,128)(2,1)}), bf16[64,1,3,4,256]{4,3,2,1,0:T(4,128)(2,1)S(1)}, u32[]{:S(2)}, u32[]{:S(2)}) async-start(bf16[64,1,3,4,256]{4,3,2,1,0:T(4,128)(2,1)} %broadcast_in_dim.23), calls=%async_computation.6 | async-start | bytes 786432 | tf_op jit(solution)/shard_map/all_to_all | solution.py:30
  166.5 0.7 copy-start.4
where the time goes:
time: 188 us; the launch traced here: 187 us
  blocking collectives  86.4 us (46%)
  waiting for transfers between devices  56.5 us (30%)
  starting transfers between devices  25.9 us (14%)
  matrix products  9.55 us (5%)
  local copies, waits for them, and re-layouts  5.8 us (3%)
  other arithmetic  1.91 us (1%)
    all_to_all x1, blocking collectives, sum_at_owner(): parts = lax.all_to_all(cut_along(array, dim, peers), axis, 0, 0, tiled=True)  44.8 us
    all_to_all x2, blocking collectives, from_everyone(): return lax.all_to_all(copies, axis, split_axis=0, concat_axis=0, tiled=True)  41.5 us
    all_to_all x3, waiting for transfers between devices, from_everyone(): return lax.all_to_all(copies, axis, split_axis=0, concat_axis=0, tiled=True)  34.2 us
    all_to_all x1, waiting for transfers between devices, sum_at_owner(): parts = lax.all_to_all(cut_along(array, dim, peers), axis, 0, 0, tiled=True)  22.3 us
    all_to_all x3, starting transfers between devices, from_everyone(): return lax.all_to_all(copies, axis, split_axis=0, concat_axis=0, tiled=True)  18.8 us
    all_to_all x1, starting transfers between devices, sum_at_owner(): parts = lax.all_to_all(cut_along(array, dim, peers), axis, 0, 0, tiled=True)  7.07 us
  transfers between devices with their start and end apart: 4, of which 4 were waited for; matrix products, arithmetic and copies ran while one was open for 1% of the time, Pallas kernels for 0%

commit v1 on v0

v1 whole, which is shorter than its diff:
```python
import jax
import jax.numpy as jnp
from jax import lax
from jax.experimental import pallas as pl
from jax.experimental.pallas import tpu as pltpu
from jax.sharding import PartitionSpec as P

D = 2048
DH = 256
NS_STEPS = 2
PEERS = 8
SHARE = 3 * DH // PEERS

coef_a = 3.4445
coef_b = -4.775
coef_c = 2.0315
step_size = 0.5

F32 = jnp.float32
BF16 = jnp.bfloat16


def token_index(x, y_hi, y_lo, z_hi):
    return ((x * 4 + y_hi) * 2 + y_lo) * 2 + z_hi


NEAR = [
    [token_index(x, y_hi, y_lo, z_hi) for x in range(4) for y_lo in range(2)]
    for y_hi in range(4)
    for z_hi in range(2)
]
FAR = [
    [token_index(x, y_hi, y_lo, z_hi) for y_hi in range(4) for z_hi in range(2)]
    for x in range(4)
    for y_lo in range(2)
]


def exchange(array, groups):
    return lax.all_to_all(array, "tokens", 0, 0, axis_index_groups=groups, tiled=True)


def mm(a, b, ca=1, cb=0):
    return lax.dot_general(a, b, (((ca,), (cb,)), ((), ())), preferred_element_type=F32)


def call(body, out_shape, *args, flops=0, scratch=()):
    outs = out_shape if isinstance(out_shape, (tuple, list)) else [out_shape]
    moved = sum(a.size * a.dtype.itemsize for a in (*args, *outs))
    return pl.pallas_call(
        body,
        out_shape=out_shape,
        in_specs=[pl.BlockSpec(memory_space=pltpu.VMEM)] * len(args),
        out_specs=jax.tree.map(lambda _: pl.BlockSpec(memory_space=pltpu.VMEM), out_shape),
        scratch_shapes=list(scratch),
        compiler_params=pltpu.CompilerParams(vmem_limit_bytes=30 * 2**20),
        cost_estimate=pl.CostEstimate(flops=flops, bytes_accessed=moved, transcendentals=0),
    )(*args)


def scale_rows(rate_row, rows):
    tall = jnp.transpose(jnp.broadcast_to(rate_row, (128, rate_row.shape[1])))
    return (jnp.concatenate([tall, tall], axis=1) * rows.astype(F32)).astype(BF16)


def back_terms(keys, scaled, gate_w, up_w, down_w):
    gate = mm(keys, gate_w)
    up = mm(keys, up_w)
    back = mm(scaled, down_w, 1, 1)
    sig = jax.nn.sigmoid(gate)
    hidden = (gate * sig * up).astype(BF16)
    grad_gate = (back * up * sig * (1.0 + gate * (1.0 - sig))).astype(BF16)
    grad_up = (back * gate * sig).astype(BF16)
    return hidden, grad_gate, grad_up


def put_grads(out_ref, which, grad):
    grad = grad.astype(BF16)
    done = 0
    while done < DH:
        row = which * DH + done
        peer, inside = row // SHARE, row % SHARE
        count = min(SHARE - inside, DH - done)
        out_ref[peer, pl.ds(inside, count)] = grad[done : done + count]
        done += count


def first_kernel(k_ref, v_ref, r_ref, w_ref, grads_ref, ahead_ref):
    keys = k_ref[0]
    scaled = scale_rows(r_ref[0], v_ref[0])
    hidden, grad_gate, grad_up = back_terms(keys, scaled, w_ref[0, 0], w_ref[0, 1], w_ref[0, 2])
    put_grads(grads_ref, 0, mm(keys, grad_gate, 0, 0))
    put_grads(grads_ref, 1, mm(keys, grad_up, 0, 0))
    put_grads(grads_ref, 2, mm(hidden, scaled, 0, 0))
    later_keys = k_ref[1]
    later_scaled = scale_rows(r_ref[1], v_ref[1])
    ahead_ref[0] = later_keys
    ahead_ref[1] = later_scaled


def share_kernel(parts_ref, copies_ref):
    total = parts_ref[0].astype(F32)
    for peer in range(1, PEERS):
        total = total + parts_ref[peer].astype(F32)
    total = total.astype(BF16)
    for peer in range(PEERS):
        copies_ref[peer] = total


def newton_update(grads_ref, w_ref):
    stacked = grads_ref[...].reshape(3, DH, DH)
    current = []
    for m in range(3):
        wide = stacked[m].astype(F32)
        square = jnp.sum(jnp.sum(wide * wide, axis=0, keepdims=True), axis=1, keepdims=True)
        current.append((wide / (jnp.sqrt(square) + 1e-07)).astype(BF16))
    for step in range(NS_STEPS):
        grams = [mm(x, x, 1, 1).astype(BF16) for x in current]
        squares = [mm(a, a) for a in grams]
        mixers = [
            (coef_b * a.astype(F32) + coef_c * s).astype(BF16) for a, s in zip(grams, squares)
        ]
        products = [mm(b, x) for b, x in zip(mixers, current)]
        current = [(coef_a * x.astype(F32) + p).astype(BF16) for x, p in zip(current, products)]
    return [
        (w_ref[0, m].astype(F32) + step_size * current[m].astype(F32)).astype(BF16)
        for m in range(3)
    ]


def middle_kernel(grads_ref, w_ref, ahead_ref, fresh_ref, out_ref, hid_ref, dg_ref, du_ref):
    fresh = newton_update(grads_ref, w_ref)
    for m in range(3):
        fresh_ref[0, m] = fresh[m]
    step = 2
    for start in range(0, PEERS, step):
        keys = ahead_ref[start : start + step, 0].reshape(step * 128, DH)
        scaled = ahead_ref[start : start + step, 1].reshape(step * 128, DH)
        hidden, grad_gate, grad_up = back_terms(
            keys, scaled, fresh_ref[0, 0], fresh_ref[0, 1], fresh_ref[0, 2]
        )
        rows = pl.ds(start * 128, step * 128)
        hid_ref[rows] = hidden
        dg_ref[rows] = grad_gate
        du_ref[rows] = grad_up
    all_keys = ahead_ref[:, 0].reshape(PEERS * 128, DH)
    all_scaled = ahead_ref[:, 1].reshape(PEERS * 128, DH)
    put_grads(out_ref, 0, mm(all_keys, dg_ref[...], 0, 0))
    put_grads(out_ref, 1, mm(all_keys, du_ref[...], 0, 0))
    put_grads(out_ref, 2, mm(hid_ref[...], all_scaled, 0, 0))


def last_kernel(grads_ref, w_ref, fresh_ref):
    fresh = newton_update(grads_ref, w_ref)
    for m in range(3):
        fresh_ref[0, m] = fresh[m]


def query_kernel(q_ref, w0_ref, w1_ref, y_ref, squares_ref):
    for block, w_ref in enumerate((w0_ref, w1_ref)):
        gate = mm(q_ref[block], w_ref[0, 0])
        up = mm(q_ref[block], w_ref[0, 1])
        hidden = (gate * jax.nn.sigmoid(gate) * up).astype(BF16)
        out = mm(hidden, w_ref[0, 2])
        y_ref[block] = out
        sums = jnp.sum(out * out, axis=1, keepdims=True)
        row = jnp.transpose(jnp.broadcast_to(sums, (128, 128)))
        for peer in range(PEERS):
            squares_ref[peer, pl.ds(block, 1)] = row[:1]


def finish_kernel(y_ref, squares_ref, gain_ref, out_ref):
    total = squares_ref[0]
    for peer in range(1, PEERS):
        total = total + squares_ref[peer]
    root = jnp.sqrt(total / D + 1e-06)
    for block in range(2):
        tall = jnp.transpose(jnp.broadcast_to(root[block : block + 1], (128, 128)))
        both = jnp.concatenate([tall, tall], axis=1)
        out_ref[block] = (y_ref[block] / both * gain_ref[...]).astype(BF16)


def shaped(shape, dtype=BF16):
    return jax.ShapeDtypeStruct(shape, dtype)


def per_device(queries, keys, values, rates, fast_init, out_gain):
    pieces = shaped((PEERS, SHARE, DH))
    weights = shaped((1, 3, DH, DH))
    grads, ahead = call(
        first_kernel,
        (pieces, shaped((2, 128, DH))),
        keys, values, rates, fast_init, flops=10**8,
    )
    parts = exchange(grads, NEAR)
    ahead = lax.all_gather(ahead, "tokens", axis=0, axis_index_groups=FAR)
    parts = exchange(call(share_kernel, pieces, parts), FAR)
    whole = exchange(call(share_kernel, pieces, parts), NEAR)
    wide = [pltpu.VMEM((PEERS * 128, DH), BF16)] * 3
    fresh, grads = call(
        middle_kernel, (weights, pieces), whole, fast_init, ahead, flops=14 * 10**8, scratch=wide
    )
    parts = exchange(grads, NEAR)
    y, squares = call(
        query_kernel,
        (shaped((2, 128, DH), F32), shaped((PEERS, 2, 128), F32)),
        queries, fast_init, fresh, flops=10**8,
    )
    squares = lax.all_to_all(squares, "heads", 0, 0, tiled=True)
    whole = exchange(call(share_kernel, pieces, parts), NEAR)
    mixed = call(finish_kernel, shaped((2, 128, DH)), y, squares, out_gain.reshape(1, DH))
    final = call(last_kernel, weights, whole, fresh, flops=6 * 10**8)
    return mixed, final


def solution(mesh):
    in_specs = (
        P(None, "tokens", "heads"),
        P(None, "tokens", "heads"),
        P(None, "tokens", "heads"),
        P(None, "heads", "tokens"),
        P("heads", None, None, None),
        P("heads"),
    )
    out_specs = (P(None, "tokens", "heads"), P("heads", None, None, None))
    return jax.shard_map(
        per_device, mesh=mesh, in_specs=in_specs, out_specs=out_specs, check_vma=False
    )
```

time: 188 us -> 150 us (0.80)
  blocking collectives: 86.4 us -> 29.8 us
  between operations: 1.05 us -> 14.1 us
  Pallas kernels: 0 us -> 10.4 us
  matrix products: 9.55 us -> 0 us
  starting transfers between devices: 25.9 us -> 29.8 us
  other arithmetic: 1.91 us -> 0 us
  waiting for transfers between devices: 56.5 us -> 58.4 us
    all_to_all x3 -> x1, blocking collectives: 86.4 us -> 29.8 us  [exchange(): lax.all_to_all(array, 'tokens', 0, 0, axis_index_groups=groups, tiled=True)]
    all_gather x0 -> x1, waiting for transfers between devices: none -> 38.6 us  [per_device(): ahead = lax.all_gather(ahead, 'tokens', axis=0, axis_index_groups=FAR)]
    all_to_all x4 -> x5, waiting for transfers between devices: 56.5 us -> 19.1 us  [the longest x4 14.4 us: exchange(): lax.all_to_all(array, 'tokens', 0, 0, axis_index_groups=groups, tiled=True)]
    pallas_call x0 -> x8, Pallas kernels: none -> 10.4 us  [call(): pl.pallas_call(body, out_shape=out_shape, in_specs=[pl.BlockSpec(memory_s...]
    dot_general x24 -> x0, matrix products: 9.55 us -> none  [the longest x4 2.43 us: newton(): jnp.einsum('hmij,hmjk->hmik', mixer, current, preferred_element_type=jnp....]
    unnamed x12 -> x16, local copies, waits for them, and re-layouts: 0.7 us -> 5.39 us
    all_to_all x4 -> x5, starting transfers between devices: 25.9 us -> 29.8 us  [the longest x4 26.5 us: exchange(): lax.all_to_all(array, 'tokens', 0, 0, axis_index_groups=groups, tiled=True)]
    broadcast_in_dim x5 -> x0, local copies, waits for them, and re-layouts: 2.22 us -> none  [from_everyone(): copies = jnp.broadcast_to(array, (lax.axis_size(axis), *array.shape))]
  transfers between devices with their start and end apart: 4 -> 6, of which waited for: 4 -> 5; matrix products, arithmetic and copies ran while one was open for 1% -> 0% of each run, Pallas kernels for 0% -> 2%
where the time goes in v1:
time: 150 us; the launch traced here: 148 us
  waiting for transfers between devices  58.4 us (39%)
  starting transfers between devices  29.8 us (20%)
  blocking collectives  29.8 us (20%)
  between operations  14.1 us (9%)
  Pallas kernels  10.4 us (7%)
  local copies, waits for them, and re-layouts  5.39 us (4%)
    all_gather x1, waiting for transfers between devices, per_device(): ahead = lax.all_gather(ahead, 'tokens', axis=0, axis_index_groups=FAR)  38.6 us
    all_to_all x1, blocking collectives, exchange(): lax.all_to_all(array, 'tokens', 0, 0, axis_index_groups=groups, tiled=True)  29.8 us
    all_to_all x4, starting transfers between devices, exchange(): lax.all_to_all(array, 'tokens', 0, 0, axis_index_groups=groups, tiled=True)  26.5 us
    all_to_all x4, waiting for transfers between devices, exchange(): lax.all_to_all(array, 'tokens', 0, 0, axis_index_groups=groups, tiled=True)  14.4 us
    pallas_call x8, Pallas kernels, call(): pl.pallas_call(body, out_shape=out_shape, in_specs=[pl.BlockSpec(memory_s...  10.4 us
    unnamed x16, local copies, waits for them, and re-layouts  5.39 us
    all_to_all x1, waiting for transfers between devices, per_device(): squares = lax.all_to_all(squares, 'heads', 0, 0, tiled=True)  4.73 us
    all_to_all x1, starting transfers between devices, per_device(): squares = lax.all_to_all(squares, 'heads', 0, 0, tiled=True)  3.33 us
  transfers between devices with their start and end apart: 6, of which 5 were waited for; matrix products, arithmetic and copies ran while one was open for 0% of the time, Pallas kernels for 2%

profile of v1, /device:TPU:6, one launch (start us, length us, event | category | flops | bytes accessed | tf_op | source)
XLA Modules:
  0.0 147.9 jit_solution(13711512312036240640)
XLA Ops:
  7.2 0.0 copy-start
  7.2 1.0 copy-done
  8.2 0.0 copy-start.2
  8.2 0.9 copy-done.2
  9.1 0.0 copy-start.3
  9.1 0.9 copy-done.3
  10.0 0.0 copy-start.5
  10.0 0.7 copy-done.5
  10.7 1.3 shard_map.77
  12.0 9.2 %all-to-all-start = ((bf16[8,96,256]{2,1,0:T(8,128)(2,1)}), bf16[8,96,256]{2,1,0:T(8,128)(2,1)S(1)}, u32[]{:S(2)}, u32[]{:S(2)}) async-start(bf16[8,96,256]{2,1,0:T(8,128)(2,1)} %get-tuple-element.8), calls=%async_computation | async-start | bytes 786432 | tf_op jit(solution)/shard_map/all_to_all | solution.py:40
  21.2 0.0 all-gather.3.cloned.1.call-start
  21.2 0.7 all-gather.3.cloned.1.call-update
  21.9 4.9 %all-to-all-done.parts_ref = bf16[8,96,256]{2,1,0:T(8,128)(2,1)S(1)} async-done(((bf16[8,96,256]{2,1,0:T(8,128)(2,1)}), bf16[8,96,256]{2,1,0:T(8,128)(2,1)S(1)}, u32[]{:S(2)}, u32[]{:S(2)}) %all-to-all-start) | async-done | bytes 393248 | tf_op jit(solution)/shard_map/all_to_all | solution.py:40
  26.8 0.1 shard_map.78
  26.9 29.8 %all_to_all.30.parts_ref = bf16[8,96,256]{2,1,0:T(8,128)(2,1)S(1)} all-to-all(bf16[8,96,256]{2,1,0:T(8,128)(2,1)S(1)} %shard_map.78), channel_id=1, replica_groups={{0,1,4,5,8,9,12,13},{2,3,6,7,10,11,14,15},{16,17,20,21,24,25,28,29},{18..., dimensions={0} | all-to-all | bytes 786432 | tf_op jit(solution)/shard_map/all_to_all | solution.py:40
  56.6 0.8 shard_map.79
  57.4 0.0 copy-start.1
  57.4 6.5 %all-to-all-start.2 = ((bf16[8,96,256]{2,1,0:T(8,128)(2,1)}), bf16[8,96,256]{2,1,0:T(8,128)(2,1)S(1)}, u32[]{:S(2)}, u32[]{:S(2)}) async-start(bf16[8,96,256]{2,1,0:T(8,128)(2,1)} %shard_map.79), calls=%async_computation.2 | async-start | bytes 786432 | tf_op jit(solution)/shard_map/all_to_all | solution.py:40
  64.0 38.6 %all-gather.3.cloned.1.call-done = bf16[16,128,256]{2,1,0:T(8,128)(2,1)} async-done(((bf16[2,128,256]{2,1,0:T(8,128)(2,1)}), bf16[16,128,256]{2,1,0:T(8,128)(2,1)}) %all-gather.3.cloned.1.call-update) | async-done | bytes 1048592 | tf_op jit(solution)/shard_map/all_gather | solution.py:196
  102.5 0.0 all-to-all-done.2.grads_ref
  102.5 0.0 copy-done.1
  102.6 0.0 copy-start.7
  102.6 1.2 copy-done.7
  103.8 3.4 %shard_map.80 = (bf16[1,3,256,256]{3,2,1,0:T(8,128)(2,1)S(1)}, bf16[8,96,256]{2,1,0:T(8,128)(2,1)}) custom-call(bf16[8,96,256]{2,1,0:T(8,128)(2,1)S(1)} %all-to-all-done.2.grads_ref, bf16[1,3,256,256]{3,2,1,0:T(8,128)(2,1)S(1)} %copy-done.1, bf16[8,2,128,256]{3,2,1,0:T(8,128)(2,1)S(1)} %bitcast.3), custom_call_target="tpu_custom_call" | custom-call | flops 1400000000 | bytes 2621440 | tf_op jit(solution)/shard_map/pallas_call | solution.py:50
  107.2 0.0 copy-start.4
  107.2 4.9 %all-to-all-start.4 = ((bf16[8,96,256]{2,1,0:T(8,128)(2,1)}), bf16[8,96,256]{2,1,0:T(8,128)(2,1)S(1)}, u32[]{:S(2)}, u32[]{:S(2)}) async-start(bf16[8,96,256]{2,1,0:T(8,128)(2,1)} %get-tuple-element.13), calls=%async_computation.4 | async-start | bytes 786432 | tf_op jit(solution)/shard_map/all_to_all | solution.py:40
  112.1 0.0 copy-done.4
  112.1 1.2 shard_map.81
  113.3 4.4 %all-to-all-done.4.parts_ref = bf16[8,96,256]{2,1,0:T(8,128)(2,1)S(1)} async-done(((bf16[8,96,256]{2,1,0:T(8,128)(2,1)}), bf16[8,96,256]{2,1,0:T(8,128)(2,1)S(1)}, u32[]{:S(2)}, u32[]{:S(2)}) %all-to-all-start.4) | async-done | bytes 393248 | tf_op jit(solution)/shard_map/all_to_all | solution.py:40
  117.7 3.3 %all-to-all-start.3 = ((f32[8,2,128]{2,1,0:T(2,128)}), f32[8,2,128]{2,1,0:T(2,128)S(1)}, u32[]{:S(2)}, u32[]{:S(2)}) async-start(f32[8,2,128]{2,1,0:T(2,128)} %get-tuple-element.12), calls=%async_computation.3 | async-start | bytes 16384 | tf_op jit(solution)/shard_map/all_to_all | solution.py:209
  121.1 0.8 shard_map.83
  121.9 4.7 %all-to-all-done.3.squares_ref = f32[8,2,128]{2,1,0:T(2,128)S(1)} async-done(((f32[8,2,128]{2,1,0:T(2,128)}), f32[8,2,128]{2,1,0:T(2,128)S(1)}, u32[]{:S(2)}, u32[]{:S(2)}) %all-to-all-start.3) | async-done | bytes 8224 | tf_op jit(solution)/shard_map/all_to_all | solution.py:209
  126.6 5.8 %all-to-all-start.5 = ((bf16[8,96,256]{2,1,0:T(8,128)(2,1)}), bf16[8,96,256]{2,1,0:T(8,128)(2,1)S(1)}, u32[]{:S(2)}, u32[]{:S(2)}) async-start(bf16[8,96,256]{2,1,0:T(8,128)(2,1)} %shard_map.83), calls=%async_computation.5 | async-start | bytes 786432 | tf_op jit(solution)/shard_map/all_to_all | solution.py:40
  132.4 0.0 copy-start.6
  132.4 0.7 copy-done.6
  133.1 0.8 shard_map.82
  133.8 5.1 %all-to-all-done.5.grads_ref = bf16[8,96,256]{2,1,0:T(8,128)(2,1)S(1)} async-done(((bf16[8,96,256]{2,1,0:T(8,128)(2,1)}), bf16[8,96,256]{2,1,0:T(8,128)(2,1)S(1)}, u32[]{:S(2)}, u32[]{:S(2)}) %all-to-all-start.5) | async-done | bytes 393248 | tf_op jit(solution)/shard_map/all_to_all | solution.py:40
  138.9 2.1 %shard_map.84 = bf16[1,3,256,256]{3,2,1,0:T(8,128)(2,1)} custom-call(bf16[8,96,256]{2,1,0:T(8,128)(2,1)S(1)} %all-to-all-done.5.grads_ref, bf16[1,3,256,256]{3,2,1,0:T(8,128)(2,1)S(1)} %get-tuple-element.10.w1_ref.w_ref), custom_call_target="tpu_custom_call" | custom-call | flops 600000000 | bytes 1179648 | tf_op jit(solution)/shard_map/pallas_call | solution.py:50
Async XLA Ops:
  7.2 1.0 copy-start
  8.2 0.9 copy-start.2
  9.1 0.9 copy-start.3
  10.0 0.7 copy-start.5
  12.0 14.8 %all-to-all-start = ((bf16[8,96,256]{2,1,0:T(8,128)(2,1)}), bf16[8,96,256]{2,1,0:T(8,128)(2,1)S(1)}, u32[]{:S(2)}, u32[]{:S(2)}) async-start(bf16[8,96,256]{2,1,0:T(8,128)(2,1)} %get-tuple-element.8), calls=%async_computation | async-start | bytes 786432 | tf_op jit(solution)/shard_map/all_to_all | solution.py:40
  21.2 81.3 %all-gather.3.cloned.1.call-start = ((), (), s32[]{:S(2)}) async-start(), calls=%async_computation.6 | async-start | bytes 1179648 | tf_op jit(solution)/shard_map/all_gather | solution.py:196
  57.4 45.1 %copy-start.1 = (bf16[1,3,256,256]{3,2,1,0:T(8,128)(2,1)S(1)}, bf16[1,3,256,256]{3,2,1,0:T(8,128)(2,1)}, u32[]{:S(2)}) copy-start(bf16[1,3,256,256]{3,2,1,0:T(8,128)(2,1)} %w0_ref.1) | copy-start | bytes 1179652
  57.4 45.1 %all-to-all-start.2 = ((bf16[8,96,256]{2,1,0:T(8,128)(2,1)}), bf16[8,96,256]{2,1,0:T(8,128)(2,1)S(1)}, u32[]{:S(2)}, u32[]{:S(2)}) async-start(bf16[8,96,256]{2,1,0:T(8,128)(2,1)} %shard_map.79), calls=%async_computation.2 | async-start | bytes 786432 | tf_op jit(solution)/shard_map/all_to_all | solution.py:40
  102.6 1.2 copy-start.7
  107.2 4.9 %copy-start.4 = (bf16[2,128,256]{2,1,0:T(8,128)(2,1)S(1)}, bf16[2,128,256]{2,1,0:T(8,128)(2,1)}, u32[]{:S(2)}) copy-start(bf16[2,128,256]{2,1,0:T(8,128)(2,1)} %q_ref.1) | copy-start | bytes 393220
  107.2 10.5 %all-to-all-start.4 = ((bf16[8,96,256]{2,1,0:T(8,128)(2,1)}), bf16[8,96,256]{2,1,0:T(8,128)(2,1)S(1)}, u32[]{:S(2)}, u32[]{:S(2)}) async-start(bf16[8,96,256]{2,1,0:T(8,128)(2,1)} %get-tuple-element.13), calls=%async_computation.4 | async-start | bytes 786432 | tf_op jit(solution)/shard_map/all_to_all | solution.py:40
  117.7 8.9 %all-to-all-start.3 = ((f32[8,2,128]{2,1,0:T(2,128)}), f32[8,2,128]{2,1,0:T(2,128)S(1)}, u32[]{:S(2)}, u32[]{:S(2)}) async-start(f32[8,2,128]{2,1,0:T(2,128)} %get-tuple-element.12), calls=%async_computation.3 | async-start | bytes 16384 | tf_op jit(solution)/shard_map/all_to_all | solution.py:209
  126.6 12.3 %all-to-all-start.5 = ((bf16[8,96,256]{2,1,0:T(8,128)(2,1)}), bf16[8,96,256]{2,1,0:T(8,128)(2,1)S(1)}, u32[]{:S(2)}, u32[]{:S(2)}) async-start(bf16[8,96,256]{2,1,0:T(8,128)(2,1)} %shard_map.83), calls=%async_computation.5 | async-start | bytes 786432 | tf_op jit(solution)/shard_map/all_to_all | solution.py:40
  132.4 0.7 copy-start.6
Sparse Core Ops, SparseCore 0:
  25.8 76.7 all-gather.2

commit v2 on v1

--- a/solution.py
+++ b/solution.py
@@ -44,16 +44,16 @@
     return lax.dot_general(a, b, (((ca,), (cb,)), ((), ())), preferred_element_type=F32)
 
 
-def call(body, out_shape, *args, flops=0, scratch=()):
+def call(body, out_shape, *args, flops=0, scratch=(), space=pltpu.VMEM, limit=30):
     outs = out_shape if isinstance(out_shape, (tuple, list)) else [out_shape]
     moved = sum(a.size * a.dtype.itemsize for a in (*args, *outs))
     return pl.pallas_call(
         body,
         out_shape=out_shape,
-        in_specs=[pl.BlockSpec(memory_space=pltpu.VMEM)] * len(args),
+        in_specs=[pl.BlockSpec(memory_space=space)] * len(args),
         out_specs=jax.tree.map(lambda _: pl.BlockSpec(memory_space=pltpu.VMEM), out_shape),
         scratch_shapes=list(scratch),
-        compiler_params=pltpu.CompilerParams(vmem_limit_bytes=30 * 2**20),
+        compiler_params=pltpu.CompilerParams(vmem_limit_bytes=limit * 2**20),
         cost_estimate=pl.CostEstimate(flops=flops, bytes_accessed=moved, transcendentals=0),
     )(*args)
 
@@ -85,17 +85,22 @@
         done += count
 
 
-def first_kernel(k_ref, v_ref, r_ref, w_ref, grads_ref, ahead_ref):
-    keys = k_ref[0]
-    scaled = scale_rows(r_ref[0], v_ref[0])
-    hidden, grad_gate, grad_up = back_terms(keys, scaled, w_ref[0, 0], w_ref[0, 1], w_ref[0, 2])
+def local_grads(keys, scaled, gate_w, up_w, down_w, grads_ref):
+    hidden, grad_gate, grad_up = back_terms(keys, scaled, gate_w, up_w, down_w)
     put_grads(grads_ref, 0, mm(keys, grad_gate, 0, 0))
     put_grads(grads_ref, 1, mm(keys, grad_up, 0, 0))
     put_grads(grads_ref, 2, mm(hidden, scaled, 0, 0))
-    later_keys = k_ref[1]
-    later_scaled = scale_rows(r_ref[1], v_ref[1])
-    ahead_ref[0] = later_keys
-    ahead_ref[1] = later_scaled
+
+
+def first_kernel(k_hbm, v_hbm, r_hbm, w_hbm, grads_ref, k_ref, v_ref, r_ref, w_ref, sems):
+    pairs = ((w_hbm, w_ref), (k_hbm.at[0], k_ref), (v_hbm.at[0], v_ref), (r_hbm.at[0], r_ref))
+    copies = [pltpu.make_async_copy(a, b, sems.at[n]) for n, (a, b) in enumerate(pairs)]
+    for copy in copies:
+        copy.start()
+    for copy in copies:
+        copy.wait()
+    scaled = scale_rows(r_ref[...], v_ref[...])
+    local_grads(k_ref[...], scaled, w_ref[0, 0], w_ref[0, 1], w_ref[0, 2], grads_ref)
 
 
 def share_kernel(parts_ref, copies_ref):
@@ -128,26 +133,12 @@
     ]
 
 
-def middle_kernel(grads_ref, w_ref, ahead_ref, fresh_ref, out_ref, hid_ref, dg_ref, du_ref):
+def middle_kernel(grads_ref, w_ref, k_ref, v_ref, r_ref, fresh_ref, out_ref):
     fresh = newton_update(grads_ref, w_ref)
     for m in range(3):
         fresh_ref[0, m] = fresh[m]
-    step = 2
-    for start in range(0, PEERS, step):
-        keys = ahead_ref[start : start + step, 0].reshape(step * 128, DH)
-        scaled = ahead_ref[start : start + step, 1].reshape(step * 128, DH)
-        hidden, grad_gate, grad_up = back_terms(
-            keys, scaled, fresh_ref[0, 0], fresh_ref[0, 1], fresh_ref[0, 2]
-        )
-        rows = pl.ds(start * 128, step * 128)
-        hid_ref[rows] = hidden
-        dg_ref[rows] = grad_gate
-        du_ref[rows] = grad_up
-    all_keys = ahead_ref[:, 0].reshape(PEERS * 128, DH)
-    all_scaled = ahead_ref[:, 1].reshape(PEERS * 128, DH)
-    put_grads(out_ref, 0, mm(all_keys, dg_ref[...], 0, 0))
-    put_grads(out_ref, 1, mm(all_keys, du_ref[...], 0, 0))
-    put_grads(out_ref, 2, mm(hid_ref[...], all_scaled, 0, 0))
+    scaled = scale_rows(r_ref[1], v_ref[1])
+    local_grads(k_ref[1], scaled, fresh[0], fresh[1], fresh[2], out_ref)
 
 
 def last_kernel(grads_ref, w_ref, fresh_ref):
@@ -164,16 +155,11 @@
         out = mm(hidden, w_ref[0, 2])
         y_ref[block] = out
         sums = jnp.sum(out * out, axis=1, keepdims=True)
-        row = jnp.transpose(jnp.broadcast_to(sums, (128, 128)))
-        for peer in range(PEERS):
-            squares_ref[peer, pl.ds(block, 1)] = row[:1]
+        squares_ref[pl.ds(block, 1)] = jnp.transpose(jnp.broadcast_to(sums, (128, 128)))[:1]
 
 
 def finish_kernel(y_ref, squares_ref, gain_ref, out_ref):
-    total = squares_ref[0]
-    for peer in range(1, PEERS):
-        total = total + squares_ref[peer]
-    root = jnp.sqrt(total / D + 1e-06)
+    root = jnp.sqrt(squares_ref[...] / D + 1e-06)
     for block in range(2):
         tall = jnp.transpose(jnp.broadcast_to(root[block : block + 1], (128, 128)))
         both = jnp.concatenate([tall, tall], axis=1)
@@ -184,30 +170,51 @@
     return jax.ShapeDtypeStruct(shape, dtype)
 
 
+def add_partner(squares, bit):
+    pairs = [(h, h ^ bit) for h in range(8)]
+    return squares + lax.ppermute(squares, "heads", pairs)
+
+
+def reduced(grads, beside=lambda: None):
+    pieces = shaped((PEERS, SHARE, DH))
+    aside = beside()
+    parts, aside = lax.optimization_barrier((exchange(grads, NEAR), aside))
+    parts = exchange(call(share_kernel, pieces, parts), FAR)
+    if aside is not None:
+        parts, aside = lax.optimization_barrier((parts, (aside[0], add_partner(aside[1], 2))))
+    whole = exchange(call(share_kernel, pieces, parts), NEAR)
+    if aside is None:
+        return whole
+    return whole, aside[0], add_partner(aside[1], 4)
+
+
 def per_device(queries, keys, values, rates, fast_init, out_gain):
     pieces = shaped((PEERS, SHARE, DH))
     weights = shaped((1, 3, DH, DH))
-    grads, ahead = call(
-        first_kernel,
-        (pieces, shaped((2, 128, DH))),
-        keys, values, rates, fast_init, flops=10**8,
-    )
-    parts = exchange(grads, NEAR)
-    ahead = lax.all_gather(ahead, "tokens", axis=0, axis_index_groups=FAR)
-    parts = exchange(call(share_kernel, pieces, parts), FAR)
-    whole = exchange(call(share_kernel, pieces, parts), NEAR)
-    wide = [pltpu.VMEM((PEERS * 128, DH), BF16)] * 3
+    inputs = [
+        pltpu.VMEM((1, 3, DH, DH), BF16),
+        pltpu.VMEM((128, DH), BF16),
+        pltpu.VMEM((128, DH), BF16),
+        pltpu.VMEM((1, 128), F32),
+    ]
+    grads = call(
+        first_kernel, pieces, keys, values, rates, fast_init, flops=10**8,
+        scratch=[*inputs[1:], inputs[0], pltpu.SemaphoreType.DMA((4,))], space=pl.ANY, limit=58,
+    )
+    whole = reduced(grads)
     fresh, grads = call(
-        middle_kernel, (weights, pieces), whole, fast_init, ahead, flops=14 * 10**8, scratch=wide
-    )
-    parts = exchange(grads, NEAR)
-    y, squares = call(
-        query_kernel,
-        (shaped((2, 128, DH), F32), shaped((PEERS, 2, 128), F32)),
-        queries, fast_init, fresh, flops=10**8,
-    )
-    squares = lax.all_to_all(squares, "heads", 0, 0, tiled=True)
-    whole = exchange(call(share_kernel, pieces, parts), NEAR)
+        middle_kernel, (weights, pieces), whole, fast_init, keys, values, rates, flops=7 * 10**8
+    )
+
+    def outputs():
+        y, squares = call(
+            query_kernel,
+            (shaped((2, 128, DH), F32), shaped((2, 128), F32)),
+            queries, fast_init, fresh, flops=10**8,
+        )
+        return y, add_partner(squares, 1)
+
+    whole, y, squares = reduced(grads, outputs)
     mixed = call(finish_kernel, shaped((2, 128, DH)), y, squares, out_gain.reshape(1, DH))
     final = call(last_kernel, weights, whole, fresh, flops=6 * 10**8)
     return mixed, final

time: 150 us -> 110 us (0.73)
  waiting for transfers between devices: 58.4 us -> 16.9 us
  blocking collectives: 29.8 us -> 54.6 us
  between operations: 14.1 us -> 0.72 us
  local copies, waits for them, and re-layouts: 5.39 us -> 0.71 us
  starting transfers between devices: 29.8 us -> 26 us
    all_gather x1 -> x0, waiting for transfers between devices: 38.6 us -> none  [per_device(): ahead = lax.all_gather(ahead, 'tokens', axis=0, axis_index_groups=FAR)]
    all_to_all x1 -> x3, blocking collectives: 29.8 us -> 54.6 us  [exchange(): lax.all_to_all(array, 'tokens', 0, 0, axis_index_groups=groups, tiled=True)]
    all_to_all x4 -> x3, starting transfers between devices: 26.5 us -> 16.3 us  [exchange(): lax.all_to_all(array, 'tokens', 0, 0, axis_index_groups=groups, tiled=True)]
    ppermute x0 -> x3, starting transfers between devices: none -> 9.68 us  [add_partner(): return squares + lax.ppermute(squares, 'heads', pairs)]
    ppermute x0 -> x3, waiting for transfers between devices: none -> 5.18 us  [add_partner(): return squares + lax.ppermute(squares, 'heads', pairs)]
    all_to_all x1 -> x0, waiting for transfers between devices: 4.73 us -> none  [per_device(): squares = lax.all_to_all(squares, 'heads', 0, 0, tiled=True)]
    unnamed x16 -> x12, local copies, waits for them, and re-layouts: 5.39 us -> 0.71 us
    all_to_all x1 -> x0, starting transfers between devices: 3.33 us -> none  [per_device(): squares = lax.all_to_all(squares, 'heads', 0, 0, tiled=True)]
  transfers between devices with their start and end apart: 6 -> 6, of which waited for: 5 -> 5; matrix products, arithmetic and copies ran while one was open for 0% -> 0% of each run, Pallas kernels for 2% -> 1%
where the time goes in v2:
time: 110 us; the launch traced here: 109 us
  blocking collectives  54.6 us (50%)
  starting transfers between devices  26 us (24%)
  waiting for transfers between devices  16.9 us (15%)
  Pallas kernels  10.1 us (9%)
    all_to_all x3, blocking collectives, exchange(): lax.all_to_all(array, 'tokens', 0, 0, axis_index_groups=groups, tiled=True)  54.6 us
    all_to_all x3, starting transfers between devices, exchange(): lax.all_to_all(array, 'tokens', 0, 0, axis_index_groups=groups, tiled=True)  16.3 us
    all_to_all x3, waiting for transfers between devices, exchange(): lax.all_to_all(array, 'tokens', 0, 0, axis_index_groups=groups, tiled=True)  11.7 us
    pallas_call x9, Pallas kernels, call(): pl.pallas_call(body, out_shape=out_shape, in_specs=[pl.BlockSpec(memory_s...  10.1 us
    ppermute x3, starting transfers between devices, add_partner(): return squares + lax.ppermute(squares, 'heads', pairs)  9.68 us
    ppermute x3, waiting for transfers between devices, add_partner(): return squares + lax.ppermute(squares, 'heads', pairs)  5.18 us
  transfers between devices with their start and end apart: 6, of which 5 were waited for; matrix products, arithmetic and copies ran while one was open for 0% of the time, Pallas kernels for 1%

profile of v2, /device:TPU:6, one launch (start us, length us, event | category | flops | bytes accessed | tf_op | source)
XLA Modules:
  0.0 109.0 jit_solution(3680615205631724140)
XLA Ops:
  0.6 2.3 %shard_map.77 = bf16[8,96,256]{2,1,0:T(8,128)(2,1)} custom-call(bf16[2,128,256]{2,1,0:T(8,128)(2,1)} %k_ref.1, bf16[2,128,256]{2,1,0:T(8,128)(2,1)} %v_ref.1, f32[2,1,128]{2,1,0:T(1,128)} %r_ref.1, bf16[1,3,256,256]{3,2,1,0:T(8,128)(2,1)} %w0_ref.1), custom_call_target="tpu_custom_call" | custom-call | flops 100000000 | bytes 1049600 | tf_op jit(solution)/shard_map/pallas_call | solution.py:50
  3.0 15.1 %all_to_all.30.parts_ref = bf16[8,96,256]{2,1,0:T(8,128)(2,1)S(1)} all-to-all(bf16[8,96,256]{2,1,0:T(8,128)(2,1)} %shard_map.77), channel_id=1, replica_groups={{0,2,16,18,32,34,48,50},{1,3,17,19,33,35,49,51},{4,6,20,22,36,38,52,54}..., dimensions={0} | all-to-all | bytes 786432 | tf_op jit(solution)/shard_map/all_to_all | solution.py:40
  18.0 0.1 shard_map.78
  18.1 27.9 %all_to_all.31.parts_ref = bf16[8,96,256]{2,1,0:T(8,128)(2,1)S(1)} all-to-all(bf16[8,96,256]{2,1,0:T(8,128)(2,1)S(1)} %shard_map.78), channel_id=1, replica_groups={{0,1,4,5,8,9,12,13},{2,3,6,7,10,11,14,15},{16,17,20,21,24,25,28,29},{18..., dimensions={0} | all-to-all | bytes 786432 | tf_op jit(solution)/shard_map/all_to_all | solution.py:40
  46.0 0.1 shard_map.79
  46.1 0.0 copy-start
  46.1 0.0 copy-start.1
  46.1 0.0 copy-start.2
  46.1 0.0 copy-start.4
  46.1 11.6 %all_to_all.32.grads_ref = bf16[8,96,256]{2,1,0:T(8,128)(2,1)S(1)} all-to-all(bf16[8,96,256]{2,1,0:T(8,128)(2,1)S(1)} %shard_map.79), channel_id=1, replica_groups={{0,2,16,18,32,34,48,50},{1,3,17,19,33,35,49,51},{4,6,20,22,36,38,52,54}..., dimensions={0} | all-to-all | bytes 786432 | tf_op jit(solution)/shard_map/all_to_all | solution.py:40
  57.7 0.0 copy-done
  57.7 0.0 copy-done.1
  57.7 0.0 copy-done.2
  57.7 0.0 copy-done.4
  57.8 2.6 %shard_map.80 = (bf16[1,3,256,256]{3,2,1,0:T(8,128)(2,1)S(1)}, bf16[8,96,256]{2,1,0:T(8,128)(2,1)}) custom-call(bf16[8,96,256]{2,1,0:T(8,128)(2,1)S(1)} %all_to_all.32.grads_ref, bf16[1,3,256,256]{3,2,1,0:T(8,128)(2,1)S(1)} %copy-done, bf16[2,128,256]{2,1,0:T(8,128)(2,1)S(1)} %copy-done.1, bf16[2,128,256]{2,1,0:T(8,128)(2,1)S(1)} %copy-done.2, ...), custom_call_target="tpu_custom_call" | custom-call | flops 700000000 | bytes 1836032 | tf_op jit(solution)/shard_map/pallas_call | solution.py:50
  60.3 0.0 copy-start.3
  60.3 5.8 %all-to-all-start.3 = ((bf16[8,96,256]{2,1,0:T(8,128)(2,1)}), bf16[8,96,256]{2,1,0:T(8,128)(2,1)S(1)}, u32[]{:S(2)}, u32[]{:S(2)}) async-start(bf16[8,96,256]{2,1,0:T(8,128)(2,1)} %get-tuple-element.12), calls=%async_computation.3 | async-start | bytes 786432 | tf_op jit(solution)/shard_map/all_to_all | solution.py:40
  66.1 0.0 copy-done.3
  66.1 0.6 shard_map.81
  66.7 1.9 %collective-permute-start = (f32[2,128]{1,0:T(2,128)S(1)}, f32[2,128]{1,0:T(2,128)S(1)}, u32[]{:S(2)}, u32[]{:S(2)}) collective-permute-start(f32[2,128]{1,0:T(2,128)S(1)} %get-tuple-element.15), channel_id=1, source_target_pairs={{0,64},{64,0},{128,192},{192,128},{256,320},{320,256},{384,448},{4... | collective-permute-start | bytes 3080 | tf_op jit(solution)/shard_map/ppermute | solution.py:175
  68.6 1.1 %collective-permute-done = f32[2,128]{1,0:T(2,128)S(1)} collective-permute-done((f32[2,128]{1,0:T(2,128)S(1)}, f32[2,128]{1,0:T(2,128)S(1)}, u32[]{:S(2)}, u32[]{:S(2)}) %collective-permute-start) | collective-permute-done | bytes 1056 | tf_op jit(solution)/shard_map/ppermute | solution.py:175
  69.7 2.0 %all-to-all-done.3.parts_ref = bf16[8,96,256]{2,1,0:T(8,128)(2,1)S(1)} async-done(((bf16[8,96,256]{2,1,0:T(8,128)(2,1)}), bf16[8,96,256]{2,1,0:T(8,128)(2,1)S(1)}, u32[]{:S(2)}, u32[]{:S(2)}) %all-to-all-start.3) | async-done | bytes 393248 | tf_op jit(solution)/shard_map/all_to_all | solution.py:40
  71.7 0.8 shard_map.82
  72.5 3.7 %all-to-all-start.4 = ((bf16[8,96,256]{2,1,0:T(8,128)(2,1)}), bf16[8,96,256]{2,1,0:T(8,128)(2,1)S(1)}, u32[]{:S(2)}, u32[]{:S(2)}) async-start(bf16[8,96,256]{2,1,0:T(8,128)(2,1)} %shard_map.82), calls=%async_computation.4 | async-start | bytes 786432 | tf_op jit(solution)/shard_map/all_to_all | solution.py:40
  76.2 3.3 %collective-permute-start.1 = (f32[2,128]{1,0:T(2,128)S(1)}, f32[2,128]{1,0:T(2,128)S(1)}, u32[]{:S(2)}, u32[]{:S(2)}) collective-permute-start(f32[2,128]{1,0:T(2,128)S(1)} %add.9), channel_id=1, source_target_pairs={{0,128},{64,192},{128,0},{192,64},{256,384},{320,448},{384,256},{4... | collective-permute-start | bytes 3080 | tf_op jit(solution)/shard_map/ppermute | solution.py:175
  79.5 2.2 %collective-permute-done.1 = f32[2,128]{1,0:T(2,128)S(1)} collective-permute-done((f32[2,128]{1,0:T(2,128)S(1)}, f32[2,128]{1,0:T(2,128)S(1)}, u32[]{:S(2)}, u32[]{:S(2)}) %collective-permute-start.1) | collective-permute-done | bytes 1056 | tf_op jit(solution)/shard_map/ppermute | solution.py:175
  81.7 9.7 %all-to-all-done.4.parts_ref = bf16[8,96,256]{2,1,0:T(8,128)(2,1)S(1)} async-done(((bf16[8,96,256]{2,1,0:T(8,128)(2,1)}), bf16[8,96,256]{2,1,0:T(8,128)(2,1)S(1)}, u32[]{:S(2)}, u32[]{:S(2)}) %all-to-all-start.4) | async-done | bytes 393248 | tf_op jit(solution)/shard_map/all_to_all | solution.py:40
  91.4 0.8 shard_map.84
  92.2 6.9 %all-to-all-start.5 = ((bf16[8,96,256]{2,1,0:T(8,128)(2,1)}), bf16[8,96,256]{2,1,0:T(8,128)(2,1)S(1)}, u32[]{:S(2)}, u32[]{:S(2)}) async-start(bf16[8,96,256]{2,1,0:T(8,128)(2,1)} %shard_map.84), calls=%async_computation.5 | async-start | bytes 786432 | tf_op jit(solution)/shard_map/all_to_all | solution.py:40
  99.1 4.4 %collective-permute-start.2 = (f32[2,128]{1,0:T(2,128)S(1)}, f32[2,128]{1,0:T(2,128)S(1)}, u32[]{:S(2)}, u32[]{:S(2)}) collective-permute-start(f32[2,128]{1,0:T(2,128)S(1)} %add.10), channel_id=1, source_target_pairs={{0,256},{64,320},{128,384},{192,448},{256,0},{320,64},{384,128},{4... | collective-permute-start | bytes 3080 | tf_op jit(solution)/shard_map/ppermute | solution.py:175
  103.6 1.9 %collective-permute-done.2 = f32[2,128]{1,0:T(2,128)S(1)} collective-permute-done((f32[2,128]{1,0:T(2,128)S(1)}, f32[2,128]{1,0:T(2,128)S(1)}, u32[]{:S(2)}, u32[]{:S(2)}) %collective-permute-start.2) | collective-permute-done | bytes 1056 | tf_op jit(solution)/shard_map/ppermute | solution.py:175
  105.5 0.0 copy-start.5
  105.5 0.7 copy-done.5
  106.2 0.8 shard_map.83
  106.9 0.0 all-to-all-done.5.grads_ref
  106.9 2.1 %shard_map.85 = bf16[1,3,256,256]{3,2,1,0:T(8,128)(2,1)} custom-call(bf16[8,96,256]{2,1,0:T(8,128)(2,1)S(1)} %all-to-all-done.5.grads_ref, bf16[1,3,256,256]{3,2,1,0:T(8,128)(2,1)S(1)} %get-tuple-element.13.w1_ref.w_ref), custom_call_target="tpu_custom_call" | custom-call | flops 600000000 | bytes 1179648 | tf_op jit(solution)/shard_map/pallas_call | solution.py:50
  (3 shorter events, 0.0 us)
Async XLA Ops:
  46.1 11.7 %copy-start = (bf16[1,3,256,256]{3,2,1,0:T(8,128)(2,1)S(1)}, bf16[1,3,256,256]{3,2,1,0:T(8,128)(2,1)}, u32[]{:S(2)}) copy-start(bf16[1,3,256,256]{3,2,1,0:T(8,128)(2,1)} %w0_ref.1) | copy-start | bytes 1179652
  46.1 11.6 %copy-start.1 = (bf16[2,128,256]{2,1,0:T(8,128)(2,1)S(1)}, bf16[2,128,256]{2,1,0:T(8,128)(2,1)}, u32[]{:S(2)}) copy-start(bf16[2,128,256]{2,1,0:T(8,128)(2,1)} %k_ref.1) | copy-start | bytes 393220
  46.1 11.6 %copy-start.2 = (bf16[2,128,256]{2,1,0:T(8,128)(2,1)S(1)}, bf16[2,128,256]{2,1,0:T(8,128)(2,1)}, u32[]{:S(2)}) copy-start(bf16[2,128,256]{2,1,0:T(8,128)(2,1)} %v_ref.1) | copy-start | bytes 393220
  46.1 11.6 %copy-start.4 = (f32[2,1,128]{2,1,0:T(1,128)S(1)}, f32[2,1,128]{2,1,0:T(1,128)}, u32[]{:S(2)}) copy-start(f32[2,1,128]{2,1,0:T(1,128)} %r_ref.1) | copy-start | bytes 3076
  60.3 5.8 %copy-start.3 = (bf16[2,128,256]{2,1,0:T(8,128)(2,1)S(1)}, bf16[2,128,256]{2,1,0:T(8,128)(2,1)}, u32[]{:S(2)}) copy-start(bf16[2,128,256]{2,1,0:T(8,128)(2,1)} %q_ref.1) | copy-start | bytes 393220
  60.3 11.4 %all-to-all-start.3 = ((bf16[8,96,256]{2,1,0:T(8,128)(2,1)}), bf16[8,96,256]{2,1,0:T(8,128)(2,1)S(1)}, u32[]{:S(2)}, u32[]{:S(2)}) async-start(bf16[8,96,256]{2,1,0:T(8,128)(2,1)} %get-tuple-element.12), calls=%async_computation.3 | async-start | bytes 786432 | tf_op jit(solution)/shard_map/all_to_all | solution.py:40
  66.7 3.0 %collective-permute-start = (f32[2,128]{1,0:T(2,128)S(1)}, f32[2,128]{1,0:T(2,128)S(1)}, u32[]{:S(2)}, u32[]{:S(2)}) collective-permute-start(f32[2,128]{1,0:T(2,128)S(1)} %get-tuple-element.15), channel_id=1, source_target_pairs={{0,64},{64,0},{128,192},{192,128},{256,320},{320,256},{384,448},{4... | collective-permute-start | bytes 3080 | tf_op jit(solution)/shard_map/ppermute | solution.py:175
  72.5 18.9 %all-to-all-start.4 = ((bf16[8,96,256]{2,1,0:T(8,128)(2,1)}), bf16[8,96,256]{2,1,0:T(8,128)(2,1)S(1)}, u32[]{:S(2)}, u32[]{:S(2)}) async-start(bf16[8,96,256]{2,1,0:T(8,128)(2,1)} %shard_map.82), calls=%async_computation.4 | async-start | bytes 786432 | tf_op jit(solution)/shard_map/all_to_all | solution.py:40
  76.2 5.5 %collective-permute-start.1 = (f32[2,128]{1,0:T(2,128)S(1)}, f32[2,128]{1,0:T(2,128)S(1)}, u32[]{:S(2)}, u32[]{:S(2)}) collective-permute-start(f32[2,128]{1,0:T(2,128)S(1)} %add.9), channel_id=1, source_target_pairs={{0,128},{64,192},{128,0},{192,64},{256,384},{320,448},{384,256},{4... | collective-permute-start | bytes 3080 | tf_op jit(solution)/shard_map/ppermute | solution.py:175
  92.2 14.7 %all-to-all-start.5 = ((bf16[8,96,256]{2,1,0:T(8,128)(2,1)}), bf16[8,96,256]{2,1,0:T(8,128)(2,1)S(1)}, u32[]{:S(2)}, u32[]{:S(2)}) async-start(bf16[8,96,256]{2,1,0:T(8,128)(2,1)} %shard_map.84), calls=%async_computation.5 | async-start | bytes 786432 | tf_op jit(solution)/shard_map/all_to_all | solution.py:40
  99.1 6.3 %collective-permute-start.2 = (f32[2,128]{1,0:T(2,128)S(1)}, f32[2,128]{1,0:T(2,128)S(1)}, u32[]{:S(2)}, u32[]{:S(2)}) collective-permute-start(f32[2,128]{1,0:T(2,128)S(1)} %add.10), channel_id=1, source_target_pairs={{0,256},{64,320},{128,384},{192,448},{256,0},{320,64},{384,128},{4... | collective-permute-start | bytes 3080 | tf_op jit(solution)/shard_map/ppermute | solution.py:175
  105.5 0.7 copy-start.5

commit v3 on v2

--- a/solution.py
+++ b/solution.py
@@ -34,6 +34,20 @@
     for x in range(4)
     for y_lo in range(2)
 ]
+
+
+def token_pairs(move):
+    places = [(x, h, l, z) for x in range(4) for h in range(4) for l in range(2) for z in range(2)]
+    return [(token_index(*p), token_index(*move(*p))) for p in places]
+
+
+def from_across(array):
+    return lax.ppermute(array, "tokens", token_pairs(lambda x, h, l, z: (x, h, l, 1 - z)))
+
+
+def from_along(array, steps):
+    pairs = token_pairs(lambda x, h, l, z: (x, (h + steps) % 4, l, z))
+    return lax.ppermute(array, "tokens", pairs)
 
 
 def exchange(array, groups):
@@ -92,15 +106,17 @@
     put_grads(grads_ref, 2, mm(hidden, scaled, 0, 0))
 
 
-def first_kernel(k_hbm, v_hbm, r_hbm, w_hbm, grads_ref, k_ref, v_ref, r_ref, w_ref, sems):
-    pairs = ((w_hbm, w_ref), (k_hbm.at[0], k_ref), (v_hbm.at[0], v_ref), (r_hbm.at[0], r_ref))
+def first_kernel(k_hbm, v_hbm, r_hbm, w_hbm, grads_ref, ahead_ref, k_ref, v_ref, r_ref, w_ref, sems):
+    pairs = ((w_hbm, w_ref), (k_hbm, k_ref), (v_hbm, v_ref), (r_hbm, r_ref))
     copies = [pltpu.make_async_copy(a, b, sems.at[n]) for n, (a, b) in enumerate(pairs)]
     for copy in copies:
         copy.start()
     for copy in copies:
         copy.wait()
-    scaled = scale_rows(r_ref[...], v_ref[...])
-    local_grads(k_ref[...], scaled, w_ref[0, 0], w_ref[0, 1], w_ref[0, 2], grads_ref)
+    scaled = scale_rows(r_ref[0], v_ref[0])
+    local_grads(k_ref[0], scaled, w_ref[0, 0], w_ref[0, 1], w_ref[0, 2], grads_ref)
+    ahead_ref[0] = k_ref[1]
+    ahead_ref[1] = scale_rows(r_ref[1], v_ref[1])
 
 
 def share_kernel(parts_ref, copies_ref):
@@ -133,12 +149,23 @@
     ]
 
 
-def middle_kernel(grads_ref, w_ref, k_ref, v_ref, r_ref, fresh_ref, out_ref):
+def middle_kernel(grads_ref, w_ref, *refs):
+    tokens, (fresh_ref, out_ref, k_ref, s_ref, hid_ref, dg_ref, du_ref) = refs[:4], refs[4:]
     fresh = newton_update(grads_ref, w_ref)
     for m in range(3):
         fresh_ref[0, m] = fresh[m]
-    scaled = scale_rows(r_ref[1], v_ref[1])
-    local_grads(k_ref[1], scaled, fresh[0], fresh[1], fresh[2], out_ref)
+    for n, token_ref in enumerate(tokens):
+        rows = pl.ds(n * 256, 256)
+        keys = token_ref[:, 0].reshape(256, DH)
+        scaled = token_ref[:, 1].reshape(256, DH)
+        k_ref[rows] = keys
+        s_ref[rows] = scaled
+        hid_ref[rows], dg_ref[rows], du_ref[rows] = back_terms(
+            keys, scaled, fresh_ref[0, 0], fresh_ref[0, 1], fresh_ref[0, 2]
+        )
+    put_grads(out_ref, 0, mm(k_ref[...], dg_ref[...], 0, 0))
+    put_grads(out_ref, 1, mm(k_ref[...], du_ref[...], 0, 0))
+    put_grads(out_ref, 2, mm(hid_ref[...], s_ref[...], 0, 0))
 
 
 def last_kernel(grads_ref, w_ref, fresh_ref):
@@ -175,46 +202,40 @@
     return squares + lax.ppermute(squares, "heads", pairs)
 
 
-def reduced(grads, beside=lambda: None):
-    pieces = shaped((PEERS, SHARE, DH))
-    aside = beside()
-    parts, aside = lax.optimization_barrier((exchange(grads, NEAR), aside))
-    parts = exchange(call(share_kernel, pieces, parts), FAR)
-    if aside is not None:
-        parts, aside = lax.optimization_barrier((parts, (aside[0], add_partner(aside[1], 2))))
-    whole = exchange(call(share_kernel, pieces, parts), NEAR)
-    if aside is None:
-        return whole
-    return whole, aside[0], add_partner(aside[1], 4)
+def together(*values):
+    return lax.optimization_barrier(values)
 
 
 def per_device(queries, keys, values, rates, fast_init, out_gain):
     pieces = shaped((PEERS, SHARE, DH))
     weights = shaped((1, 3, DH, DH))
-    inputs = [
-        pltpu.VMEM((1, 3, DH, DH), BF16),
-        pltpu.VMEM((128, DH), BF16),
-        pltpu.VMEM((128, DH), BF16),
-        pltpu.VMEM((1, 128), F32),
-    ]
-    grads = call(
-        first_kernel, pieces, keys, values, rates, fast_init, flops=10**8,
-        scratch=[*inputs[1:], inputs[0], pltpu.SemaphoreType.DMA((4,))], space=pl.ANY, limit=58,
-    )
-    whole = reduced(grads)
+    copied = [(2, 128, DH), (2, 128, DH), (2, 1, 128), (1, 3, DH, DH)]
+    own = [pltpu.VMEM(shape, F32 if shape[1] == 1 else BF16) for shape in copied]
+    grads, ahead = call(
+        first_kernel, (pieces, shaped((2, 128, DH))), keys, values, rates, fast_init, flops=10**8,
+        scratch=[*own, pltpu.SemaphoreType.DMA((4,))], space=pl.ANY, limit=58,
+    )
+    parts, across = together(exchange(grads, NEAR), from_across(ahead))
+    shares = call(share_kernel, pieces, parts)
+    pair = jnp.stack([ahead, across])
+    shares, pair = together(shares, pair)
+    parts, *others = together(exchange(shares, FAR), from_along(pair, 1), from_along(pair, 3))
+    others.append(from_along(pair, 2))
+    whole = exchange(call(share_kernel, pieces, parts), NEAR)
+    wide = [pltpu.VMEM((PEERS * 128, DH), BF16)] * 5
     fresh, grads = call(
-        middle_kernel, (weights, pieces), whole, fast_init, keys, values, rates, flops=7 * 10**8
-    )
-
-    def outputs():
-        y, squares = call(
-            query_kernel,
-            (shaped((2, 128, DH), F32), shaped((2, 128), F32)),
-            queries, fast_init, fresh, flops=10**8,
-        )
-        return y, add_partner(squares, 1)
-
-    whole, y, squares = reduced(grads, outputs)
+        middle_kernel, (weights, pieces), whole, fast_init, pair, *others, flops=14 * 10**8,
+        scratch=wide,
+    )
+    y, squares = call(
+        query_kernel,
+        (shaped((2, 128, DH), F32), shaped((2, 128), F32)),
+        queries, fast_init, fresh, flops=10**8,
+    )
+    squares = add_partner(add_partner(squares, 1), 2)
+    parts, y, squares = together(exchange(grads, NEAR), y, squares)
+    whole = exchange(call(share_kernel, pieces, parts), NEAR)
+    squares = add_partner(squares, 4)
     mixed = call(finish_kernel, shaped((2, 128, DH)), y, squares, out_gain.reshape(1, DH))
     final = call(last_kernel, weights, whole, fresh, flops=6 * 10**8)
     return mixed, final

time: 110 us -> 121 us (1.10)
  blocking collectives: 54.6 us -> 0 us
  starting transfers between devices: 26 us -> 74.2 us
  waiting for transfers between devices: 16.9 us -> 32.9 us
  Pallas kernels: 10.1 us -> 11.7 us
    all_to_all x3 -> x0, blocking collectives: 54.6 us -> none  [exchange(): lax.all_to_all(array, 'tokens', 0, 0, axis_index_groups=groups, tiled=True)]
    ppermute x0 -> x4, waiting for transfers between devices: none -> 27.8 us  [the longest x3 24.5 us: from_along(): return lax.ppermute(array, 'tokens', pairs)]
    all_to_all x3 -> x5, starting transfers between devices: 16.3 us -> 43.3 us  [exchange(): lax.all_to_all(array, 'tokens', 0, 0, axis_index_groups=groups, tiled=True)]
    ppermute x0 -> x4, starting transfers between devices: none -> 19.1 us  [the longest x3 11.7 us: from_along(): return lax.ppermute(array, 'tokens', pairs)]
    all_to_all x3 -> x5, waiting for transfers between devices: 11.7 us -> 0.01 us  [exchange(): lax.all_to_all(array, 'tokens', 0, 0, axis_index_groups=groups, tiled=True)]
    ppermute x3, starting transfers between devices: 9.68 us -> 11.8 us  [add_partner(): return squares + lax.ppermute(squares, 'heads', pairs)]
    pallas_call x9 -> x8, Pallas kernels: 10.1 us -> 11.7 us  [call(): pl.pallas_call(body, out_shape=out_shape, in_specs=[pl.BlockSpec(memory_s...]
  transfers between devices with their start and end apart: 6 -> 12, of which waited for: 5 -> 7; matrix products, arithmetic and copies ran while one was open for 0% -> 0% of each run, Pallas kernels for 1% -> 1%
where the time goes in v3:
time: 121 us; the launch traced here: 120 us
  starting transfers between devices  74.2 us (61%)
  waiting for transfers between devices  32.9 us (27%)
  Pallas kernels  11.7 us (10%)
    all_to_all x5, starting transfers between devices, exchange(): lax.all_to_all(array, 'tokens', 0, 0, axis_index_groups=groups, tiled=True)  43.3 us
    ppermute x3, waiting for transfers between devices, from_along(): return lax.ppermute(array, 'tokens', pairs)  24.5 us
    ppermute x3, starting transfers between devices, add_partner(): return squares + lax.ppermute(squares, 'heads', pairs)  11.8 us
    pallas_call x8, Pallas kernels, call(): pl.pallas_call(body, out_shape=out_shape, in_specs=[pl.BlockSpec(memory_s...  11.7 us
    ppermute x3, starting transfers between devices, from_along(): return lax.ppermute(array, 'tokens', pairs)  11.7 us
    ppermute x1, starting transfers between devices, from_across(): lax.ppermute(array, 'tokens', token_pairs(lambda x, h, l, z: (x, h, l, 1...  7.46 us
    ppermute x3, waiting for transfers between devices, add_partner(): return squares + lax.ppermute(squares, 'heads', pairs)  5.06 us
    ppermute x1, waiting for transfers between devices, from_across(): lax.ppermute(array, 'tokens', token_pairs(lambda x, h, l, z: (x, h, l, 1...  3.29 us
  transfers between devices with their start and end apart: 12, of which 7 were waited for; matrix products, arithmetic and copies ran while one was open for 0% of the time, Pallas kernels for 1%

profile of v3, /device:TPU:6, one launch (start us, length us, event | category | flops | bytes accessed | tf_op | source)
XLA Modules:
  0.0 120.2 jit_solution(13342436550817282744)
XLA Ops:
  0.6 2.4 %shard_map.77 = (bf16[8,96,256]{2,1,0:T(8,128)(2,1)}, bf16[2,128,256]{2,1,0:T(8,128)(2,1)}) custom-call(bf16[2,128,256]{2,1,0:T(8,128)(2,1)} %k_hbm.1, bf16[2,128,256]{2,1,0:T(8,128)(2,1)} %v_hbm.1, f32[2,1,128]{2,1,0:T(1,128)} %r_hbm.1, bf16[1,3,256,256]{3,2,1,0:T(8,128)(2,1)} %w0_ref.1), custom_call_target="tpu_custom_call" | custom-call | flops 100000000 | bytes 1180672 | tf_op jit(solution)/shard_map/pallas_call | solution.py:64
  3.1 0.0 copy-start.3
  3.1 9.4 %all-to-all-start = ((bf16[8,96,256]{2,1,0:T(8,128)(2,1)}), bf16[8,96,256]{2,1,0:T(8,128)(2,1)S(1)}, u32[]{:S(2)}, u32[]{:S(2)}) async-start(bf16[8,96,256]{2,1,0:T(8,128)(2,1)} %get-tuple-element.18), calls=%async_computation | async-start | bytes 786432 | tf_op jit(solution)/shard_map/all_to_all | solution.py:54
  12.5 0.0 copy-done.3
  12.5 7.5 %collective-permute-start = (bf16[2,128,256]{2,1,0:T(8,128)(2,1)S(1)}, bf16[2,128,256]{2,1,0:T(8,128)(2,1)S(1)}, u32[]{:S(2)}, u32[]{:S(2)}) collective-permute-start(bf16[2,128,256]{2,1,0:T(8,128)(2,1)S(1)} %copy-done.3), channel_id=1, source_target_pairs={{0,1},{1,0},{2,3},{3,2},{4,5},{5,4},{6,7},{7,6},{8,9},{9,8},{10,11... | collective-permute-start | bytes 393224 | tf_op jit(solution)/shard_map/ppermute | solution.py:45
  19.9 3.3 %collective-permute-done = bf16[2,128,256]{2,1,0:T(8,128)(2,1)S(1)} collective-permute-done((bf16[2,128,256]{2,1,0:T(8,128)(2,1)S(1)}, bf16[2,128,256]{2,1,0:T(8,128)(2,1)S(1)}, u32[]{:S(2)}, u32[]{:S(2)}) %collective-permute-start) | collective-permute-done | bytes 131104 | tf_op jit(solution)/shard_map/ppermute | solution.py:45
  23.2 0.0 all-to-all-done.parts_ref
  23.2 0.8 shard_map.78
  24.0 13.9 %all-to-all-start.1 = ((bf16[8,96,256]{2,1,0:T(8,128)(2,1)}), bf16[8,96,256]{2,1,0:T(8,128)(2,1)S(1)}, u32[]{:S(2)}, u32[]{:S(2)}) async-start(bf16[8,96,256]{2,1,0:T(8,128)(2,1)} %shard_map.78), calls=%async_computation.1 | async-start | bytes 786432 | tf_op jit(solution)/shard_map/all_to_all | solution.py:54
  38.0 6.0 %collective-permute-start.2 = (bf16[2,2,128,256]{3,2,1,0:T(8,128)(2,1)S(1)}, bf16[2,2,128,256]{3,2,1,0:T(8,128)(2,1)S(1)}, u32[]{:S(2)}, u32[]{:S(2)}) collective-permute-start(bf16[2,2,128,256]{3,2,1,0:T(8,128)(2,1)S(1)} %pad_maximum_fusion.refs_0_), channel_id=1, source_target_pairs={{0,12},{1,13},{2,14},{3,15},{4,0},{5,1},{6,2},{7,3},{8,4},{9,5},{1... | collective-permute-start | bytes 786440 | tf_op jit(solution)/shard_map/ppermute | solution.py:50
  44.0 1.9 %collective-permute-start.1 = (bf16[2,2,128,256]{3,2,1,0:T(8,128)(2,1)S(1)}, bf16[2,2,128,256]{3,2,1,0:T(8,128)(2,1)S(1)}, u32[]{:S(2)}, u32[]{:S(2)}) collective-permute-start(bf16[2,2,128,256]{3,2,1,0:T(8,128)(2,1)S(1)} %pad_maximum_fusion.refs_0_), channel_id=1, source_target_pairs={{0,4},{1,5},{2,6},{3,7},{4,8},{5,9},{6,10},{7,11},{8,12},{9,13},{1... | collective-permute-start | bytes 786440 | tf_op jit(solution)/shard_map/ppermute | solution.py:50
  45.9 10.7 %collective-permute-done.2.refs_2_ = bf16[2,2,128,256]{3,2,1,0:T(8,128)(2,1)S(1)} collective-permute-done((bf16[2,2,128,256]{3,2,1,0:T(8,128)(2,1)S(1)}, bf16[2,2,128,256]{3,2,1,0:T(8,128)(2,1)S(1)}, u32[]{:S(2)}, u32[]{:S(2)}) %collective-permute-start.2) | collective-permute-done | bytes 262176 | tf_op jit(solution)/shard_map/ppermute | solution.py:50
  56.6 0.3 collective-permute-done.1.refs_1_
  56.9 0.0 all-to-all-done.1.parts_ref
  56.9 0.8 shard_map.79
  57.7 0.0 copy-start
  57.7 8.3 %all-to-all-start.2 = ((bf16[8,96,256]{2,1,0:T(8,128)(2,1)}), bf16[8,96,256]{2,1,0:T(8,128)(2,1)S(1)}, u32[]{:S(2)}, u32[]{:S(2)}) async-start(bf16[8,96,256]{2,1,0:T(8,128)(2,1)} %shard_map.79), calls=%async_computation.2 | async-start | bytes 786432 | tf_op jit(solution)/shard_map/all_to_all | solution.py:54
  65.9 3.7 %collective-permute-start.3 = (bf16[2,2,128,256]{3,2,1,0:T(8,128)(2,1)S(1)}, bf16[2,2,128,256]{3,2,1,0:T(8,128)(2,1)S(1)}, u32[]{:S(2)}, u32[]{:S(2)}) collective-permute-start(bf16[2,2,128,256]{3,2,1,0:T(8,128)(2,1)S(1)} %pad_maximum_fusion.refs_0_), channel_id=1, source_target_pairs={{0,8},{1,9},{2,10},{3,11},{4,12},{5,13},{6,14},{7,15},{8,0},{9,1},... | collective-permute-start | bytes 786440 | tf_op jit(solution)/shard_map/ppermute | solution.py:50
  69.7 13.6 %collective-permute-done.3.refs_3_ = bf16[2,2,128,256]{3,2,1,0:T(8,128)(2,1)S(1)} collective-permute-done((bf16[2,2,128,256]{3,2,1,0:T(8,128)(2,1)S(1)}, bf16[2,2,128,256]{3,2,1,0:T(8,128)(2,1)S(1)}, u32[]{:S(2)}, u32[]{:S(2)}) %collective-permute-start.3) | collective-permute-done | bytes 262176 | tf_op jit(solution)/shard_map/ppermute | solution.py:50
  83.2 0.0 all-to-all-done.2.grads_ref
  83.2 0.0 copy-done
  83.2 3.5 %shard_map.80 = (bf16[1,3,256,256]{3,2,1,0:T(8,128)(2,1)S(1)}, bf16[8,96,256]{2,1,0:T(8,128)(2,1)}) custom-call(bf16[8,96,256]{2,1,0:T(8,128)(2,1)S(1)} %all-to-all-done.2.grads_ref, bf16[1,3,256,256]{3,2,1,0:T(8,128)(2,1)S(1)} %copy-done, bf16[2,2,128,256]{3,2,1,0:T(8,128)(2,1)S(1)} %pad_maximum_fusion.refs_0_, ...), custom_call_target="tpu_custom_call" | custom-call | flops 1400000000 | bytes 2621440 | tf_op jit(solution)/shard_map/pallas_call | solution.py:64
  86.7 0.0 copy-start.1
  86.7 6.0 %all-to-all-start.3 = ((bf16[8,96,256]{2,1,0:T(8,128)(2,1)}), bf16[8,96,256]{2,1,0:T(8,128)(2,1)S(1)}, u32[]{:S(2)}, u32[]{:S(2)}) async-start(bf16[8,96,256]{2,1,0:T(8,128)(2,1)} %get-tuple-element.27), calls=%async_computation.3 | async-start | bytes 786432 | tf_op jit(solution)/shard_map/all_to_all | solution.py:54
  92.7 0.0 copy-done.1
  92.7 0.6 shard_map.81
  93.3 1.9 %collective-permute-start.4 = (f32[2,128]{1,0:T(2,128)S(1)}, f32[2,128]{1,0:T(2,128)S(1)}, u32[]{:S(2)}, u32[]{:S(2)}) collective-permute-start(f32[2,128]{1,0:T(2,128)S(1)} %get-tuple-element.30), channel_id=1, source_target_pairs={{0,64},{64,0},{128,192},{192,128},{256,320},{320,256},{384,448},{4... | collective-permute-start | bytes 3080 | tf_op jit(solution)/shard_map/ppermute | solution.py:202
  95.2 1.1 collective-permute-done.4
  96.3 3.0 %collective-permute-start.5 = (f32[2,128]{1,0:T(2,128)S(1)}, f32[2,128]{1,0:T(2,128)S(1)}, u32[]{:S(2)}, u32[]{:S(2)}) collective-permute-start(f32[2,128]{1,0:T(2,128)S(1)} %add.9), channel_id=1, source_target_pairs={{0,128},{64,192},{128,0},{192,64},{256,384},{320,448},{384,256},{4... | collective-permute-start | bytes 3080 | tf_op jit(solution)/shard_map/ppermute | solution.py:202
  99.3 2.4 %collective-permute-done.5 = f32[2,128]{1,0:T(2,128)S(1)} collective-permute-done((f32[2,128]{1,0:T(2,128)S(1)}, f32[2,128]{1,0:T(2,128)S(1)}, u32[]{:S(2)}, u32[]{:S(2)}) %collective-permute-start.5) | collective-permute-done | bytes 1056 | tf_op jit(solution)/shard_map/ppermute | solution.py:202
  101.8 0.0 all-to-all-done.3.parts_ref
  101.8 0.8 shard_map.83
  102.6 5.7 %all-to-all-start.4 = ((bf16[8,96,256]{2,1,0:T(8,128)(2,1)}), bf16[8,96,256]{2,1,0:T(8,128)(2,1)S(1)}, u32[]{:S(2)}, u32[]{:S(2)}) async-start(bf16[8,96,256]{2,1,0:T(8,128)(2,1)} %shard_map.83), calls=%async_computation.4 | async-start | bytes 786432 | tf_op jit(solution)/shard_map/all_to_all | solution.py:54
  108.3 6.8 %collective-permute-start.6 = (f32[2,128]{1,0:T(2,128)S(1)}, f32[2,128]{1,0:T(2,128)S(1)}, u32[]{:S(2)}, u32[]{:S(2)}) collective-permute-start(f32[2,128]{1,0:T(2,128)S(1)} %add.10), channel_id=1, source_target_pairs={{0,256},{64,320},{128,384},{192,448},{256,0},{320,64},{384,128},{4... | collective-permute-start | bytes 3080 | tf_op jit(solution)/shard_map/ppermute | solution.py:202
  115.1 1.5 %collective-permute-done.6 = f32[2,128]{1,0:T(2,128)S(1)} collective-permute-done((f32[2,128]{1,0:T(2,128)S(1)}, f32[2,128]{1,0:T(2,128)S(1)}, u32[]{:S(2)}, u32[]{:S(2)}) %collective-permute-start.6) | collective-permute-done | bytes 1056 | tf_op jit(solution)/shard_map/ppermute | solution.py:202
  116.7 0.0 copy-start.2
  116.7 0.7 copy-done.2
  117.3 0.8 shard_map.82
  118.1 0.0 all-to-all-done.4.grads_ref
  118.1 2.1 %shard_map.84 = bf16[1,3,256,256]{3,2,1,0:T(8,128)(2,1)} custom-call(bf16[8,96,256]{2,1,0:T(8,128)(2,1)S(1)} %all-to-all-done.4.grads_ref, bf16[1,3,256,256]{3,2,1,0:T(8,128)(2,1)S(1)} %get-tuple-element.28.w1_ref.w_ref), custom_call_target="tpu_custom_call" | custom-call | flops 600000000 | bytes 1179648 | tf_op jit(solution)/shard_map/pallas_call | solution.py:64
  (4 shorter events, 0.0 us)
Async XLA Ops:
  3.1 9.4 %copy-start.3 = (bf16[2,128,256]{2,1,0:T(8,128)(2,1)S(1)}, bf16[2,128,256]{2,1,0:T(8,128)(2,1)}, u32[]{:S(2)}) copy-start(bf16[2,128,256]{2,1,0:T(8,128)(2,1)} %get-tuple-element.19) | copy-start | bytes 393220
  3.1 20.1 %all-to-all-start = ((bf16[8,96,256]{2,1,0:T(8,128)(2,1)}), bf16[8,96,256]{2,1,0:T(8,128)(2,1)S(1)}, u32[]{:S(2)}, u32[]{:S(2)}) async-start(bf16[8,96,256]{2,1,0:T(8,128)(2,1)} %get-tuple-element.18), calls=%async_computation | async-start | bytes 786432 | tf_op jit(solution)/shard_map/all_to_all | solution.py:54
  12.5 10.8 %collective-permute-start = (bf16[2,128,256]{2,1,0:T(8,128)(2,1)S(1)}, bf16[2,128,256]{2,1,0:T(8,128)(2,1)S(1)}, u32[]{:S(2)}, u32[]{:S(2)}) collective-permute-start(bf16[2,128,256]{2,1,0:T(8,128)(2,1)S(1)} %copy-done.3), channel_id=1, source_target_pairs={{0,1},{1,0},{2,3},{3,2},{4,5},{5,4},{6,7},{7,6},{8,9},{9,8},{10,11... | collective-permute-start | bytes 393224 | tf_op jit(solution)/shard_map/ppermute | solution.py:45
  24.0 32.8 %all-to-all-start.1 = ((bf16[8,96,256]{2,1,0:T(8,128)(2,1)}), bf16[8,96,256]{2,1,0:T(8,128)(2,1)S(1)}, u32[]{:S(2)}, u32[]{:S(2)}) async-start(bf16[8,96,256]{2,1,0:T(8,128)(2,1)} %shard_map.78), calls=%async_computation.1 | async-start | bytes 786432 | tf_op jit(solution)/shard_map/all_to_all | solution.py:54
  38.0 18.6 %collective-permute-start.2 = (bf16[2,2,128,256]{3,2,1,0:T(8,128)(2,1)S(1)}, bf16[2,2,128,256]{3,2,1,0:T(8,128)(2,1)S(1)}, u32[]{:S(2)}, u32[]{:S(2)}) collective-permute-start(bf16[2,2,128,256]{3,2,1,0:T(8,128)(2,1)S(1)} %pad_maximum_fusion.refs_0_), channel_id=1, source_target_pairs={{0,12},{1,13},{2,14},{3,15},{4,0},{5,1},{6,2},{7,3},{8,4},{9,5},{1... | collective-permute-start | bytes 786440 | tf_op jit(solution)/shard_map/ppermute | solution.py:50
  44.0 12.9 %collective-permute-start.1 = (bf16[2,2,128,256]{3,2,1,0:T(8,128)(2,1)S(1)}, bf16[2,2,128,256]{3,2,1,0:T(8,128)(2,1)S(1)}, u32[]{:S(2)}, u32[]{:S(2)}) collective-permute-start(bf16[2,2,128,256]{3,2,1,0:T(8,128)(2,1)S(1)} %pad_maximum_fusion.refs_0_), channel_id=1, source_target_pairs={{0,4},{1,5},{2,6},{3,7},{4,8},{5,9},{6,10},{7,11},{8,12},{9,13},{1... | collective-permute-start | bytes 786440 | tf_op jit(solution)/shard_map/ppermute | solution.py:50
  57.7 25.5 %copy-start = (bf16[1,3,256,256]{3,2,1,0:T(8,128)(2,1)S(1)}, bf16[1,3,256,256]{3,2,1,0:T(8,128)(2,1)}, u32[]{:S(2)}) copy-start(bf16[1,3,256,256]{3,2,1,0:T(8,128)(2,1)} %w0_ref.1) | copy-start | bytes 1179652
  57.7 25.5 %all-to-all-start.2 = ((bf16[8,96,256]{2,1,0:T(8,128)(2,1)}), bf16[8,96,256]{2,1,0:T(8,128)(2,1)S(1)}, u32[]{:S(2)}, u32[]{:S(2)}) async-start(bf16[8,96,256]{2,1,0:T(8,128)(2,1)} %shard_map.79), calls=%async_computation.2 | async-start | bytes 786432 | tf_op jit(solution)/shard_map/all_to_all | solution.py:54
  65.9 17.3 %collective-permute-start.3 = (bf16[2,2,128,256]{3,2,1,0:T(8,128)(2,1)S(1)}, bf16[2,2,128,256]{3,2,1,0:T(8,128)(2,1)S(1)}, u32[]{:S(2)}, u32[]{:S(2)}) collective-permute-start(bf16[2,2,128,256]{3,2,1,0:T(8,128)(2,1)S(1)} %pad_maximum_fusion.refs_0_), channel_id=1, source_target_pairs={{0,8},{1,9},{2,10},{3,11},{4,12},{5,13},{6,14},{7,15},{8,0},{9,1},... | collective-permute-start | bytes 786440 | tf_op jit(solution)/shard_map/ppermute | solution.py:50
  86.7 6.0 %copy-start.1 = (bf16[2,128,256]{2,1,0:T(8,128)(2,1)S(1)}, bf16[2,128,256]{2,1,0:T(8,128)(2,1)}, u32[]{:S(2)}) copy-start(bf16[2,128,256]{2,1,0:T(8,128)(2,1)} %q_ref.1) | copy-start | bytes 393220
  86.7 15.1 %all-to-all-start.3 = ((bf16[8,96,256]{2,1,0:T(8,128)(2,1)}), bf16[8,96,256]{2,1,0:T(8,128)(2,1)S(1)}, u32[]{:S(2)}, u32[]{:S(2)}) async-start(bf16[8,96,256]{2,1,0:T(8,128)(2,1)} %get-tuple-element.27), calls=%async_computation.3 | async-start | bytes 786432 | tf_op jit(solution)/shard_map/all_to_all | solution.py:54
  93.3 3.0 %collective-permute-start.4 = (f32[2,128]{1,0:T(2,128)S(1)}, f32[2,128]{1,0:T(2,128)S(1)}, u32[]{:S(2)}, u32[]{:S(2)}) collective-permute-start(f32[2,128]{1,0:T(2,128)S(1)} %get-tuple-element.30), channel_id=1, source_target_pairs={{0,64},{64,0},{128,192},{192,128},{256,320},{320,256},{384,448},{4... | collective-permute-start | bytes 3080 | tf_op jit(solution)/shard_map/ppermute | solution.py:202
  96.3 5.5 %collective-permute-start.5 = (f32[2,128]{1,0:T(2,128)S(1)}, f32[2,128]{1,0:T(2,128)S(1)}, u32[]{:S(2)}, u32[]{:S(2)}) collective-permute-start(f32[2,128]{1,0:T(2,128)S(1)} %add.9), channel_id=1, source_target_pairs={{0,128},{64,192},{128,0},{192,64},{256,384},{320,448},{384,256},{4... | collective-permute-start | bytes 3080 | tf_op jit(solution)/shard_map/ppermute | solution.py:202
  102.6 15.5 %all-to-all-start.4 = ((bf16[8,96,256]{2,1,0:T(8,128)(2,1)}), bf16[8,96,256]{2,1,0:T(8,128)(2,1)S(1)}, u32[]{:S(2)}, u32[]{:S(2)}) async-start(bf16[8,96,256]{2,1,0:T(8,128)(2,1)} %shard_map.83), calls=%async_computation.4 | async-start | bytes 786432 | tf_op jit(solution)/shard_map/all_to_all | solution.py:54
  108.3 8.4 %collective-permute-start.6 = (f32[2,128]{1,0:T(2,128)S(1)}, f32[2,128]{1,0:T(2,128)S(1)}, u32[]{:S(2)}, u32[]{:S(2)}) collective-permute-start(f32[2,128]{1,0:T(2,128)S(1)} %add.10), channel_id=1, source_target_pairs={{0,256},{64,320},{128,384},{192,448},{256,0},{320,64},{384,128},{4... | collective-permute-start | bytes 3080 | tf_op jit(solution)/shard_map/ppermute | solution.py:202
  116.7 0.7 copy-start.2

commit v4 on v3

--- a/solution.py
+++ b/solution.py
@@ -34,6 +34,12 @@
     for x in range(4)
     for y_lo in range(2)
 ]
+ALONG = [
+    [token_index(x, y_hi, y_lo, z_hi) for y_hi in range(4)]
+    for x in range(4)
+    for y_lo in range(2)
+    for z_hi in range(2)
+]
 
 
 def token_pairs(move):
@@ -43,11 +49,6 @@
 
 def from_across(array):
     return lax.ppermute(array, "tokens", token_pairs(lambda x, h, l, z: (x, h, l, 1 - z)))
-
-
-def from_along(array, steps):
-    pairs = token_pairs(lambda x, h, l, z: (x, (h + steps) % 4, l, z))
-    return lax.ppermute(array, "tokens", pairs)
 
 
 def exchange(array, groups):
@@ -121,10 +122,10 @@
 
 def share_kernel(parts_ref, copies_ref):
     total = parts_ref[0].astype(F32)
-    for peer in range(1, PEERS):
+    for peer in range(1, parts_ref.shape[0]):
         total = total + parts_ref[peer].astype(F32)
     total = total.astype(BF16)
-    for peer in range(PEERS):
+    for peer in range(copies_ref.shape[0]):
         copies_ref[peer] = total
 
 
@@ -149,23 +150,13 @@
     ]
 
 
-def middle_kernel(grads_ref, w_ref, *refs):
-    tokens, (fresh_ref, out_ref, k_ref, s_ref, hid_ref, dg_ref, du_ref) = refs[:4], refs[4:]
+def middle_kernel(grads_ref, w_ref, own_ref, across_ref, fresh_ref, out_ref):
     fresh = newton_update(grads_ref, w_ref)
     for m in range(3):
         fresh_ref[0, m] = fresh[m]
-    for n, token_ref in enumerate(tokens):
-        rows = pl.ds(n * 256, 256)
-        keys = token_ref[:, 0].reshape(256, DH)
-        scaled = token_ref[:, 1].reshape(256, DH)
-        k_ref[rows] = keys
-        s_ref[rows] = scaled
-        hid_ref[rows], dg_ref[rows], du_ref[rows] = back_terms(
-            keys, scaled, fresh_ref[0, 0], fresh_ref[0, 1], fresh_ref[0, 2]
-        )
-    put_grads(out_ref, 0, mm(k_ref[...], dg_ref[...], 0, 0))
-    put_grads(out_ref, 1, mm(k_ref[...], du_ref[...], 0, 0))
-    put_grads(out_ref, 2, mm(hid_ref[...], s_ref[...], 0, 0))
+    keys = jnp.concatenate([own_ref[0], across_ref[0]], axis=0)
+    scaled = jnp.concatenate([own_ref[1], across_ref[1]], axis=0)
+    local_grads(keys, scaled, fresh[0], fresh[1], fresh[2], out_ref)
 
 
 def last_kernel(grads_ref, w_ref, fresh_ref):
@@ -174,23 +165,23 @@
         fresh_ref[0, m] = fresh[m]
 
 
-def query_kernel(q_ref, w0_ref, w1_ref, y_ref, squares_ref):
+def query_kernel(q_ref, w0_ref, w1_ref, gain_ref, y_ref, squares_ref):
     for block, w_ref in enumerate((w0_ref, w1_ref)):
         gate = mm(q_ref[block], w_ref[0, 0])
         up = mm(q_ref[block], w_ref[0, 1])
         hidden = (gate * jax.nn.sigmoid(gate) * up).astype(BF16)
         out = mm(hidden, w_ref[0, 2])
-        y_ref[block] = out
+        y_ref[block] = out * gain_ref[...]
         sums = jnp.sum(out * out, axis=1, keepdims=True)
         squares_ref[pl.ds(block, 1)] = jnp.transpose(jnp.broadcast_to(sums, (128, 128)))[:1]
 
 
-def finish_kernel(y_ref, squares_ref, gain_ref, out_ref):
+def finish_kernel(y_ref, squares_ref, out_ref):
     root = jnp.sqrt(squares_ref[...] / D + 1e-06)
     for block in range(2):
         tall = jnp.transpose(jnp.broadcast_to(root[block : block + 1], (128, 128)))
         both = jnp.concatenate([tall, tall], axis=1)
-        out_ref[block] = (y_ref[block] / both * gain_ref[...]).astype(BF16)
+        out_ref[block] = (y_ref[block] / both).astype(BF16)
 
 
 def shaped(shape, dtype=BF16):
@@ -215,28 +206,25 @@
         first_kernel, (pieces, shaped((2, 128, DH))), keys, values, rates, fast_init, flops=10**8,
         scratch=[*own, pltpu.SemaphoreType.DMA((4,))], space=pl.ANY, limit=58,
     )
-    parts, across = together(exchange(grads, NEAR), from_across(ahead))
-    shares = call(share_kernel, pieces, parts)
-    pair = jnp.stack([ahead, across])
-    shares, pair = together(shares, pair)
-    parts, *others = together(exchange(shares, FAR), from_along(pair, 1), from_along(pair, 3))
-    others.append(from_along(pair, 2))
+    share = shaped((4, SHARE, DH))
+    parts = exchange(grads, NEAR)
+    shares, ahead = together(call(share_kernel, pieces, parts), ahead)
+    parts, across = together(exchange(shares, FAR), from_across(ahead))
     whole = exchange(call(share_kernel, pieces, parts), NEAR)
-    wide = [pltpu.VMEM((PEERS * 128, DH), BF16)] * 5
     fresh, grads = call(
-        middle_kernel, (weights, pieces), whole, fast_init, pair, *others, flops=14 * 10**8,
-        scratch=wide,
+        middle_kernel, (weights, pieces), whole, fast_init, ahead, across, flops=9 * 10**8
     )
     y, squares = call(
         query_kernel,
         (shaped((2, 128, DH), F32), shaped((2, 128), F32)),
-        queries, fast_init, fresh, flops=10**8,
+        queries, fast_init, fresh, out_gain.reshape(1, DH), flops=10**8,
     )
     squares = add_partner(add_partner(squares, 1), 2)
     parts, y, squares = together(exchange(grads, NEAR), y, squares)
+    shares = call(share_kernel, share, parts)
+    parts, y, squares = together(exchange(shares, ALONG), y, add_partner(squares, 4))
     whole = exchange(call(share_kernel, pieces, parts), NEAR)
-    squares = add_partner(squares, 4)
-    mixed = call(finish_kernel, shaped((2, 128, DH)), y, squares, out_gain.reshape(1, DH))
+    mixed = call(finish_kernel, shaped((2, 128, DH)), y, squares)
     final = call(last_kernel, weights, whole, fresh, flops=6 * 10**8)
     return mixed, final
 

time: 121 us -> 112 us (0.926)
  blocking collectives: 0 us -> 26.5 us
  starting transfers between devices: 74.2 us -> 48.9 us
  waiting for transfers between devices: 32.9 us -> 22.7 us
    all_to_all x0 -> x2, blocking collectives: none -> 26.5 us  [exchange(): lax.all_to_all(array, 'tokens', 0, 0, axis_index_groups=groups, tiled=True)]
    ppermute x3 -> x0, waiting for transfers between devices: 24.5 us -> none  [from_along(): return lax.ppermute(array, 'tokens', pairs)]
    all_to_all x5 -> x4, starting transfers between devices: 43.3 us -> 31.1 us  [exchange(): lax.all_to_all(array, 'tokens', 0, 0, axis_index_groups=groups, tiled=True)]
    ppermute x3 -> x0, starting transfers between devices: 11.7 us -> none  [from_along(): return lax.ppermute(array, 'tokens', pairs)]
    all_to_all x5 -> x4, waiting for transfers between devices: 0.01 us -> 7.69 us  [exchange(): lax.all_to_all(array, 'tokens', 0, 0, axis_index_groups=groups, tiled=True)]
    ppermute x1, waiting for transfers between devices: 3.29 us -> 10.2 us  [from_across(): lax.ppermute(array, 'tokens', token_pairs(lambda x, h, l, z: (x, h, l, 1...]
    ppermute x3, starting transfers between devices: 11.8 us -> 10 us  [add_partner(): return squares + lax.ppermute(squares, 'heads', pairs)]
    pallas_call x8 -> x9, Pallas kernels: 11.7 us -> 10.9 us  [call(): pl.pallas_call(body, out_shape=out_shape, in_specs=[pl.BlockSpec(memory_s...]
  transfers between devices with their start and end apart: 12 -> 8, of which waited for: 7 -> 6; matrix products, arithmetic and copies ran while one was open for 0% -> 0% of each run, Pallas kernels for 1% -> 1%
where the time goes in v4:
time: 112 us; the launch traced here: 110 us
  starting transfers between devices  48.9 us (44%)
  blocking collectives  26.5 us (24%)
  waiting for transfers between devices  22.7 us (20%)
  Pallas kernels  10.9 us (10%)
    all_to_all x4, starting transfers between devices, exchange(): lax.all_to_all(array, 'tokens', 0, 0, axis_index_groups=groups, tiled=True)  31.1 us
    all_to_all x2, blocking collectives, exchange(): lax.all_to_all(array, 'tokens', 0, 0, axis_index_groups=groups, tiled=True)  26.5 us
    pallas_call x9, Pallas kernels, call(): pl.pallas_call(body, out_shape=out_shape, in_specs=[pl.BlockSpec(memory_s...  10.9 us
    ppermute x1, waiting for transfers between devices, from_across(): lax.ppermute(array, 'tokens', token_pairs(lambda x, h, l, z: (x, h, l, 1...  10.2 us
    ppermute x3, starting transfers between devices, add_partner(): return squares + lax.ppermute(squares, 'heads', pairs)  10 us
    ppermute x1, starting transfers between devices, from_across(): lax.ppermute(array, 'tokens', token_pairs(lambda x, h, l, z: (x, h, l, 1...  7.82 us
    all_to_all x4, waiting for transfers between devices, exchange(): lax.all_to_all(array, 'tokens', 0, 0, axis_index_groups=groups, tiled=True)  7.69 us
    ppermute x3, waiting for transfers between devices, add_partner(): return squares + lax.ppermute(squares, 'heads', pairs)  4.85 us
  transfers between devices with their start and end apart: 8, of which 6 were waited for; matrix products, arithmetic and copies ran while one was open for 0% of the time, Pallas kernels for 1%

profile of v4, /device:TPU:6, one launch (start us, length us, event | category | flops | bytes accessed | tf_op | source)
XLA Modules:
  0.0 110.4 jit_solution(5610446756562003798)
XLA Ops:
  0.6 2.4 %shard_map.77 = (bf16[8,96,256]{2,1,0:T(8,128)(2,1)}, bf16[2,128,256]{2,1,0:T(8,128)(2,1)}) custom-call(bf16[2,128,256]{2,1,0:T(8,128)(2,1)} %k_hbm.1, bf16[2,128,256]{2,1,0:T(8,128)(2,1)} %v_hbm.1, f32[2,1,128]{2,1,0:T(1,128)} %r_hbm.1, bf16[1,3,256,256]{3,2,1,0:T(8,128)(2,1)} %w0_ref.1), custom_call_target="tpu_custom_call" | custom-call | flops 100000000 | bytes 1180672 | tf_op jit(solution)/shard_map/pallas_call | solution.py:65
  3.1 15.1 %all_to_all.30.parts_ref = bf16[8,96,256]{2,1,0:T(8,128)(2,1)S(1)} all-to-all(bf16[8,96,256]{2,1,0:T(8,128)(2,1)} %get-tuple-element.18), channel_id=1, replica_groups={{0,2,16,18,32,34,48,50},{1,3,17,19,33,35,49,51},{4,6,20,22,36,38,52,54}..., dimensions={0} | all-to-all | bytes 786432 | tf_op jit(solution)/shard_map/all_to_all | solution.py:55
  18.1 0.8 shard_map.78
  18.9 0.0 copy-start.3
  18.9 12.1 %all-to-all-start.1 = ((bf16[8,96,256]{2,1,0:T(8,128)(2,1)}), bf16[8,96,256]{2,1,0:T(8,128)(2,1)S(1)}, u32[]{:S(2)}, u32[]{:S(2)}) async-start(bf16[8,96,256]{2,1,0:T(8,128)(2,1)} %shard_map.78), calls=%async_computation.1 | async-start | bytes 786432 | tf_op jit(solution)/shard_map/all_to_all | solution.py:55
  31.0 0.0 copy-done.3
  31.0 7.8 %collective-permute-start = (bf16[2,128,256]{2,1,0:T(8,128)(2,1)S(1)}, bf16[2,128,256]{2,1,0:T(8,128)(2,1)S(1)}, u32[]{:S(2)}, u32[]{:S(2)}) collective-permute-start(bf16[2,128,256]{2,1,0:T(8,128)(2,1)S(1)} %copy-done.3), channel_id=1, source_target_pairs={{0,1},{1,0},{2,3},{3,2},{4,5},{5,4},{6,7},{7,6},{8,9},{9,8},{10,11... | collective-permute-start | bytes 393224 | tf_op jit(solution)/shard_map/ppermute | solution.py:51
  38.8 10.2 %collective-permute-done.across_ref = bf16[2,128,256]{2,1,0:T(8,128)(2,1)S(1)} collective-permute-done((bf16[2,128,256]{2,1,0:T(8,128)(2,1)S(1)}, bf16[2,128,256]{2,1,0:T(8,128)(2,1)S(1)}, u32[]{:S(2)}, u32[]{:S(2)}) %collective-permute-start) | collective-permute-done | bytes 131104 | tf_op jit(solution)/shard_map/ppermute | solution.py:51
  49.0 0.0 all-to-all-done.1.parts_ref
  49.0 0.1 shard_map.79
  49.1 0.0 copy-start
  49.1 11.4 %all_to_all.31.grads_ref = bf16[8,96,256]{2,1,0:T(8,128)(2,1)S(1)} all-to-all(bf16[8,96,256]{2,1,0:T(8,128)(2,1)S(1)} %shard_map.79), channel_id=1, replica_groups={{0,2,16,18,32,34,48,50},{1,3,17,19,33,35,49,51},{4,6,20,22,36,38,52,54}..., dimensions={0} | all-to-all | bytes 786432 | tf_op jit(solution)/shard_map/all_to_all | solution.py:55
  60.5 0.0 copy-done
  60.5 2.6 %shard_map.80 = (bf16[1,3,256,256]{3,2,1,0:T(8,128)(2,1)S(1)}, bf16[8,96,256]{2,1,0:T(8,128)(2,1)}) custom-call(bf16[8,96,256]{2,1,0:T(8,128)(2,1)S(1)} %all_to_all.31.grads_ref, bf16[1,3,256,256]{3,2,1,0:T(8,128)(2,1)S(1)} %copy-done, bf16[2,128,256]{2,1,0:T(8,128)(2,1)S(1)} %copy-done.3, bf16[2,128,256]{2,1,0:T(8,128)(2,1)S(1)} %collective-permute-done.across_ref), custom_call_target="tpu_custom_call" | custom-call | flops 900000000 | bytes 1835008 | tf_op jit(solution)/shard_map/pallas_call | solution.py:65
  63.1 0.0 copy-start.1
  63.1 5.8 %all-to-all-start.3 = ((bf16[8,96,256]{2,1,0:T(8,128)(2,1)}), bf16[8,96,256]{2,1,0:T(8,128)(2,1)S(1)}, u32[]{:S(2)}, u32[]{:S(2)}) async-start(bf16[8,96,256]{2,1,0:T(8,128)(2,1)} %get-tuple-element.24), calls=%async_computation.3 | async-start | bytes 786432 | tf_op jit(solution)/shard_map/all_to_all | solution.py:55
  68.9 0.0 copy-start.2
  68.9 0.0 copy-done.1
  68.9 0.7 copy-done.2
  69.6 0.6 shard_map.81
  70.2 1.9 %collective-permute-start.1 = (f32[2,128]{1,0:T(2,128)S(1)}, f32[2,128]{1,0:T(2,128)S(1)}, u32[]{:S(2)}, u32[]{:S(2)}) collective-permute-start(f32[2,128]{1,0:T(2,128)S(1)} %get-tuple-element.27), channel_id=1, source_target_pairs={{0,64},{64,0},{128,192},{192,128},{256,320},{320,256},{384,448},{4... | collective-permute-start | bytes 3080 | tf_op jit(solution)/shard_map/ppermute | solution.py:193
  72.1 1.1 %collective-permute-done.1 = f32[2,128]{1,0:T(2,128)S(1)} collective-permute-done((f32[2,128]{1,0:T(2,128)S(1)}, f32[2,128]{1,0:T(2,128)S(1)}, u32[]{:S(2)}, u32[]{:S(2)}) %collective-permute-start.1) | collective-permute-done | bytes 1056 | tf_op jit(solution)/shard_map/ppermute | solution.py:193
  73.2 4.0 %collective-permute-start.2 = (f32[2,128]{1,0:T(2,128)S(1)}, f32[2,128]{1,0:T(2,128)S(1)}, u32[]{:S(2)}, u32[]{:S(2)}) collective-permute-start(f32[2,128]{1,0:T(2,128)S(1)} %add.9), channel_id=1, source_target_pairs={{0,128},{64,192},{128,0},{192,64},{256,384},{320,448},{384,256},{4... | collective-permute-start | bytes 3080 | tf_op jit(solution)/shard_map/ppermute | solution.py:193
  77.2 1.5 %collective-permute-done.2 = f32[2,128]{1,0:T(2,128)S(1)} collective-permute-done((f32[2,128]{1,0:T(2,128)S(1)}, f32[2,128]{1,0:T(2,128)S(1)}, u32[]{:S(2)}, u32[]{:S(2)}) %collective-permute-start.2) | collective-permute-done | bytes 1056 | tf_op jit(solution)/shard_map/ppermute | solution.py:193
  78.7 0.0 all-to-all-done.3.parts_ref
  78.7 0.7 shard_map.82
  79.5 7.4 %all-to-all-start.4 = ((bf16[4,96,256]{2,1,0:T(8,128)(2,1)}), bf16[4,96,256]{2,1,0:T(8,128)(2,1)S(1)}, u32[]{:S(2)}, u32[]{:S(2)}) async-start(bf16[4,96,256]{2,1,0:T(8,128)(2,1)} %shard_map.82), calls=%async_computation.4 | async-start | bytes 393216 | tf_op jit(solution)/shard_map/all_to_all | solution.py:55
  86.9 4.1 %collective-permute-start.3 = (f32[2,128]{1,0:T(2,128)S(1)}, f32[2,128]{1,0:T(2,128)S(1)}, u32[]{:S(2)}, u32[]{:S(2)}) collective-permute-start(f32[2,128]{1,0:T(2,128)S(1)} %add.10), channel_id=1, source_target_pairs={{0,256},{64,320},{128,384},{192,448},{256,0},{320,64},{384,128},{4... | collective-permute-start | bytes 3080 | tf_op jit(solution)/shard_map/ppermute | solution.py:193
  91.0 2.2 %collective-permute-done.3 = f32[2,128]{1,0:T(2,128)S(1)} collective-permute-done((f32[2,128]{1,0:T(2,128)S(1)}, f32[2,128]{1,0:T(2,128)S(1)}, u32[]{:S(2)}, u32[]{:S(2)}) %collective-permute-start.3) | collective-permute-done | bytes 1056 | tf_op jit(solution)/shard_map/ppermute | solution.py:193
  93.2 2.8 %all-to-all-done.4.parts_ref = bf16[4,96,256]{2,1,0:T(8,128)(2,1)S(1)} async-done(((bf16[4,96,256]{2,1,0:T(8,128)(2,1)}), bf16[4,96,256]{2,1,0:T(8,128)(2,1)S(1)}, u32[]{:S(2)}, u32[]{:S(2)}) %all-to-all-start.4) | async-done | bytes 196640 | tf_op jit(solution)/shard_map/all_to_all | solution.py:55
  96.1 0.8 shard_map.84
  96.9 5.9 %all-to-all-start.5 = ((bf16[8,96,256]{2,1,0:T(8,128)(2,1)}), bf16[8,96,256]{2,1,0:T(8,128)(2,1)S(1)}, u32[]{:S(2)}, u32[]{:S(2)}) async-start(bf16[8,96,256]{2,1,0:T(8,128)(2,1)} %shard_map.84), calls=%async_computation.5 | async-start | bytes 786432 | tf_op jit(solution)/shard_map/all_to_all | solution.py:55
  102.7 0.8 shard_map.83
  103.5 4.8 %all-to-all-done.5.grads_ref = bf16[8,96,256]{2,1,0:T(8,128)(2,1)S(1)} async-done(((bf16[8,96,256]{2,1,0:T(8,128)(2,1)}), bf16[8,96,256]{2,1,0:T(8,128)(2,1)S(1)}, u32[]{:S(2)}, u32[]{:S(2)}) %all-to-all-start.5) | async-done | bytes 393248 | tf_op jit(solution)/shard_map/all_to_all | solution.py:55
  108.3 2.1 %shard_map.85 = bf16[1,3,256,256]{3,2,1,0:T(8,128)(2,1)} custom-call(bf16[8,96,256]{2,1,0:T(8,128)(2,1)S(1)} %all-to-all-done.5.grads_ref, bf16[1,3,256,256]{3,2,1,0:T(8,128)(2,1)S(1)} %get-tuple-element.25.w1_ref.w_ref), custom_call_target="tpu_custom_call" | custom-call | flops 600000000 | bytes 1179648 | tf_op jit(solution)/shard_map/pallas_call | solution.py:65
  (3 shorter events, 0.0 us)
Async XLA Ops:
  18.9 12.1 %copy-start.3 = (bf16[2,128,256]{2,1,0:T(8,128)(2,1)S(1)}, bf16[2,128,256]{2,1,0:T(8,128)(2,1)}, u32[]{:S(2)}) copy-start(bf16[2,128,256]{2,1,0:T(8,128)(2,1)} %get-tuple-element.21.own_ref) | copy-start | bytes 393220
  18.9 30.1 %all-to-all-start.1 = ((bf16[8,96,256]{2,1,0:T(8,128)(2,1)}), bf16[8,96,256]{2,1,0:T(8,128)(2,1)S(1)}, u32[]{:S(2)}, u32[]{:S(2)}) async-start(bf16[8,96,256]{2,1,0:T(8,128)(2,1)} %shard_map.78), calls=%async_computation.1 | async-start | bytes 786432 | tf_op jit(solution)/shard_map/all_to_all | solution.py:55
  31.0 18.0 %collective-permute-start = (bf16[2,128,256]{2,1,0:T(8,128)(2,1)S(1)}, bf16[2,128,256]{2,1,0:T(8,128)(2,1)S(1)}, u32[]{:S(2)}, u32[]{:S(2)}) collective-permute-start(bf16[2,128,256]{2,1,0:T(8,128)(2,1)S(1)} %copy-done.3), channel_id=1, source_target_pairs={{0,1},{1,0},{2,3},{3,2},{4,5},{5,4},{6,7},{7,6},{8,9},{9,8},{10,11... | collective-permute-start | bytes 393224 | tf_op jit(solution)/shard_map/ppermute | solution.py:51
  49.1 11.4 %copy-start = (bf16[1,3,256,256]{3,2,1,0:T(8,128)(2,1)S(1)}, bf16[1,3,256,256]{3,2,1,0:T(8,128)(2,1)}, u32[]{:S(2)}) copy-start(bf16[1,3,256,256]{3,2,1,0:T(8,128)(2,1)} %w0_ref.1) | copy-start | bytes 1179652
  63.1 5.8 %copy-start.1 = (bf16[2,128,256]{2,1,0:T(8,128)(2,1)S(1)}, bf16[2,128,256]{2,1,0:T(8,128)(2,1)}, u32[]{:S(2)}) copy-start(bf16[2,128,256]{2,1,0:T(8,128)(2,1)} %q_ref.1) | copy-start | bytes 393220
  63.1 15.6 %all-to-all-start.3 = ((bf16[8,96,256]{2,1,0:T(8,128)(2,1)}), bf16[8,96,256]{2,1,0:T(8,128)(2,1)S(1)}, u32[]{:S(2)}, u32[]{:S(2)}) async-start(bf16[8,96,256]{2,1,0:T(8,128)(2,1)} %get-tuple-element.24), calls=%async_computation.3 | async-start | bytes 786432 | tf_op jit(solution)/shard_map/all_to_all | solution.py:55
  68.9 0.7 copy-start.2
  70.2 3.0 %collective-permute-start.1 = (f32[2,128]{1,0:T(2,128)S(1)}, f32[2,128]{1,0:T(2,128)S(1)}, u32[]{:S(2)}, u32[]{:S(2)}) collective-permute-start(f32[2,128]{1,0:T(2,128)S(1)} %get-tuple-element.27), channel_id=1, source_target_pairs={{0,64},{64,0},{128,192},{192,128},{256,320},{320,256},{384,448},{4... | collective-permute-start | bytes 3080 | tf_op jit(solution)/shard_map/ppermute | solution.py:193
  73.2 5.5 %collective-permute-start.2 = (f32[2,128]{1,0:T(2,128)S(1)}, f32[2,128]{1,0:T(2,128)S(1)}, u32[]{:S(2)}, u32[]{:S(2)}) collective-permute-start(f32[2,128]{1,0:T(2,128)S(1)} %add.9), channel_id=1, source_target_pairs={{0,128},{64,192},{128,0},{192,64},{256,384},{320,448},{384,256},{4... | collective-permute-start | bytes 3080 | tf_op jit(solution)/shard_map/ppermute | solution.py:193
  79.5 16.6 %all-to-all-start.4 = ((bf16[4,96,256]{2,1,0:T(8,128)(2,1)}), bf16[4,96,256]{2,1,0:T(8,128)(2,1)S(1)}, u32[]{:S(2)}, u32[]{:S(2)}) async-start(bf16[4,96,256]{2,1,0:T(8,128)(2,1)} %shard_map.82), calls=%async_computation.4 | async-start | bytes 393216 | tf_op jit(solution)/shard_map/all_to_all | solution.py:55
  86.9 6.3 %collective-permute-start.3 = (f32[2,128]{1,0:T(2,128)S(1)}, f32[2,128]{1,0:T(2,128)S(1)}, u32[]{:S(2)}, u32[]{:S(2)}) collective-permute-start(f32[2,128]{1,0:T(2,128)S(1)} %add.10), channel_id=1, source_target_pairs={{0,256},{64,320},{128,384},{192,448},{256,0},{320,64},{384,128},{4... | collective-permute-start | bytes 3080 | tf_op jit(solution)/shard_map/ppermute | solution.py:193
  96.9 11.5 %all-to-all-start.5 = ((bf16[8,96,256]{2,1,0:T(8,128)(2,1)}), bf16[8,96,256]{2,1,0:T(8,128)(2,1)S(1)}, u32[]{:S(2)}, u32[]{:S(2)}) async-start(bf16[8,96,256]{2,1,0:T(8,128)(2,1)} %shard_map.84), calls=%async_computation.5 | async-start | bytes 786432 | tf_op jit(solution)/shard_map/all_to_all | solution.py:55

commit v5 on v4

--- a/solution.py
+++ b/solution.py
@@ -10,6 +10,7 @@
 NS_STEPS = 2
 PEERS = 8
 SHARE = 3 * DH // PEERS
+UNITS = DH // PEERS
 
 coef_a = 3.4445
 coef_b = -4.775
@@ -34,21 +35,19 @@
     for x in range(4)
     for y_lo in range(2)
 ]
-ALONG = [
-    [token_index(x, y_hi, y_lo, z_hi) for y_hi in range(4)]
-    for x in range(4)
-    for y_lo in range(2)
-    for z_hi in range(2)
-]
-
 
 def token_pairs(move):
     places = [(x, h, l, z) for x in range(4) for h in range(4) for l in range(2) for z in range(2)]
     return [(token_index(*p), token_index(*move(*p))) for p in places]
 
 
-def from_across(array):
-    return lax.ppermute(array, "tokens", token_pairs(lambda x, h, l, z: (x, h, l, 1 - z)))
+def from_beside(array):
+    return lax.ppermute(array, "tokens", token_pairs(lambda x, h, l, z: (x, h, 1 - l, z)))
+
+
+def from_along(array, steps):
+    pairs = token_pairs(lambda x, h, l, z: ((x + steps) % 4, h, l, z))
+    return lax.ppermute(array, "tokens", pairs)
 
 
 def exchange(array, groups):
@@ -65,7 +64,9 @@
     return pl.pallas_call(
         body,
         out_shape=out_shape,
-        in_specs=[pl.BlockSpec(memory_space=space)] * len(args),
+        in_specs=[
+            pl.BlockSpec(memory_space=pltpu.SMEM if a.dtype == jnp.int32 else space) for a in args
+        ],
         out_specs=jax.tree.map(lambda _: pl.BlockSpec(memory_space=pltpu.VMEM), out_shape),
         scratch_shapes=list(scratch),
         compiler_params=pltpu.CompilerParams(vmem_limit_bytes=limit * 2**20),
@@ -78,10 +79,7 @@
     return (jnp.concatenate([tall, tall], axis=1) * rows.astype(F32)).astype(BF16)
 
 
-def back_terms(keys, scaled, gate_w, up_w, down_w):
-    gate = mm(keys, gate_w)
-    up = mm(keys, up_w)
-    back = mm(scaled, down_w, 1, 1)
+def elementwise(gate, up, back):
     sig = jax.nn.sigmoid(gate)
     hidden = (gate * sig * up).astype(BF16)
     grad_gate = (back * up * sig * (1.0 + gate * (1.0 - sig))).astype(BF16)
@@ -101,7 +99,8 @@
 
 
 def local_grads(keys, scaled, gate_w, up_w, down_w, grads_ref):
-    hidden, grad_gate, grad_up = back_terms(keys, scaled, gate_w, up_w, down_w)
+    gate, up, back = mm(keys, gate_w), mm(keys, up_w), mm(scaled, down_w, 1, 1)
+    hidden, grad_gate, grad_up = elementwise(gate, up, back)
     put_grads(grads_ref, 0, mm(keys, grad_gate, 0, 0))
     put_grads(grads_ref, 1, mm(keys, grad_up, 0, 0))
     put_grads(grads_ref, 2, mm(hidden, scaled, 0, 0))
@@ -129,8 +128,7 @@
         copies_ref[peer] = total
 
 
-def newton_update(grads_ref, w_ref):
-    stacked = grads_ref[...].reshape(3, DH, DH)
+def newton_update(stacked, w_ref):
     current = []
     for m in range(3):
         wide = stacked[m].astype(F32)
@@ -150,17 +148,35 @@
     ]
 
 
-def middle_kernel(grads_ref, w_ref, own_ref, across_ref, fresh_ref, out_ref):
-    fresh = newton_update(grads_ref, w_ref)
+def middle_kernel(grads_ref, w_ref, place_ref, *refs):
+    tokens, (fresh_ref, out_ref, gate_ref, up_ref) = refs[:4], refs[4:]
+    fresh = newton_update(grads_ref[...].reshape(3, DH, DH), w_ref)
     for m in range(3):
         fresh_ref[0, m] = fresh[m]
-    keys = jnp.concatenate([own_ref[0], across_ref[0]], axis=0)
-    scaled = jnp.concatenate([own_ref[1], across_ref[1]], axis=0)
-    local_grads(keys, scaled, fresh[0], fresh[1], fresh[2], out_ref)
+    gate_ref[...] = jnp.transpose(fresh[0])
+    up_ref[...] = jnp.transpose(fresh[1])
+    units = pl.ds(pl.multiple_of(place_ref[0] * UNITS, UNITS), UNITS)
+    gate_w, up_w, down_w = gate_ref[units], up_ref[units], fresh_ref[0, 2, units]
+    sums = [jnp.zeros((UNITS, DH), F32)] * 3
+    for token_ref in tokens:
+        keys = token_ref[:, 0].reshape(256, DH)
+        scaled = token_ref[:, 1].reshape(256, DH)
+        gate = mm(gate_w, keys, 1, 1)
+        up = mm(up_w, keys, 1, 1)
+        back = mm(down_w, scaled, 1, 1)
+        hidden, grad_gate, grad_up = elementwise(gate, up, back)
+        terms = mm(grad_gate, keys), mm(grad_up, keys), mm(hidden, scaled)
+        sums = [s + t for s, t in zip(sums, terms)]
+    for m in range(3):
+        part = sums[m].astype(BF16)
+        for peer in range(PEERS):
+            out_ref[peer, pl.ds(m * UNITS, UNITS)] = part
 
 
 def last_kernel(grads_ref, w_ref, fresh_ref):
-    fresh = newton_update(grads_ref, w_ref)
+    rows = [grads_ref[:, m * UNITS : (m + 1) * UNITS].reshape(DH, DH) for m in range(3)]
+    stacked = [jnp.transpose(rows[0]), jnp.transpose(rows[1]), rows[2]]
+    fresh = newton_update(stacked, w_ref)
     for m in range(3):
         fresh_ref[0, m] = fresh[m]
 
@@ -206,23 +222,27 @@
         first_kernel, (pieces, shaped((2, 128, DH))), keys, values, rates, fast_init, flops=10**8,
         scratch=[*own, pltpu.SemaphoreType.DMA((4,))], space=pl.ANY, limit=58,
     )
-    share = shaped((4, SHARE, DH))
-    parts = exchange(grads, NEAR)
-    shares, ahead = together(call(share_kernel, pieces, parts), ahead)
-    parts, across = together(exchange(shares, FAR), from_across(ahead))
+    parts, beside = together(exchange(grads, NEAR), from_beside(ahead))
+    shares = call(share_kernel, pieces, parts)
+    shares, pair = together(shares, jnp.stack([ahead, beside]))
+    parts, *others = together(
+        exchange(shares, FAR), *(from_along(pair, steps) for steps in (1, 3, 2))
+    )
     whole = exchange(call(share_kernel, pieces, parts), NEAR)
-    fresh, grads = call(
-        middle_kernel, (weights, pieces), whole, fast_init, ahead, across, flops=9 * 10**8
+    token = lax.axis_index("tokens")
+    place = (token // 16 * 2 + token // 2 % 2).reshape(1)
+    fresh, shares = call(
+        middle_kernel, (weights, pieces), whole, fast_init, place, pair, *others, flops=9 * 10**8,
+        scratch=[pltpu.VMEM((DH, DH), BF16)] * 2,
     )
     y, squares = call(
         query_kernel,
         (shaped((2, 128, DH), F32), shaped((2, 128), F32)),
         queries, fast_init, fresh, out_gain.reshape(1, DH), flops=10**8,
     )
-    squares = add_partner(add_partner(squares, 1), 2)
-    parts, y, squares = together(exchange(grads, NEAR), y, squares)
-    shares = call(share_kernel, share, parts)
-    parts, y, squares = together(exchange(shares, ALONG), y, add_partner(squares, 4))
+    for bit in (1, 2, 4):
+        squares = add_partner(squares, bit)
+    parts, y, squares = together(exchange(shares, FAR), y, squares)
     whole = exchange(call(share_kernel, pieces, parts), NEAR)
     mixed = call(finish_kernel, shaped((2, 128, DH)), y, squares)
     final = call(last_kernel, weights, whole, fresh, flops=6 * 10**8)

time: 112 us -> 110 us (0.982)
  the two profiles are of different devices: /device:TPU:6 before, /device:TPU:16 now
where the time goes in v5:
time: 110 us; the launch traced here: 109 us
  starting transfers between devices  63.2 us (57%)
  waiting for transfers between devices  33.1 us (30%)
  Pallas kernels  11.5 us (10%)
    all_to_all x5, starting transfers between devices, exchange(): lax.all_to_all(array, 'tokens', 0, 0, axis_index_groups=groups, tiled=True)  39.6 us
    all_to_all x5, waiting for transfers between devices, exchange(): lax.all_to_all(array, 'tokens', 0, 0, axis_index_groups=groups, tiled=True)  15.8 us
    pallas_call x8, Pallas kernels, call(): pl.pallas_call(body, out_shape=out_shape, in_specs=[pl.BlockSpec(memory_s...  11.5 us
    ppermute x3, starting transfers between devices, from_along(): return lax.ppermute(array, 'tokens', pairs)  9.98 us
    ppermute x3, starting transfers between devices, add_partner(): return squares + lax.ppermute(squares, 'heads', pairs)  9.65 us
    ppermute x3, waiting for transfers between devices, from_along(): return lax.ppermute(array, 'tokens', pairs)  6.73 us
    ppermute x1, waiting for transfers between devices, from_beside(): lax.ppermute(array, 'tokens', token_pairs(lambda x, h, l, z: (x, h, 1 - l...  5.45 us
    ppermute x3, waiting for transfers between devices, add_partner(): return squares + lax.ppermute(squares, 'heads', pairs)  5.15 us
  transfers between devices with their start and end apart: 12, of which 10 were waited for; matrix products, arithmetic and copies ran while one was open for 0% of the time, Pallas kernels for 1%

profile of v5, /device:TPU:16, one launch (start us, length us, event | category | flops | bytes accessed | tf_op | source)
XLA Modules:
  0.0 109.3 jit_solution(11379411373956647676)
XLA Ops:
  0.6 2.4 %shard_map.77 = (bf16[8,96,256]{2,1,0:T(8,128)(2,1)}, bf16[2,128,256]{2,1,0:T(8,128)(2,1)}) custom-call(bf16[2,128,256]{2,1,0:T(8,128)(2,1)} %k_hbm.1, bf16[2,128,256]{2,1,0:T(8,128)(2,1)} %v_hbm.1, f32[2,1,128]{2,1,0:T(1,128)} %r_hbm.1, bf16[1,3,256,256]{3,2,1,0:T(8,128)(2,1)} %w0_ref.1), custom_call_target="tpu_custom_call" | custom-call | flops 100000000 | bytes 1180672 | tf_op jit(solution)/shard_map/pallas_call | solution.py:64
  3.1 0.0 copy-start.3
  3.1 5.5 %all-to-all-start = ((bf16[8,96,256]{2,1,0:T(8,128)(2,1)}), bf16[8,96,256]{2,1,0:T(8,128)(2,1)S(1)}, u32[]{:S(2)}, u32[]{:S(2)}) async-start(bf16[8,96,256]{2,1,0:T(8,128)(2,1)} %get-tuple-element.19), calls=%async_computation | async-start | bytes 786432 | tf_op jit(solution)/shard_map/all_to_all | solution.py:54
  8.5 0.0 copy-done.3
  8.5 3.9 %collective-permute-start = (bf16[2,128,256]{2,1,0:T(8,128)(2,1)S(1)}, bf16[2,128,256]{2,1,0:T(8,128)(2,1)S(1)}, u32[]{:S(2)}, u32[]{:S(2)}) collective-permute-start(bf16[2,128,256]{2,1,0:T(8,128)(2,1)S(1)} %copy-done.3), channel_id=1, source_target_pairs={{0,2},{1,3},{2,0},{3,1},{4,6},{5,7},{6,4},{7,5},{8,10},{9,11},{10,... | collective-permute-start | bytes 393224 | tf_op jit(solution)/shard_map/ppermute | solution.py:45
  12.5 5.4 %collective-permute-done = bf16[2,128,256]{2,1,0:T(8,128)(2,1)S(1)} collective-permute-done((bf16[2,128,256]{2,1,0:T(8,128)(2,1)S(1)}, bf16[2,128,256]{2,1,0:T(8,128)(2,1)S(1)}, u32[]{:S(2)}, u32[]{:S(2)}) %collective-permute-start) | collective-permute-done | bytes 131104 | tf_op jit(solution)/shard_map/ppermute | solution.py:45
  17.9 0.7 all-to-all-done.parts_ref
  18.6 0.8 shard_map.78
  19.5 15.0 %all-to-all-start.1 = ((bf16[8,96,256]{2,1,0:T(8,128)(2,1)}), bf16[8,96,256]{2,1,0:T(8,128)(2,1)S(1)}, u32[]{:S(2)}, u32[]{:S(2)}) async-start(bf16[8,96,256]{2,1,0:T(8,128)(2,1)} %shard_map.78), calls=%async_computation.1 | async-start | bytes 786432 | tf_op jit(solution)/shard_map/all_to_all | solution.py:54
  34.5 4.1 %collective-permute-start.3 = (bf16[2,2,128,256]{3,2,1,0:T(8,128)(2,1)S(1)}, bf16[2,2,128,256]{3,2,1,0:T(8,128)(2,1)S(1)}, u32[]{:S(2)}, u32[]{:S(2)}) collective-permute-start(bf16[2,2,128,256]{3,2,1,0:T(8,128)(2,1)S(1)} %pad_maximum_fusion.refs_0_), channel_id=1, source_target_pairs={{0,32},{1,33},{2,34},{3,35},{4,36},{5,37},{6,38},{7,39},{8,40},{9,... | collective-permute-start | bytes 786440 | tf_op jit(solution)/shard_map/ppermute | solution.py:50
  38.6 3.1 %collective-permute-start.2 = (bf16[2,2,128,256]{3,2,1,0:T(8,128)(2,1)S(1)}, bf16[2,2,128,256]{3,2,1,0:T(8,128)(2,1)S(1)}, u32[]{:S(2)}, u32[]{:S(2)}) collective-permute-start(bf16[2,2,128,256]{3,2,1,0:T(8,128)(2,1)S(1)} %pad_maximum_fusion.refs_0_), channel_id=1, source_target_pairs={{0,48},{1,49},{2,50},{3,51},{4,52},{5,53},{6,54},{7,55},{8,56},{9,... | collective-permute-start | bytes 786440 | tf_op jit(solution)/shard_map/ppermute | solution.py:50
  41.7 2.7 %collective-permute-start.1 = (bf16[2,2,128,256]{3,2,1,0:T(8,128)(2,1)S(1)}, bf16[2,2,128,256]{3,2,1,0:T(8,128)(2,1)S(1)}, u32[]{:S(2)}, u32[]{:S(2)}) collective-permute-start(bf16[2,2,128,256]{3,2,1,0:T(8,128)(2,1)S(1)} %pad_maximum_fusion.refs_0_), channel_id=1, source_target_pairs={{0,16},{1,17},{2,18},{3,19},{4,20},{5,21},{6,22},{7,23},{8,24},{9,... | collective-permute-start | bytes 786440 | tf_op jit(solution)/shard_map/ppermute | solution.py:50
  44.5 0.5 collective-permute-done.3.refs_3_
  44.9 4.2 %collective-permute-done.2.refs_2_ = bf16[2,2,128,256]{3,2,1,0:T(8,128)(2,1)S(1)} collective-permute-done((bf16[2,2,128,256]{3,2,1,0:T(8,128)(2,1)S(1)}, bf16[2,2,128,256]{3,2,1,0:T(8,128)(2,1)S(1)}, u32[]{:S(2)}, u32[]{:S(2)}) %collective-permute-start.2) | collective-permute-done | bytes 262176 | tf_op jit(solution)/shard_map/ppermute | solution.py:50
  49.1 2.1 %collective-permute-done.1.refs_1_ = bf16[2,2,128,256]{3,2,1,0:T(8,128)(2,1)S(1)} collective-permute-done((bf16[2,2,128,256]{3,2,1,0:T(8,128)(2,1)S(1)}, bf16[2,2,128,256]{3,2,1,0:T(8,128)(2,1)S(1)}, u32[]{:S(2)}, u32[]{:S(2)}) %collective-permute-start.1) | collective-permute-done | bytes 262176 | tf_op jit(solution)/shard_map/ppermute | solution.py:50
  51.2 0.0 all-to-all-done.1.parts_ref
  51.2 0.8 shard_map.79
  52.0 0.0 copy-start
  52.0 3.6 %all-to-all-start.2 = ((bf16[8,96,256]{2,1,0:T(8,128)(2,1)}), bf16[8,96,256]{2,1,0:T(8,128)(2,1)S(1)}, u32[]{:S(2)}, u32[]{:S(2)}) async-start(bf16[8,96,256]{2,1,0:T(8,128)(2,1)} %shard_map.79), calls=%async_computation.2 | async-start | bytes 786432 | tf_op jit(solution)/shard_map/all_to_all | solution.py:54
  55.6 7.9 %all-to-all-done.2.grads_ref = bf16[8,96,256]{2,1,0:T(8,128)(2,1)S(1)} async-done(((bf16[8,96,256]{2,1,0:T(8,128)(2,1)}), bf16[8,96,256]{2,1,0:T(8,128)(2,1)S(1)}, u32[]{:S(2)}, u32[]{:S(2)}) %all-to-all-start.2) | async-done | bytes 393248 | tf_op jit(solution)/shard_map/all_to_all | solution.py:54
  63.5 0.0 copy-done
  63.5 3.1 %shard_map.80 = (bf16[1,3,256,256]{3,2,1,0:T(8,128)(2,1)S(1)}, bf16[8,96,256]{2,1,0:T(8,128)(2,1)}) custom-call(bf16[8,96,256]{2,1,0:T(8,128)(2,1)S(1)} %all-to-all-done.2.grads_ref, bf16[1,3,256,256]{3,2,1,0:T(8,128)(2,1)S(1)} %copy-done, s32[1]{0:T(128)} %bitcast.2.place_ref, bf16[2,2,128,256]{3,2,1,0:T(8,128)(2,1)S(1)} %pad_maximum_fusion.refs_0_, ...), custom_call_target="tpu_custom_call" | custom-call | flops 900000000 | bytes 2621444 | tf_op jit(solution)/shard_map/pallas_call | solution.py:64
  66.6 0.0 copy-start.1
  66.6 12.1 %all-to-all-start.3 = ((bf16[8,96,256]{2,1,0:T(8,128)(2,1)}), bf16[8,96,256]{2,1,0:T(8,128)(2,1)S(1)}, u32[]{:S(2)}, u32[]{:S(2)}) async-start(bf16[8,96,256]{2,1,0:T(8,128)(2,1)} %get-tuple-element.29), calls=%async_computation.3 | async-start | bytes 786432 | tf_op jit(solution)/shard_map/all_to_all | solution.py:54
  78.8 0.0 copy-start.2
  78.8 0.0 copy-done.1
  78.8 0.7 copy-done.2
  79.4 0.6 shard_map.81
  80.0 1.9 %collective-permute-start.4 = (f32[2,128]{1,0:T(2,128)S(1)}, f32[2,128]{1,0:T(2,128)S(1)}, u32[]{:S(2)}, u32[]{:S(2)}) collective-permute-start(f32[2,128]{1,0:T(2,128)S(1)} %get-tuple-element.32), channel_id=1, source_target_pairs={{0,64},{64,0},{128,192},{192,128},{256,320},{320,256},{384,448},{4... | collective-permute-start | bytes 3080 | tf_op jit(solution)/shard_map/ppermute | solution.py:209
  82.0 1.1 %collective-permute-done.4 = f32[2,128]{1,0:T(2,128)S(1)} collective-permute-done((f32[2,128]{1,0:T(2,128)S(1)}, f32[2,128]{1,0:T(2,128)S(1)}, u32[]{:S(2)}, u32[]{:S(2)}) %collective-permute-start.4) | collective-permute-done | bytes 1056 | tf_op jit(solution)/shard_map/ppermute | solution.py:209
  83.1 3.4 %collective-permute-start.5 = (f32[2,128]{1,0:T(2,128)S(1)}, f32[2,128]{1,0:T(2,128)S(1)}, u32[]{:S(2)}, u32[]{:S(2)}) collective-permute-start(f32[2,128]{1,0:T(2,128)S(1)} %add.20), channel_id=1, source_target_pairs={{0,128},{64,192},{128,0},{192,64},{256,384},{320,448},{384,256},{4... | collective-permute-start | bytes 3080 | tf_op jit(solution)/shard_map/ppermute | solution.py:209
  86.4 2.1 %collective-permute-done.5 = f32[2,128]{1,0:T(2,128)S(1)} collective-permute-done((f32[2,128]{1,0:T(2,128)S(1)}, f32[2,128]{1,0:T(2,128)S(1)}, u32[]{:S(2)}, u32[]{:S(2)}) %collective-permute-start.5) | collective-permute-done | bytes 1056 | tf_op jit(solution)/shard_map/ppermute | solution.py:209
  88.5 4.4 %collective-permute-start.6 = (f32[2,128]{1,0:T(2,128)S(1)}, f32[2,128]{1,0:T(2,128)S(1)}, u32[]{:S(2)}, u32[]{:S(2)}) collective-permute-start(f32[2,128]{1,0:T(2,128)S(1)} %add.21), channel_id=1, source_target_pairs={{0,256},{64,320},{128,384},{192,448},{256,0},{320,64},{384,128},{4... | collective-permute-start | bytes 3080 | tf_op jit(solution)/shard_map/ppermute | solution.py:209
  92.9 2.0 %collective-permute-done.6 = f32[2,128]{1,0:T(2,128)S(1)} collective-permute-done((f32[2,128]{1,0:T(2,128)S(1)}, f32[2,128]{1,0:T(2,128)S(1)}, u32[]{:S(2)}, u32[]{:S(2)}) %collective-permute-start.6) | collective-permute-done | bytes 1056 | tf_op jit(solution)/shard_map/ppermute | solution.py:209
  94.9 0.0 all-to-all-done.3.parts_ref
  94.9 0.8 shard_map.83
  95.7 3.5 %all-to-all-start.4 = ((bf16[8,96,256]{2,1,0:T(8,128)(2,1)}), bf16[8,96,256]{2,1,0:T(8,128)(2,1)S(1)}, u32[]{:S(2)}, u32[]{:S(2)}) async-start(bf16[8,96,256]{2,1,0:T(8,128)(2,1)} %shard_map.83), calls=%async_computation.4 | async-start | bytes 786432 | tf_op jit(solution)/shard_map/all_to_all | solution.py:54
  99.1 0.8 shard_map.82
  99.9 7.1 %all-to-all-done.4.grads_ref = bf16[8,96,256]{2,1,0:T(8,128)(2,1)S(1)} async-done(((bf16[8,96,256]{2,1,0:T(8,128)(2,1)}), bf16[8,96,256]{2,1,0:T(8,128)(2,1)S(1)}, u32[]{:S(2)}, u32[]{:S(2)}) %all-to-all-start.4) | async-done | bytes 393248 | tf_op jit(solution)/shard_map/all_to_all | solution.py:54
  107.1 2.2 %shard_map.84 = bf16[1,3,256,256]{3,2,1,0:T(8,128)(2,1)} custom-call(bf16[8,96,256]{2,1,0:T(8,128)(2,1)S(1)} %all-to-all-done.4.grads_ref, bf16[1,3,256,256]{3,2,1,0:T(8,128)(2,1)S(1)} %get-tuple-element.30.w1_ref.w_ref), custom_call_target="tpu_custom_call" | custom-call | flops 600000000 | bytes 1179648 | tf_op jit(solution)/shard_map/pallas_call | solution.py:64
  (4 shorter events, 0.0 us)
Async XLA Ops:
  3.1 5.5 %copy-start.3 = (bf16[2,128,256]{2,1,0:T(8,128)(2,1)S(1)}, bf16[2,128,256]{2,1,0:T(8,128)(2,1)}, u32[]{:S(2)}) copy-start(bf16[2,128,256]{2,1,0:T(8,128)(2,1)} %get-tuple-element.20) | copy-start | bytes 393220
  3.1 15.6 %all-to-all-start = ((bf16[8,96,256]{2,1,0:T(8,128)(2,1)}), bf16[8,96,256]{2,1,0:T(8,128)(2,1)S(1)}, u32[]{:S(2)}, u32[]{:S(2)}) async-start(bf16[8,96,256]{2,1,0:T(8,128)(2,1)} %get-tuple-element.19), calls=%async_computation | async-start | bytes 786432 | tf_op jit(solution)/shard_map/all_to_all | solution.py:54
  8.5 9.4 %collective-permute-start = (bf16[2,128,256]{2,1,0:T(8,128)(2,1)S(1)}, bf16[2,128,256]{2,1,0:T(8,128)(2,1)S(1)}, u32[]{:S(2)}, u32[]{:S(2)}) collective-permute-start(bf16[2,128,256]{2,1,0:T(8,128)(2,1)S(1)} %copy-done.3), channel_id=1, source_target_pairs={{0,2},{1,3},{2,0},{3,1},{4,6},{5,7},{6,4},{7,5},{8,10},{9,11},{10,... | collective-permute-start | bytes 393224 | tf_op jit(solution)/shard_map/ppermute | solution.py:45
  19.5 31.7 %all-to-all-start.1 = ((bf16[8,96,256]{2,1,0:T(8,128)(2,1)}), bf16[8,96,256]{2,1,0:T(8,128)(2,1)S(1)}, u32[]{:S(2)}, u32[]{:S(2)}) async-start(bf16[8,96,256]{2,1,0:T(8,128)(2,1)} %shard_map.78), calls=%async_computation.1 | async-start | bytes 786432 | tf_op jit(solution)/shard_map/all_to_all | solution.py:54
  34.5 10.5 %collective-permute-start.3 = (bf16[2,2,128,256]{3,2,1,0:T(8,128)(2,1)S(1)}, bf16[2,2,128,256]{3,2,1,0:T(8,128)(2,1)S(1)}, u32[]{:S(2)}, u32[]{:S(2)}) collective-permute-start(bf16[2,2,128,256]{3,2,1,0:T(8,128)(2,1)S(1)} %pad_maximum_fusion.refs_0_), channel_id=1, source_target_pairs={{0,32},{1,33},{2,34},{3,35},{4,36},{5,37},{6,38},{7,39},{8,40},{9,... | collective-permute-start | bytes 786440 | tf_op jit(solution)/shard_map/ppermute | solution.py:50
  38.6 10.5 %collective-permute-start.2 = (bf16[2,2,128,256]{3,2,1,0:T(8,128)(2,1)S(1)}, bf16[2,2,128,256]{3,2,1,0:T(8,128)(2,1)S(1)}, u32[]{:S(2)}, u32[]{:S(2)}) collective-permute-start(bf16[2,2,128,256]{3,2,1,0:T(8,128)(2,1)S(1)} %pad_maximum_fusion.refs_0_), channel_id=1, source_target_pairs={{0,48},{1,49},{2,50},{3,51},{4,52},{5,53},{6,54},{7,55},{8,56},{9,... | collective-permute-start | bytes 786440 | tf_op jit(solution)/shard_map/ppermute | solution.py:50
  41.7 9.5 %collective-permute-start.1 = (bf16[2,2,128,256]{3,2,1,0:T(8,128)(2,1)S(1)}, bf16[2,2,128,256]{3,2,1,0:T(8,128)(2,1)S(1)}, u32[]{:S(2)}, u32[]{:S(2)}) collective-permute-start(bf16[2,2,128,256]{3,2,1,0:T(8,128)(2,1)S(1)} %pad_maximum_fusion.refs_0_), channel_id=1, source_target_pairs={{0,16},{1,17},{2,18},{3,19},{4,20},{5,21},{6,22},{7,23},{8,24},{9,... | collective-permute-start | bytes 786440 | tf_op jit(solution)/shard_map/ppermute | solution.py:50
  52.0 11.5 %copy-start = (bf16[1,3,256,256]{3,2,1,0:T(8,128)(2,1)S(1)}, bf16[1,3,256,256]{3,2,1,0:T(8,128)(2,1)}, u32[]{:S(2)}) copy-start(bf16[1,3,256,256]{3,2,1,0:T(8,128)(2,1)} %w0_ref.1) | copy-start | bytes 1179652
  52.0 11.5 %all-to-all-start.2 = ((bf16[8,96,256]{2,1,0:T(8,128)(2,1)}), bf16[8,96,256]{2,1,0:T(8,128)(2,1)S(1)}, u32[]{:S(2)}, u32[]{:S(2)}) async-start(bf16[8,96,256]{2,1,0:T(8,128)(2,1)} %shard_map.79), calls=%async_computation.2 | async-start | bytes 786432 | tf_op jit(solution)/shard_map/all_to_all | solution.py:54
  66.6 12.2 %copy-start.1 = (bf16[2,128,256]{2,1,0:T(8,128)(2,1)S(1)}, bf16[2,128,256]{2,1,0:T(8,128)(2,1)}, u32[]{:S(2)}) copy-start(bf16[2,128,256]{2,1,0:T(8,128)(2,1)} %q_ref.1) | copy-start | bytes 393220
  66.6 28.3 %all-to-all-start.3 = ((bf16[8,96,256]{2,1,0:T(8,128)(2,1)}), bf16[8,96,256]{2,1,0:T(8,128)(2,1)S(1)}, u32[]{:S(2)}, u32[]{:S(2)}) async-start(bf16[8,96,256]{2,1,0:T(8,128)(2,1)} %get-tuple-element.29), calls=%async_computation.3 | async-start | bytes 786432 | tf_op jit(solution)/shard_map/all_to_all | solution.py:54
  78.8 0.7 copy-start.2
  80.0 3.0 %collective-permute-start.4 = (f32[2,128]{1,0:T(2,128)S(1)}, f32[2,128]{1,0:T(2,128)S(1)}, u32[]{:S(2)}, u32[]{:S(2)}) collective-permute-start(f32[2,128]{1,0:T(2,128)S(1)} %get-tuple-element.32), channel_id=1, source_target_pairs={{0,64},{64,0},{128,192},{192,128},{256,320},{320,256},{384,448},{4... | collective-permute-start | bytes 3080 | tf_op jit(solution)/shard_map/ppermute | solution.py:209
  83.1 5.5 %collective-permute-start.5 = (f32[2,128]{1,0:T(2,128)S(1)}, f32[2,128]{1,0:T(2,128)S(1)}, u32[]{:S(2)}, u32[]{:S(2)}) collective-permute-start(f32[2,128]{1,0:T(2,128)S(1)} %add.20), channel_id=1, source_target_pairs={{0,128},{64,192},{128,0},{192,64},{256,384},{320,448},{384,256},{4... | collective-permute-start | bytes 3080 | tf_op jit(solution)/shard_map/ppermute | solution.py:209
  88.5 6.3 %collective-permute-start.6 = (f32[2,128]{1,0:T(2,128)S(1)}, f32[2,128]{1,0:T(2,128)S(1)}, u32[]{:S(2)}, u32[]{:S(2)}) collective-permute-start(f32[2,128]{1,0:T(2,128)S(1)} %add.21), channel_id=1, source_target_pairs={{0,256},{64,320},{128,384},{192,448},{256,0},{320,64},{384,128},{4... | collective-permute-start | bytes 3080 | tf_op jit(solution)/shard_map/ppermute | solution.py:209
  95.7 11.4 %all-to-all-start.4 = ((bf16[8,96,256]{2,1,0:T(8,128)(2,1)}), bf16[8,96,256]{2,1,0:T(8,128)(2,1)S(1)}, u32[]{:S(2)}, u32[]{:S(2)}) async-start(bf16[8,96,256]{2,1,0:T(8,128)(2,1)} %shard_map.83), calls=%async_computation.4 | async-start | bytes 786432 | tf_op jit(solution)/shard_map/all_to_all | solution.py:54

commit v6 on v5

--- a/solution.py
+++ b/solution.py
@@ -225,9 +225,8 @@
     parts, beside = together(exchange(grads, NEAR), from_beside(ahead))
     shares = call(share_kernel, pieces, parts)
     shares, pair = together(shares, jnp.stack([ahead, beside]))
-    parts, *others = together(
-        exchange(shares, FAR), *(from_along(pair, steps) for steps in (1, 3, 2))
-    )
+    parts, first = together(exchange(shares, FAR), from_along(pair, 2))
+    others = [first, from_along(pair, 1), from_along(pair, 3)]
     whole = exchange(call(share_kernel, pieces, parts), NEAR)
     token = lax.axis_index("tokens")
     place = (token // 16 * 2 + token // 2 % 2).reshape(1)
@@ -240,12 +239,12 @@
         (shaped((2, 128, DH), F32), shaped((2, 128), F32)),
         queries, fast_init, fresh, out_gain.reshape(1, DH), flops=10**8,
     )
-    for bit in (1, 2, 4):
-        squares = add_partner(squares, bit)
-    parts, y, squares = together(exchange(shares, FAR), y, squares)
+    parts, y, squares = together(exchange(shares, FAR), y, add_partner(squares, 1))
     whole = exchange(call(share_kernel, pieces, parts), NEAR)
+    whole, squares = together(whole, add_partner(squares, 2))
+    final = call(last_kernel, weights, whole, fresh, flops=6 * 10**8)
+    final, squares = together(final, add_partner(squares, 4))
     mixed = call(finish_kernel, shaped((2, 128, DH)), y, squares)
-    final = call(last_kernel, weights, whole, fresh, flops=6 * 10**8)
     return mixed, final
 
 

time: 110 us -> 113 us (1.027)
  the two profiles are of different devices: /device:TPU:16 before, /device:TPU:6 now
where the time goes in v6:
time: 113 us; the launch traced here: 111 us
  starting transfers between devices  60.3 us (53%)
  waiting for transfers between devices  38.2 us (34%)
  Pallas kernels  11.5 us (10%)
    all_to_all x5, starting transfers between devices, exchange(): lax.all_to_all(array, 'tokens', 0, 0, axis_index_groups=groups, tiled=True)  37.5 us
    all_to_all x5, waiting for transfers between devices, exchange(): lax.all_to_all(array, 'tokens', 0, 0, axis_index_groups=groups, tiled=True)  20.3 us
    pallas_call x8, Pallas kernels, call(): pl.pallas_call(body, out_shape=out_shape, in_specs=[pl.BlockSpec(memory_s...  11.5 us
    ppermute x3, waiting for transfers between devices, from_along(): return lax.ppermute(array, 'tokens', pairs)  10.5 us
    ppermute x3, starting transfers between devices, from_along(): return lax.ppermute(array, 'tokens', pairs)  10.4 us
    ppermute x3, starting transfers between devices, add_partner(): return squares + lax.ppermute(squares, 'heads', pairs)  8.99 us
    ppermute x3, waiting for transfers between devices, add_partner(): return squares + lax.ppermute(squares, 'heads', pairs)  3.89 us
    ppermute x1, waiting for transfers between devices, from_beside(): lax.ppermute(array, 'tokens', token_pairs(lambda x, h, l, z: (x, h, 1 - l...  3.48 us
  transfers between devices with their start and end apart: 12, of which 9 were waited for; matrix products, arithmetic and copies ran while one was open for 0% of the time, Pallas kernels for 2%

profile of v6, /device:TPU:6, one launch (start us, length us, event | category | flops | bytes accessed | tf_op | source)
XLA Modules:
  0.0 111.5 jit_solution(1681545951586076358)
XLA Ops:
  0.6 2.4 %shard_map.77 = (bf16[8,96,256]{2,1,0:T(8,128)(2,1)}, bf16[2,128,256]{2,1,0:T(8,128)(2,1)}) custom-call(bf16[2,128,256]{2,1,0:T(8,128)(2,1)} %k_hbm.1, bf16[2,128,256]{2,1,0:T(8,128)(2,1)} %v_hbm.1, f32[2,1,128]{2,1,0:T(1,128)} %r_hbm.1, bf16[1,3,256,256]{3,2,1,0:T(8,128)(2,1)} %w0_ref.1), custom_call_target="tpu_custom_call" | custom-call | flops 100000000 | bytes 1180672 | tf_op jit(solution)/shard_map/pallas_call | solution.py:64
  3.1 0.0 copy-start.3
  3.1 9.4 %all-to-all-start = ((bf16[8,96,256]{2,1,0:T(8,128)(2,1)}), bf16[8,96,256]{2,1,0:T(8,128)(2,1)S(1)}, u32[]{:S(2)}, u32[]{:S(2)}) async-start(bf16[8,96,256]{2,1,0:T(8,128)(2,1)} %get-tuple-element.21), calls=%async_computation | async-start | bytes 786432 | tf_op jit(solution)/shard_map/all_to_all | solution.py:54
  12.5 0.0 copy-done.3
  12.5 3.4 %collective-permute-start = (bf16[2,128,256]{2,1,0:T(8,128)(2,1)S(1)}, bf16[2,128,256]{2,1,0:T(8,128)(2,1)S(1)}, u32[]{:S(2)}, u32[]{:S(2)}) collective-permute-start(bf16[2,128,256]{2,1,0:T(8,128)(2,1)S(1)} %copy-done.3), channel_id=1, source_target_pairs={{0,2},{1,3},{2,0},{3,1},{4,6},{5,7},{6,4},{7,5},{8,10},{9,11},{10,... | collective-permute-start | bytes 393224 | tf_op jit(solution)/shard_map/ppermute | solution.py:45
  15.8 3.5 %collective-permute-done = bf16[2,128,256]{2,1,0:T(8,128)(2,1)S(1)} collective-permute-done((bf16[2,128,256]{2,1,0:T(8,128)(2,1)S(1)}, bf16[2,128,256]{2,1,0:T(8,128)(2,1)S(1)}, u32[]{:S(2)}, u32[]{:S(2)}) %collective-permute-start) | collective-permute-done | bytes 131104 | tf_op jit(solution)/shard_map/ppermute | solution.py:45
  19.3 0.0 all-to-all-done.parts_ref
  19.3 0.8 shard_map.78
  20.1 13.2 %all-to-all-start.1 = ((bf16[8,96,256]{2,1,0:T(8,128)(2,1)}), bf16[8,96,256]{2,1,0:T(8,128)(2,1)S(1)}, u32[]{:S(2)}, u32[]{:S(2)}) async-start(bf16[8,96,256]{2,1,0:T(8,128)(2,1)} %shard_map.78), calls=%async_computation.1 | async-start | bytes 786432 | tf_op jit(solution)/shard_map/all_to_all | solution.py:54
  33.3 3.4 %collective-permute-start.1 = (bf16[2,2,128,256]{3,2,1,0:T(8,128)(2,1)S(1)}, bf16[2,2,128,256]{3,2,1,0:T(8,128)(2,1)S(1)}, u32[]{:S(2)}, u32[]{:S(2)}) collective-permute-start(bf16[2,2,128,256]{3,2,1,0:T(8,128)(2,1)S(1)} %pad_maximum_fusion.refs_0_), channel_id=1, source_target_pairs={{0,32},{1,33},{2,34},{3,35},{4,36},{5,37},{6,38},{7,39},{8,40},{9,... | collective-permute-start | bytes 786440 | tf_op jit(solution)/shard_map/ppermute | solution.py:50
  36.7 6.6 %collective-permute-done.1.refs_1_ = bf16[2,2,128,256]{3,2,1,0:T(8,128)(2,1)S(1)} collective-permute-done((bf16[2,2,128,256]{3,2,1,0:T(8,128)(2,1)S(1)}, bf16[2,2,128,256]{3,2,1,0:T(8,128)(2,1)S(1)}, u32[]{:S(2)}, u32[]{:S(2)}) %collective-permute-start.1) | collective-permute-done | bytes 262176 | tf_op jit(solution)/shard_map/ppermute | solution.py:50
  43.3 7.3 %all-to-all-done.1.parts_ref = bf16[8,96,256]{2,1,0:T(8,128)(2,1)S(1)} async-done(((bf16[8,96,256]{2,1,0:T(8,128)(2,1)}), bf16[8,96,256]{2,1,0:T(8,128)(2,1)S(1)}, u32[]{:S(2)}, u32[]{:S(2)}) %all-to-all-start.1) | async-done | bytes 393248 | tf_op jit(solution)/shard_map/all_to_all | solution.py:54
  50.6 0.8 shard_map.79
  51.4 0.0 copy-start
  51.4 4.8 %all-to-all-start.2 = ((bf16[8,96,256]{2,1,0:T(8,128)(2,1)}), bf16[8,96,256]{2,1,0:T(8,128)(2,1)S(1)}, u32[]{:S(2)}, u32[]{:S(2)}) async-start(bf16[8,96,256]{2,1,0:T(8,128)(2,1)} %shard_map.79), calls=%async_computation.2 | async-start | bytes 786432 | tf_op jit(solution)/shard_map/all_to_all | solution.py:54
  56.3 2.8 %collective-permute-start.3 = (bf16[2,2,128,256]{3,2,1,0:T(8,128)(2,1)S(1)}, bf16[2,2,128,256]{3,2,1,0:T(8,128)(2,1)S(1)}, u32[]{:S(2)}, u32[]{:S(2)}) collective-permute-start(bf16[2,2,128,256]{3,2,1,0:T(8,128)(2,1)S(1)} %pad_maximum_fusion.refs_0_), channel_id=1, source_target_pairs={{0,48},{1,49},{2,50},{3,51},{4,52},{5,53},{6,54},{7,55},{8,56},{9,... | collective-permute-start | bytes 786440 | tf_op jit(solution)/shard_map/ppermute | solution.py:50
  59.0 4.3 %collective-permute-start.2 = (bf16[2,2,128,256]{3,2,1,0:T(8,128)(2,1)S(1)}, bf16[2,2,128,256]{3,2,1,0:T(8,128)(2,1)S(1)}, u32[]{:S(2)}, u32[]{:S(2)}) collective-permute-start(bf16[2,2,128,256]{3,2,1,0:T(8,128)(2,1)S(1)} %pad_maximum_fusion.refs_0_), channel_id=1, source_target_pairs={{0,16},{1,17},{2,18},{3,19},{4,20},{5,21},{6,22},{7,23},{8,24},{9,... | collective-permute-start | bytes 786440 | tf_op jit(solution)/shard_map/ppermute | solution.py:50
  63.4 2.8 %collective-permute-done.3.refs_3_ = bf16[2,2,128,256]{3,2,1,0:T(8,128)(2,1)S(1)} collective-permute-done((bf16[2,2,128,256]{3,2,1,0:T(8,128)(2,1)S(1)}, bf16[2,2,128,256]{3,2,1,0:T(8,128)(2,1)S(1)}, u32[]{:S(2)}, u32[]{:S(2)}) %collective-permute-start.3) | collective-permute-done | bytes 262176 | tf_op jit(solution)/shard_map/ppermute | solution.py:50
  66.2 1.1 collective-permute-done.2.refs_2_
  67.3 0.0 all-to-all-done.2.grads_ref
  67.3 0.0 copy-done
  67.3 3.1 %shard_map.80 = (bf16[1,3,256,256]{3,2,1,0:T(8,128)(2,1)S(1)}, bf16[8,96,256]{2,1,0:T(8,128)(2,1)}) custom-call(bf16[8,96,256]{2,1,0:T(8,128)(2,1)S(1)} %all-to-all-done.2.grads_ref, bf16[1,3,256,256]{3,2,1,0:T(8,128)(2,1)S(1)} %copy-done, s32[1]{0:T(128)} %bitcast.2.place_ref, bf16[2,2,128,256]{3,2,1,0:T(8,128)(2,1)S(1)} %pad_maximum_fusion.refs_0_, ...), custom_call_target="tpu_custom_call" | custom-call | flops 900000000 | bytes 2621444 | tf_op jit(solution)/shard_map/pallas_call | solution.py:64
  70.4 0.0 copy-start.1
  70.4 4.8 %all-to-all-start.3 = ((bf16[8,96,256]{2,1,0:T(8,128)(2,1)}), bf16[8,96,256]{2,1,0:T(8,128)(2,1)S(1)}, u32[]{:S(2)}, u32[]{:S(2)}) async-start(bf16[8,96,256]{2,1,0:T(8,128)(2,1)} %get-tuple-element.29), calls=%async_computation.3 | async-start | bytes 786432 | tf_op jit(solution)/shard_map/all_to_all | solution.py:54
  75.2 0.0 copy-start.2
  75.2 0.0 copy-done.1
  75.2 0.7 copy-done.2
  75.9 0.6 shard_map.81
  76.5 1.9 %collective-permute-start.4 = (f32[2,128]{1,0:T(2,128)S(1)}, f32[2,128]{1,0:T(2,128)S(1)}, u32[]{:S(2)}, u32[]{:S(2)}) collective-permute-start(f32[2,128]{1,0:T(2,128)S(1)} %get-tuple-element.32), channel_id=1, source_target_pairs={{0,64},{64,0},{128,192},{192,128},{256,320},{320,256},{384,448},{4... | collective-permute-start | bytes 3080 | tf_op jit(solution)/shard_map/ppermute | solution.py:209
  78.4 1.1 collective-permute-done.4
  79.5 12.7 %all-to-all-done.3.parts_ref = bf16[8,96,256]{2,1,0:T(8,128)(2,1)S(1)} async-done(((bf16[8,96,256]{2,1,0:T(8,128)(2,1)}), bf16[8,96,256]{2,1,0:T(8,128)(2,1)S(1)}, u32[]{:S(2)}, u32[]{:S(2)}) %all-to-all-start.3) | async-done | bytes 393248 | tf_op jit(solution)/shard_map/all_to_all | solution.py:54
  92.2 0.8 shard_map.82
  93.0 5.3 %all-to-all-start.4 = ((bf16[8,96,256]{2,1,0:T(8,128)(2,1)}), bf16[8,96,256]{2,1,0:T(8,128)(2,1)S(1)}, u32[]{:S(2)}, u32[]{:S(2)}) async-start(bf16[8,96,256]{2,1,0:T(8,128)(2,1)} %shard_map.82), calls=%async_computation.4 | async-start | bytes 786432 | tf_op jit(solution)/shard_map/all_to_all | solution.py:54
  98.3 2.7 %collective-permute-start.5 = (f32[2,128]{1,0:T(2,128)S(1)}, f32[2,128]{1,0:T(2,128)S(1)}, u32[]{:S(2)}, u32[]{:S(2)}) collective-permute-start(f32[2,128]{1,0:T(2,128)S(1)} %add.20), channel_id=1, source_target_pairs={{0,128},{64,192},{128,0},{192,64},{256,384},{320,448},{384,256},{4... | collective-permute-start | bytes 3080 | tf_op jit(solution)/shard_map/ppermute | solution.py:209
  101.0 2.8 %collective-permute-done.5 = f32[2,128]{1,0:T(2,128)S(1)} collective-permute-done((f32[2,128]{1,0:T(2,128)S(1)}, f32[2,128]{1,0:T(2,128)S(1)}, u32[]{:S(2)}, u32[]{:S(2)}) %collective-permute-start.5) | collective-permute-done | bytes 1056 | tf_op jit(solution)/shard_map/ppermute | solution.py:209
  103.8 0.3 all-to-all-done.4.grads_ref
  104.1 4.4 %collective-permute-start.6 = (f32[2,128]{1,0:T(2,128)S(1)}, f32[2,128]{1,0:T(2,128)S(1)}, u32[]{:S(2)}, u32[]{:S(2)}) collective-permute-start(f32[2,128]{1,0:T(2,128)S(1)} %add.21), channel_id=1, source_target_pairs={{0,256},{64,320},{128,384},{192,448},{256,0},{320,64},{384,128},{4... | collective-permute-start | bytes 3080 | tf_op jit(solution)/shard_map/ppermute | solution.py:209
  108.5 2.2 %shard_map.83 = bf16[1,3,256,256]{3,2,1,0:T(8,128)(2,1)} custom-call(bf16[8,96,256]{2,1,0:T(8,128)(2,1)S(1)} %all-to-all-done.4.grads_ref, bf16[1,3,256,256]{3,2,1,0:T(8,128)(2,1)S(1)} %get-tuple-element.30.w1_ref.w_ref), custom_call_target="tpu_custom_call" | custom-call | flops 600000000 | bytes 1179648 | tf_op jit(solution)/shard_map/pallas_call | solution.py:64
  110.7 0.0 collective-permute-done.6
  110.7 0.8 shard_map.84
  (4 shorter events, 0.0 us)
Async XLA Ops:
  3.1 9.4 %copy-start.3 = (bf16[2,128,256]{2,1,0:T(8,128)(2,1)S(1)}, bf16[2,128,256]{2,1,0:T(8,128)(2,1)}, u32[]{:S(2)}) copy-start(bf16[2,128,256]{2,1,0:T(8,128)(2,1)} %get-tuple-element.22) | copy-start | bytes 393220
  3.1 16.2 %all-to-all-start = ((bf16[8,96,256]{2,1,0:T(8,128)(2,1)}), bf16[8,96,256]{2,1,0:T(8,128)(2,1)S(1)}, u32[]{:S(2)}, u32[]{:S(2)}) async-start(bf16[8,96,256]{2,1,0:T(8,128)(2,1)} %get-tuple-element.21), calls=%async_computation | async-start | bytes 786432 | tf_op jit(solution)/shard_map/all_to_all | solution.py:54
  12.5 6.8 %collective-permute-start = (bf16[2,128,256]{2,1,0:T(8,128)(2,1)S(1)}, bf16[2,128,256]{2,1,0:T(8,128)(2,1)S(1)}, u32[]{:S(2)}, u32[]{:S(2)}) collective-permute-start(bf16[2,128,256]{2,1,0:T(8,128)(2,1)S(1)} %copy-done.3), channel_id=1, source_target_pairs={{0,2},{1,3},{2,0},{3,1},{4,6},{5,7},{6,4},{7,5},{8,10},{9,11},{10,... | collective-permute-start | bytes 393224 | tf_op jit(solution)/shard_map/ppermute | solution.py:45
  20.1 30.5 %all-to-all-start.1 = ((bf16[8,96,256]{2,1,0:T(8,128)(2,1)}), bf16[8,96,256]{2,1,0:T(8,128)(2,1)S(1)}, u32[]{:S(2)}, u32[]{:S(2)}) async-start(bf16[8,96,256]{2,1,0:T(8,128)(2,1)} %shard_map.78), calls=%async_computation.1 | async-start | bytes 786432 | tf_op jit(solution)/shard_map/all_to_all | solution.py:54
  33.3 10.0 %collective-permute-start.1 = (bf16[2,2,128,256]{3,2,1,0:T(8,128)(2,1)S(1)}, bf16[2,2,128,256]{3,2,1,0:T(8,128)(2,1)S(1)}, u32[]{:S(2)}, u32[]{:S(2)}) collective-permute-start(bf16[2,2,128,256]{3,2,1,0:T(8,128)(2,1)S(1)} %pad_maximum_fusion.refs_0_), channel_id=1, source_target_pairs={{0,32},{1,33},{2,34},{3,35},{4,36},{5,37},{6,38},{7,39},{8,40},{9,... | collective-permute-start | bytes 786440 | tf_op jit(solution)/shard_map/ppermute | solution.py:50
  51.4 15.9 %copy-start = (bf16[1,3,256,256]{3,2,1,0:T(8,128)(2,1)S(1)}, bf16[1,3,256,256]{3,2,1,0:T(8,128)(2,1)}, u32[]{:S(2)}) copy-start(bf16[1,3,256,256]{3,2,1,0:T(8,128)(2,1)} %w0_ref.1) | copy-start | bytes 1179652
  51.4 15.9 %all-to-all-start.2 = ((bf16[8,96,256]{2,1,0:T(8,128)(2,1)}), bf16[8,96,256]{2,1,0:T(8,128)(2,1)S(1)}, u32[]{:S(2)}, u32[]{:S(2)}) async-start(bf16[8,96,256]{2,1,0:T(8,128)(2,1)} %shard_map.79), calls=%async_computation.2 | async-start | bytes 786432 | tf_op jit(solution)/shard_map/all_to_all | solution.py:54
  56.3 9.9 %collective-permute-start.3 = (bf16[2,2,128,256]{3,2,1,0:T(8,128)(2,1)S(1)}, bf16[2,2,128,256]{3,2,1,0:T(8,128)(2,1)S(1)}, u32[]{:S(2)}, u32[]{:S(2)}) collective-permute-start(bf16[2,2,128,256]{3,2,1,0:T(8,128)(2,1)S(1)} %pad_maximum_fusion.refs_0_), channel_id=1, source_target_pairs={{0,48},{1,49},{2,50},{3,51},{4,52},{5,53},{6,54},{7,55},{8,56},{9,... | collective-permute-start | bytes 786440 | tf_op jit(solution)/shard_map/ppermute | solution.py:50
  59.0 8.3 %collective-permute-start.2 = (bf16[2,2,128,256]{3,2,1,0:T(8,128)(2,1)S(1)}, bf16[2,2,128,256]{3,2,1,0:T(8,128)(2,1)S(1)}, u32[]{:S(2)}, u32[]{:S(2)}) collective-permute-start(bf16[2,2,128,256]{3,2,1,0:T(8,128)(2,1)S(1)} %pad_maximum_fusion.refs_0_), channel_id=1, source_target_pairs={{0,16},{1,17},{2,18},{3,19},{4,20},{5,21},{6,22},{7,23},{8,24},{9,... | collective-permute-start | bytes 786440 | tf_op jit(solution)/shard_map/ppermute | solution.py:50
  70.4 4.8 %copy-start.1 = (bf16[2,128,256]{2,1,0:T(8,128)(2,1)S(1)}, bf16[2,128,256]{2,1,0:T(8,128)(2,1)}, u32[]{:S(2)}) copy-start(bf16[2,128,256]{2,1,0:T(8,128)(2,1)} %q_ref.1) | copy-start | bytes 393220
  70.4 21.8 %all-to-all-start.3 = ((bf16[8,96,256]{2,1,0:T(8,128)(2,1)}), bf16[8,96,256]{2,1,0:T(8,128)(2,1)S(1)}, u32[]{:S(2)}, u32[]{:S(2)}) async-start(bf16[8,96,256]{2,1,0:T(8,128)(2,1)} %get-tuple-element.29), calls=%async_computation.3 | async-start | bytes 786432 | tf_op jit(solution)/shard_map/all_to_all | solution.py:54
  75.2 0.7 copy-start.2
  76.5 3.0 %collective-permute-start.4 = (f32[2,128]{1,0:T(2,128)S(1)}, f32[2,128]{1,0:T(2,128)S(1)}, u32[]{:S(2)}, u32[]{:S(2)}) collective-permute-start(f32[2,128]{1,0:T(2,128)S(1)} %get-tuple-element.32), channel_id=1, source_target_pairs={{0,64},{64,0},{128,192},{192,128},{256,320},{320,256},{384,448},{4... | collective-permute-start | bytes 3080 | tf_op jit(solution)/shard_map/ppermute | solution.py:209
  93.0 11.0 %all-to-all-start.4 = ((bf16[8,96,256]{2,1,0:T(8,128)(2,1)}), bf16[8,96,256]{2,1,0:T(8,128)(2,1)S(1)}, u32[]{:S(2)}, u32[]{:S(2)}) async-start(bf16[8,96,256]{2,1,0:T(8,128)(2,1)} %shard_map.82), calls=%async_computation.4 | async-start | bytes 786432 | tf_op jit(solution)/shard_map/all_to_all | solution.py:54
  98.3 5.5 %collective-permute-start.5 = (f32[2,128]{1,0:T(2,128)S(1)}, f32[2,128]{1,0:T(2,128)S(1)}, u32[]{:S(2)}, u32[]{:S(2)}) collective-permute-start(f32[2,128]{1,0:T(2,128)S(1)} %add.20), channel_id=1, source_target_pairs={{0,128},{64,192},{128,0},{192,64},{256,384},{320,448},{384,256},{4... | collective-permute-start | bytes 3080 | tf_op jit(solution)/shard_map/ppermute | solution.py:209
  104.1 6.6 %collective-permute-start.6 = (f32[2,128]{1,0:T(2,128)S(1)}, f32[2,128]{1,0:T(2,128)S(1)}, u32[]{:S(2)}, u32[]{:S(2)}) collective-permute-start(f32[2,128]{1,0:T(2,128)S(1)} %add.21), channel_id=1, source_target_pairs={{0,256},{64,320},{128,384},{192,448},{256,0},{320,64},{384,128},{4... | collective-permute-start | bytes 3080 | tf_op jit(solution)/shard_map/ppermute | solution.py:209

commit v7 on v5

--- a/solution.py
+++ b/solution.py
@@ -222,6 +222,9 @@
         first_kernel, (pieces, shaped((2, 128, DH))), keys, values, rates, fast_init, flops=10**8,
         scratch=[*own, pltpu.SemaphoreType.DMA((4,))], space=pl.ANY, limit=58,
     )
+    token = lax.axis_index("tokens")
+    place = (token // 16 * 2 + token // 2 % 2).reshape(1)
+    grads, place = together(grads, place)
     parts, beside = together(exchange(grads, NEAR), from_beside(ahead))
     shares = call(share_kernel, pieces, parts)
     shares, pair = together(shares, jnp.stack([ahead, beside]))
@@ -229,8 +232,6 @@
         exchange(shares, FAR), *(from_along(pair, steps) for steps in (1, 3, 2))
     )
     whole = exchange(call(share_kernel, pieces, parts), NEAR)
-    token = lax.axis_index("tokens")
-    place = (token // 16 * 2 + token // 2 % 2).reshape(1)
     fresh, shares = call(
         middle_kernel, (weights, pieces), whole, fast_init, place, pair, *others, flops=9 * 10**8,
         scratch=[pltpu.VMEM((DH, DH), BF16)] * 2,
@@ -240,12 +241,12 @@
         (shaped((2, 128, DH), F32), shaped((2, 128), F32)),
         queries, fast_init, fresh, out_gain.reshape(1, DH), flops=10**8,
     )
-    for bit in (1, 2, 4):
-        squares = add_partner(squares, bit)
+    squares = add_partner(add_partner(squares, 1), 2)
     parts, y, squares = together(exchange(shares, FAR), y, squares)
     whole = exchange(call(share_kernel, pieces, parts), NEAR)
+    final = call(last_kernel, weights, whole, fresh, flops=6 * 10**8)
+    squares = add_partner(squares, 4)
     mixed = call(finish_kernel, shaped((2, 128, DH)), y, squares)
-    final = call(last_kernel, weights, whole, fresh, flops=6 * 10**8)
     return mixed, final
 
 

time: 110 us -> 106 us (0.964)
  the two profiles are of different devices: /device:TPU:16 before, /device:TPU:6 now
where the time goes in v7:
time: 106 us
  starting transfers between devices  61.5 us (58%)
  waiting for transfers between devices  21.3 us (20%)
  Pallas kernels  10.7 us (10%)
  blocking collectives  10.5 us (10%)
    all_to_all x4, starting transfers between devices, exchange(): lax.all_to_all(array, 'tokens', 0, 0, axis_index_groups=groups, tiled=True)  38.2 us
    pallas_call x8, Pallas kernels, call(): pl.pallas_call(body, out_shape=out_shape, in_specs=[pl.BlockSpec(memory_s...  10.7 us
    all_to_all x1, blocking collectives, exchange(): lax.all_to_all(array, 'tokens', 0, 0, axis_index_groups=groups, tiled=True)  10.5 us
    ppermute x3, starting transfers between devices, from_along(): return lax.ppermute(array, 'tokens', pairs)  10.4 us
    ppermute x3, starting transfers between devices, add_partner(): return squares + lax.ppermute(squares, 'heads', pairs)  9.52 us
    all_to_all x4, waiting for transfers between devices, exchange(): lax.all_to_all(array, 'tokens', 0, 0, axis_index_groups=groups, tiled=True)  7.41 us
    ppermute x3, waiting for transfers between devices, add_partner(): return squares + lax.ppermute(squares, 'heads', pairs)  5.29 us
    ppermute x3, waiting for transfers between devices, from_along(): return lax.ppermute(array, 'tokens', pairs)  5.15 us
  transfers between devices with their start and end apart: 11, of which 8 were waited for; matrix products, arithmetic and copies ran while one was open for 0% of the time, Pallas kernels for 1%

profile of v7, /device:TPU:6, one launch (start us, length us, event | category | flops | bytes accessed | tf_op | source)
XLA Modules:
  0.0 105.6 jit_solution(8430072467709022311)
XLA Ops:
  0.7 2.4 %shard_map.77 = (bf16[8,96,256]{2,1,0:T(8,128)(2,1)}, bf16[2,128,256]{2,1,0:T(8,128)(2,1)}) custom-call(bf16[2,128,256]{2,1,0:T(8,128)(2,1)} %k_hbm.1, bf16[2,128,256]{2,1,0:T(8,128)(2,1)} %v_hbm.1, f32[2,1,128]{2,1,0:T(1,128)} %r_hbm.1, bf16[1,3,256,256]{3,2,1,0:T(8,128)(2,1)} %w0_ref.1), custom_call_target="tpu_custom_call" | custom-call | flops 100000000 | bytes 1180672 | tf_op jit(solution)/shard_map/pallas_call | solution.py:64
  3.1 0.0 copy-start.3
  3.1 9.4 %all-to-all-start = ((bf16[8,96,256]{2,1,0:T(8,128)(2,1)}), bf16[8,96,256]{2,1,0:T(8,128)(2,1)S(1)}, u32[]{:S(2)}, u32[]{:S(2)}) async-start(bf16[8,96,256]{2,1,0:T(8,128)(2,1)} %get-tuple-element.22), calls=%async_computation | async-start | bytes 786432 | tf_op jit(solution)/shard_map/all_to_all | solution.py:54
  12.5 0.0 copy-done.3
  12.5 3.4 %collective-permute-start = (bf16[2,128,256]{2,1,0:T(8,128)(2,1)S(1)}, bf16[2,128,256]{2,1,0:T(8,128)(2,1)S(1)}, u32[]{:S(2)}, u32[]{:S(2)}) collective-permute-start(bf16[2,128,256]{2,1,0:T(8,128)(2,1)S(1)} %copy-done.3), channel_id=1, source_target_pairs={{0,2},{1,3},{2,0},{3,1},{4,6},{5,7},{6,4},{7,5},{8,10},{9,11},{10,... | collective-permute-start | bytes 393224 | tf_op jit(solution)/shard_map/ppermute | solution.py:45
  15.9 3.5 %collective-permute-done = bf16[2,128,256]{2,1,0:T(8,128)(2,1)S(1)} collective-permute-done((bf16[2,128,256]{2,1,0:T(8,128)(2,1)S(1)}, bf16[2,128,256]{2,1,0:T(8,128)(2,1)S(1)}, u32[]{:S(2)}, u32[]{:S(2)}) %collective-permute-start) | collective-permute-done | bytes 131104 | tf_op jit(solution)/shard_map/ppermute | solution.py:45
  19.3 0.0 all-to-all-done.parts_ref
  19.3 0.8 shard_map.78
  20.2 13.2 %all-to-all-start.1 = ((bf16[8,96,256]{2,1,0:T(8,128)(2,1)}), bf16[8,96,256]{2,1,0:T(8,128)(2,1)S(1)}, u32[]{:S(2)}, u32[]{:S(2)}) async-start(bf16[8,96,256]{2,1,0:T(8,128)(2,1)} %shard_map.78), calls=%async_computation.1 | async-start | bytes 786432 | tf_op jit(solution)/shard_map/all_to_all | solution.py:54
  33.4 3.4 %collective-permute-start.3 = (bf16[2,2,128,256]{3,2,1,0:T(8,128)(2,1)S(1)}, bf16[2,2,128,256]{3,2,1,0:T(8,128)(2,1)S(1)}, u32[]{:S(2)}, u32[]{:S(2)}) collective-permute-start(bf16[2,2,128,256]{3,2,1,0:T(8,128)(2,1)S(1)} %pad_maximum_fusion.refs_0_), channel_id=1, source_target_pairs={{0,32},{1,33},{2,34},{3,35},{4,36},{5,37},{6,38},{7,39},{8,40},{9,... | collective-permute-start | bytes 786440 | tf_op jit(solution)/shard_map/ppermute | solution.py:50
  36.7 2.6 %collective-permute-start.2 = (bf16[2,2,128,256]{3,2,1,0:T(8,128)(2,1)S(1)}, bf16[2,2,128,256]{3,2,1,0:T(8,128)(2,1)S(1)}, u32[]{:S(2)}, u32[]{:S(2)}) collective-permute-start(bf16[2,2,128,256]{3,2,1,0:T(8,128)(2,1)S(1)} %pad_maximum_fusion.refs_0_), channel_id=1, source_target_pairs={{0,48},{1,49},{2,50},{3,51},{4,52},{5,53},{6,54},{7,55},{8,56},{9,... | collective-permute-start | bytes 786440 | tf_op jit(solution)/shard_map/ppermute | solution.py:50
  39.3 4.5 %collective-permute-start.1 = (bf16[2,2,128,256]{3,2,1,0:T(8,128)(2,1)S(1)}, bf16[2,2,128,256]{3,2,1,0:T(8,128)(2,1)S(1)}, u32[]{:S(2)}, u32[]{:S(2)}) collective-permute-start(bf16[2,2,128,256]{3,2,1,0:T(8,128)(2,1)S(1)} %pad_maximum_fusion.refs_0_), channel_id=1, source_target_pairs={{0,16},{1,17},{2,18},{3,19},{4,20},{5,21},{6,22},{7,23},{8,24},{9,... | collective-permute-start | bytes 786440 | tf_op jit(solution)/shard_map/ppermute | solution.py:50
  43.8 2.1 %collective-permute-done.3.refs_3_ = bf16[2,2,128,256]{3,2,1,0:T(8,128)(2,1)S(1)} collective-permute-done((bf16[2,2,128,256]{3,2,1,0:T(8,128)(2,1)S(1)}, bf16[2,2,128,256]{3,2,1,0:T(8,128)(2,1)S(1)}, u32[]{:S(2)}, u32[]{:S(2)}) %collective-permute-start.3) | collective-permute-done | bytes 262176 | tf_op jit(solution)/shard_map/ppermute | solution.py:50
  45.9 3.1 %collective-permute-done.2.refs_2_ = bf16[2,2,128,256]{3,2,1,0:T(8,128)(2,1)S(1)} collective-permute-done((bf16[2,2,128,256]{3,2,1,0:T(8,128)(2,1)S(1)}, bf16[2,2,128,256]{3,2,1,0:T(8,128)(2,1)S(1)}, u32[]{:S(2)}, u32[]{:S(2)}) %collective-permute-start.2) | collective-permute-done | bytes 262176 | tf_op jit(solution)/shard_map/ppermute | solution.py:50
  48.9 0.0 collective-permute-done.1.refs_1_
  48.9 1.7 %all-to-all-done.1.parts_ref = bf16[8,96,256]{2,1,0:T(8,128)(2,1)S(1)} async-done(((bf16[8,96,256]{2,1,0:T(8,128)(2,1)}), bf16[8,96,256]{2,1,0:T(8,128)(2,1)S(1)}, u32[]{:S(2)}, u32[]{:S(2)}) %all-to-all-start.1) | async-done | bytes 393248 | tf_op jit(solution)/shard_map/all_to_all | solution.py:54
  50.7 0.1 shard_map.79
  50.7 0.0 copy-start
  50.7 10.5 %all_to_all.25.grads_ref = bf16[8,96,256]{2,1,0:T(8,128)(2,1)S(1)} all-to-all(bf16[8,96,256]{2,1,0:T(8,128)(2,1)S(1)} %shard_map.79), channel_id=1, replica_groups={{0,2,16,18,32,34,48,50},{1,3,17,19,33,35,49,51},{4,6,20,22,36,38,52,54}..., dimensions={0} | all-to-all | bytes 786432 | tf_op jit(solution)/shard_map/all_to_all | solution.py:54
  61.3 0.0 copy-done
  61.3 3.1 %shard_map.80 = (bf16[1,3,256,256]{3,2,1,0:T(8,128)(2,1)S(1)}, bf16[8,96,256]{2,1,0:T(8,128)(2,1)}) custom-call(bf16[8,96,256]{2,1,0:T(8,128)(2,1)S(1)} %all_to_all.25.grads_ref, bf16[1,3,256,256]{3,2,1,0:T(8,128)(2,1)S(1)} %copy-done, s32[1]{0:T(128)} %bitcast.place_ref, bf16[2,2,128,256]{3,2,1,0:T(8,128)(2,1)S(1)} %pad_maximum_fusion.refs_0_, ...), custom_call_target="tpu_custom_call" | custom-call | flops 900000000 | bytes 2621444 | tf_op jit(solution)/shard_map/pallas_call | solution.py:64
  64.4 0.0 copy-start.1
  64.4 10.7 %all-to-all-start.3 = ((bf16[8,96,256]{2,1,0:T(8,128)(2,1)}), bf16[8,96,256]{2,1,0:T(8,128)(2,1)S(1)}, u32[]{:S(2)}, u32[]{:S(2)}) async-start(bf16[8,96,256]{2,1,0:T(8,128)(2,1)} %get-tuple-element.33), calls=%async_computation.3 | async-start | bytes 786432 | tf_op jit(solution)/shard_map/all_to_all | solution.py:54
  75.1 0.0 copy-start.2
  75.1 0.0 copy-done.1
  75.1 0.7 copy-done.2
  75.7 0.6 shard_map.81
  76.3 1.9 %collective-permute-start.4 = (f32[2,128]{1,0:T(2,128)S(1)}, f32[2,128]{1,0:T(2,128)S(1)}, u32[]{:S(2)}, u32[]{:S(2)}) collective-permute-start(f32[2,128]{1,0:T(2,128)S(1)} %get-tuple-element.36), channel_id=1, source_target_pairs={{0,64},{64,0},{128,192},{192,128},{256,320},{320,256},{384,448},{4... | collective-permute-start | bytes 3080 | tf_op jit(solution)/shard_map/ppermute | solution.py:209
  78.3 1.1 %collective-permute-done.4 = f32[2,128]{1,0:T(2,128)S(1)} collective-permute-done((f32[2,128]{1,0:T(2,128)S(1)}, f32[2,128]{1,0:T(2,128)S(1)}, u32[]{:S(2)}, u32[]{:S(2)}) %collective-permute-start.4) | collective-permute-done | bytes 1056 | tf_op jit(solution)/shard_map/ppermute | solution.py:209
  79.4 3.4 %collective-permute-start.5 = (f32[2,128]{1,0:T(2,128)S(1)}, f32[2,128]{1,0:T(2,128)S(1)}, u32[]{:S(2)}, u32[]{:S(2)}) collective-permute-start(f32[2,128]{1,0:T(2,128)S(1)} %add.20), channel_id=1, source_target_pairs={{0,128},{64,192},{128,0},{192,64},{256,384},{320,448},{384,256},{4... | collective-permute-start | bytes 3080 | tf_op jit(solution)/shard_map/ppermute | solution.py:209
  82.7 2.1 %collective-permute-done.5 = f32[2,128]{1,0:T(2,128)S(1)} collective-permute-done((f32[2,128]{1,0:T(2,128)S(1)}, f32[2,128]{1,0:T(2,128)S(1)}, u32[]{:S(2)}, u32[]{:S(2)}) %collective-permute-start.5) | collective-permute-done | bytes 1056 | tf_op jit(solution)/shard_map/ppermute | solution.py:209
  84.8 5.7 %all-to-all-done.3.parts_ref = bf16[8,96,256]{2,1,0:T(8,128)(2,1)S(1)} async-done(((bf16[8,96,256]{2,1,0:T(8,128)(2,1)}), bf16[8,96,256]{2,1,0:T(8,128)(2,1)S(1)}, u32[]{:S(2)}, u32[]{:S(2)}) %all-to-all-start.3) | async-done | bytes 393248 | tf_op jit(solution)/shard_map/all_to_all | solution.py:54
  90.5 0.8 shard_map.83
  91.3 4.9 %all-to-all-start.4 = ((bf16[8,96,256]{2,1,0:T(8,128)(2,1)}), bf16[8,96,256]{2,1,0:T(8,128)(2,1)S(1)}, u32[]{:S(2)}, u32[]{:S(2)}) async-start(bf16[8,96,256]{2,1,0:T(8,128)(2,1)} %shard_map.83), calls=%async_computation.4 | async-start | bytes 786432 | tf_op jit(solution)/shard_map/all_to_all | solution.py:54
  96.2 4.2 %collective-permute-start.6 = (f32[2,128]{1,0:T(2,128)S(1)}, f32[2,128]{1,0:T(2,128)S(1)}, u32[]{:S(2)}, u32[]{:S(2)}) collective-permute-start(f32[2,128]{1,0:T(2,128)S(1)} %add.21), channel_id=1, source_target_pairs={{0,256},{64,320},{128,384},{192,448},{256,0},{320,64},{384,128},{4... | collective-permute-start | bytes 3080 | tf_op jit(solution)/shard_map/ppermute | solution.py:209
  100.5 2.1 %collective-permute-done.6 = f32[2,128]{1,0:T(2,128)S(1)} collective-permute-done((f32[2,128]{1,0:T(2,128)S(1)}, f32[2,128]{1,0:T(2,128)S(1)}, u32[]{:S(2)}, u32[]{:S(2)}) %collective-permute-start.6) | collective-permute-done | bytes 1056 | tf_op jit(solution)/shard_map/ppermute | solution.py:209
  102.6 0.8 shard_map.82
  103.4 0.0 all-to-all-done.4.grads_ref
  103.4 2.2 %shard_map.84 = bf16[1,3,256,256]{3,2,1,0:T(8,128)(2,1)} custom-call(bf16[8,96,256]{2,1,0:T(8,128)(2,1)S(1)} %all-to-all-done.4.grads_ref, bf16[1,3,256,256]{3,2,1,0:T(8,128)(2,1)S(1)} %get-tuple-element.34.w1_ref.w_ref), custom_call_target="tpu_custom_call" | custom-call | flops 600000000 | bytes 1179648 | tf_op jit(solution)/shard_map/pallas_call | solution.py:64
  (4 shorter events, 0.0 us)
Async XLA Ops:
  3.1 9.4 %copy-start.3 = (bf16[2,128,256]{2,1,0:T(8,128)(2,1)S(1)}, bf16[2,128,256]{2,1,0:T(8,128)(2,1)}, u32[]{:S(2)}) copy-start(bf16[2,128,256]{2,1,0:T(8,128)(2,1)} %get-tuple-element.23) | copy-start | bytes 393220
  3.1 16.2 %all-to-all-start = ((bf16[8,96,256]{2,1,0:T(8,128)(2,1)}), bf16[8,96,256]{2,1,0:T(8,128)(2,1)S(1)}, u32[]{:S(2)}, u32[]{:S(2)}) async-start(bf16[8,96,256]{2,1,0:T(8,128)(2,1)} %get-tuple-element.22), calls=%async_computation | async-start | bytes 786432 | tf_op jit(solution)/shard_map/all_to_all | solution.py:54
  12.5 6.8 %collective-permute-start = (bf16[2,128,256]{2,1,0:T(8,128)(2,1)S(1)}, bf16[2,128,256]{2,1,0:T(8,128)(2,1)S(1)}, u32[]{:S(2)}, u32[]{:S(2)}) collective-permute-start(bf16[2,128,256]{2,1,0:T(8,128)(2,1)S(1)} %copy-done.3), channel_id=1, source_target_pairs={{0,2},{1,3},{2,0},{3,1},{4,6},{5,7},{6,4},{7,5},{8,10},{9,11},{10,... | collective-permute-start | bytes 393224 | tf_op jit(solution)/shard_map/ppermute | solution.py:45
  20.2 30.5 %all-to-all-start.1 = ((bf16[8,96,256]{2,1,0:T(8,128)(2,1)}), bf16[8,96,256]{2,1,0:T(8,128)(2,1)S(1)}, u32[]{:S(2)}, u32[]{:S(2)}) async-start(bf16[8,96,256]{2,1,0:T(8,128)(2,1)} %shard_map.78), calls=%async_computation.1 | async-start | bytes 786432 | tf_op jit(solution)/shard_map/all_to_all | solution.py:54
  33.4 12.5 %collective-permute-start.3 = (bf16[2,2,128,256]{3,2,1,0:T(8,128)(2,1)S(1)}, bf16[2,2,128,256]{3,2,1,0:T(8,128)(2,1)S(1)}, u32[]{:S(2)}, u32[]{:S(2)}) collective-permute-start(bf16[2,2,128,256]{3,2,1,0:T(8,128)(2,1)S(1)} %pad_maximum_fusion.refs_0_), channel_id=1, source_target_pairs={{0,32},{1,33},{2,34},{3,35},{4,36},{5,37},{6,38},{7,39},{8,40},{9,... | collective-permute-start | bytes 786440 | tf_op jit(solution)/shard_map/ppermute | solution.py:50
  36.7 12.2 %collective-permute-start.2 = (bf16[2,2,128,256]{3,2,1,0:T(8,128)(2,1)S(1)}, bf16[2,2,128,256]{3,2,1,0:T(8,128)(2,1)S(1)}, u32[]{:S(2)}, u32[]{:S(2)}) collective-permute-start(bf16[2,2,128,256]{3,2,1,0:T(8,128)(2,1)S(1)} %pad_maximum_fusion.refs_0_), channel_id=1, source_target_pairs={{0,48},{1,49},{2,50},{3,51},{4,52},{5,53},{6,54},{7,55},{8,56},{9,... | collective-permute-start | bytes 786440 | tf_op jit(solution)/shard_map/ppermute | solution.py:50
  39.3 9.6 %collective-permute-start.1 = (bf16[2,2,128,256]{3,2,1,0:T(8,128)(2,1)S(1)}, bf16[2,2,128,256]{3,2,1,0:T(8,128)(2,1)S(1)}, u32[]{:S(2)}, u32[]{:S(2)}) collective-permute-start(bf16[2,2,128,256]{3,2,1,0:T(8,128)(2,1)S(1)} %pad_maximum_fusion.refs_0_), channel_id=1, source_target_pairs={{0,16},{1,17},{2,18},{3,19},{4,20},{5,21},{6,22},{7,23},{8,24},{9,... | collective-permute-start | bytes 786440 | tf_op jit(solution)/shard_map/ppermute | solution.py:50
  50.7 10.5 %copy-start = (bf16[1,3,256,256]{3,2,1,0:T(8,128)(2,1)S(1)}, bf16[1,3,256,256]{3,2,1,0:T(8,128)(2,1)}, u32[]{:S(2)}) copy-start(bf16[1,3,256,256]{3,2,1,0:T(8,128)(2,1)} %w0_ref.1) | copy-start | bytes 1179652
  64.4 10.7 %copy-start.1 = (bf16[2,128,256]{2,1,0:T(8,128)(2,1)S(1)}, bf16[2,128,256]{2,1,0:T(8,128)(2,1)}, u32[]{:S(2)}) copy-start(bf16[2,128,256]{2,1,0:T(8,128)(2,1)} %q_ref.1) | copy-start | bytes 393220
  64.4 26.1 %all-to-all-start.3 = ((bf16[8,96,256]{2,1,0:T(8,128)(2,1)}), bf16[8,96,256]{2,1,0:T(8,128)(2,1)S(1)}, u32[]{:S(2)}, u32[]{:S(2)}) async-start(bf16[8,96,256]{2,1,0:T(8,128)(2,1)} %get-tuple-element.33), calls=%async_computation.3 | async-start | bytes 786432 | tf_op jit(solution)/shard_map/all_to_all | solution.py:54
  75.1 0.7 copy-start.2
  76.3 3.0 %collective-permute-start.4 = (f32[2,128]{1,0:T(2,128)S(1)}, f32[2,128]{1,0:T(2,128)S(1)}, u32[]{:S(2)}, u32[]{:S(2)}) collective-permute-start(f32[2,128]{1,0:T(2,128)S(1)} %get-tuple-element.36), channel_id=1, source_target_pairs={{0,64},{64,0},{128,192},{192,128},{256,320},{320,256},{384,448},{4... | collective-permute-start | bytes 3080 | tf_op jit(solution)/shard_map/ppermute | solution.py:209
  79.4 5.5 %collective-permute-start.5 = (f32[2,128]{1,0:T(2,128)S(1)}, f32[2,128]{1,0:T(2,128)S(1)}, u32[]{:S(2)}, u32[]{:S(2)}) collective-permute-start(f32[2,128]{1,0:T(2,128)S(1)} %add.20), channel_id=1, source_target_pairs={{0,128},{64,192},{128,0},{192,64},{256,384},{320,448},{384,256},{4... | collective-permute-start | bytes 3080 | tf_op jit(solution)/shard_map/ppermute | solution.py:209
  91.3 12.1 %all-to-all-start.4 = ((bf16[8,96,256]{2,1,0:T(8,128)(2,1)}), bf16[8,96,256]{2,1,0:T(8,128)(2,1)S(1)}, u32[]{:S(2)}, u32[]{:S(2)}) async-start(bf16[8,96,256]{2,1,0:T(8,128)(2,1)} %shard_map.83), calls=%async_computation.4 | async-start | bytes 786432 | tf_op jit(solution)/shard_map/all_to_all | solution.py:54
  96.2 6.3 %collective-permute-start.6 = (f32[2,128]{1,0:T(2,128)S(1)}, f32[2,128]{1,0:T(2,128)S(1)}, u32[]{:S(2)}, u32[]{:S(2)}) collective-permute-start(f32[2,128]{1,0:T(2,128)S(1)} %add.21), channel_id=1, source_target_pairs={{0,256},{64,320},{128,384},{192,448},{256,0},{320,64},{384,128},{4... | collective-permute-start | bytes 3080 | tf_op jit(solution)/shard_map/ppermute | solution.py:209

commit v8 on v7

--- a/solution.py
+++ b/solution.py
@@ -241,11 +241,11 @@
         (shaped((2, 128, DH), F32), shaped((2, 128), F32)),
         queries, fast_init, fresh, out_gain.reshape(1, DH), flops=10**8,
     )
-    squares = add_partner(add_partner(squares, 1), 2)
+    squares = add_partner(add_partner(squares, 2), 4)
     parts, y, squares = together(exchange(shares, FAR), y, squares)
     whole = exchange(call(share_kernel, pieces, parts), NEAR)
     final = call(last_kernel, weights, whole, fresh, flops=6 * 10**8)
-    squares = add_partner(squares, 4)
+    squares = add_partner(squares, 1)
     mixed = call(finish_kernel, shaped((2, 128, DH)), y, squares)
     return mixed, final
 

time: 106 us -> 106 us (level)
  the two profiles are of different devices: /device:TPU:6 before, /device:TPU:16 now
where the time goes in v8:
time: 106 us
  starting transfers between devices  58.3 us (55%)
  waiting for transfers between devices  23.8 us (22%)
  blocking collectives  11.1 us (10%)
  Pallas kernels  10.7 us (10%)
    all_to_all x4, starting transfers between devices, exchange(): lax.all_to_all(array, 'tokens', 0, 0, axis_index_groups=groups, tiled=True)  35.5 us
    all_to_all x1, blocking collectives, exchange(): lax.all_to_all(array, 'tokens', 0, 0, axis_index_groups=groups, tiled=True)  11.1 us
    pallas_call x8, Pallas kernels, call(): pl.pallas_call(body, out_shape=out_shape, in_specs=[pl.BlockSpec(memory_s...  10.7 us
    ppermute x3, starting transfers between devices, from_along(): return lax.ppermute(array, 'tokens', pairs)  9.99 us
    ppermute x3, starting transfers between devices, add_partner(): return squares + lax.ppermute(squares, 'heads', pairs)  8.93 us
    ppermute x3, waiting for transfers between devices, from_along(): return lax.ppermute(array, 'tokens', pairs)  6.72 us
    ppermute x3, waiting for transfers between devices, add_partner(): return squares + lax.ppermute(squares, 'heads', pairs)  6.65 us
    ppermute x1, waiting for transfers between devices, from_beside(): lax.ppermute(array, 'tokens', token_pairs(lambda x, h, l, z: (x, h, 1 - l...  5.44 us
  transfers between devices with their start and end apart: 11, of which 10 were waited for; matrix products, arithmetic and copies ran while one was open for 0% of the time, Pallas kernels for 1%

profile of v8, /device:TPU:16, one launch (start us, length us, event | category | flops | bytes accessed | tf_op | source)
XLA Modules:
  0.0 105.6 jit_solution(1518930431565812345)
XLA Ops:
  0.7 2.4 %shard_map.77 = (bf16[8,96,256]{2,1,0:T(8,128)(2,1)}, bf16[2,128,256]{2,1,0:T(8,128)(2,1)}) custom-call(bf16[2,128,256]{2,1,0:T(8,128)(2,1)} %k_hbm.1, bf16[2,128,256]{2,1,0:T(8,128)(2,1)} %v_hbm.1, f32[2,1,128]{2,1,0:T(1,128)} %r_hbm.1, bf16[1,3,256,256]{3,2,1,0:T(8,128)(2,1)} %w0_ref.1), custom_call_target="tpu_custom_call" | custom-call | flops 100000000 | bytes 1180672 | tf_op jit(solution)/shard_map/pallas_call | solution.py:64
  3.1 0.0 copy-start.3
  3.1 5.5 %all-to-all-start = ((bf16[8,96,256]{2,1,0:T(8,128)(2,1)}), bf16[8,96,256]{2,1,0:T(8,128)(2,1)S(1)}, u32[]{:S(2)}, u32[]{:S(2)}) async-start(bf16[8,96,256]{2,1,0:T(8,128)(2,1)} %get-tuple-element.22), calls=%async_computation | async-start | bytes 786432 | tf_op jit(solution)/shard_map/all_to_all | solution.py:54
  8.6 0.0 copy-done.3
  8.6 3.9 %collective-permute-start = (bf16[2,128,256]{2,1,0:T(8,128)(2,1)S(1)}, bf16[2,128,256]{2,1,0:T(8,128)(2,1)S(1)}, u32[]{:S(2)}, u32[]{:S(2)}) collective-permute-start(bf16[2,128,256]{2,1,0:T(8,128)(2,1)S(1)} %copy-done.3), channel_id=1, source_target_pairs={{0,2},{1,3},{2,0},{3,1},{4,6},{5,7},{6,4},{7,5},{8,10},{9,11},{10,... | collective-permute-start | bytes 393224 | tf_op jit(solution)/shard_map/ppermute | solution.py:45
  12.5 5.4 %collective-permute-done = bf16[2,128,256]{2,1,0:T(8,128)(2,1)S(1)} collective-permute-done((bf16[2,128,256]{2,1,0:T(8,128)(2,1)S(1)}, bf16[2,128,256]{2,1,0:T(8,128)(2,1)S(1)}, u32[]{:S(2)}, u32[]{:S(2)}) %collective-permute-start) | collective-permute-done | bytes 131104 | tf_op jit(solution)/shard_map/ppermute | solution.py:45
  17.9 0.7 all-to-all-done.parts_ref
  18.7 0.8 shard_map.78
  19.5 15.0 %all-to-all-start.1 = ((bf16[8,96,256]{2,1,0:T(8,128)(2,1)}), bf16[8,96,256]{2,1,0:T(8,128)(2,1)S(1)}, u32[]{:S(2)}, u32[]{:S(2)}) async-start(bf16[8,96,256]{2,1,0:T(8,128)(2,1)} %shard_map.78), calls=%async_computation.1 | async-start | bytes 786432 | tf_op jit(solution)/shard_map/all_to_all | solution.py:54
  34.5 4.1 %collective-permute-start.3 = (bf16[2,2,128,256]{3,2,1,0:T(8,128)(2,1)S(1)}, bf16[2,2,128,256]{3,2,1,0:T(8,128)(2,1)S(1)}, u32[]{:S(2)}, u32[]{:S(2)}) collective-permute-start(bf16[2,2,128,256]{3,2,1,0:T(8,128)(2,1)S(1)} %pad_maximum_fusion.refs_0_), channel_id=1, source_target_pairs={{0,32},{1,33},{2,34},{3,35},{4,36},{5,37},{6,38},{7,39},{8,40},{9,... | collective-permute-start | bytes 786440 | tf_op jit(solution)/shard_map/ppermute | solution.py:50
  38.6 3.1 %collective-permute-start.2 = (bf16[2,2,128,256]{3,2,1,0:T(8,128)(2,1)S(1)}, bf16[2,2,128,256]{3,2,1,0:T(8,128)(2,1)S(1)}, u32[]{:S(2)}, u32[]{:S(2)}) collective-permute-start(bf16[2,2,128,256]{3,2,1,0:T(8,128)(2,1)S(1)} %pad_maximum_fusion.refs_0_), channel_id=1, source_target_pairs={{0,48},{1,49},{2,50},{3,51},{4,52},{5,53},{6,54},{7,55},{8,56},{9,... | collective-permute-start | bytes 786440 | tf_op jit(solution)/shard_map/ppermute | solution.py:50
  41.7 2.8 %collective-permute-start.1 = (bf16[2,2,128,256]{3,2,1,0:T(8,128)(2,1)S(1)}, bf16[2,2,128,256]{3,2,1,0:T(8,128)(2,1)S(1)}, u32[]{:S(2)}, u32[]{:S(2)}) collective-permute-start(bf16[2,2,128,256]{3,2,1,0:T(8,128)(2,1)S(1)} %pad_maximum_fusion.refs_0_), channel_id=1, source_target_pairs={{0,16},{1,17},{2,18},{3,19},{4,20},{5,21},{6,22},{7,23},{8,24},{9,... | collective-permute-start | bytes 786440 | tf_op jit(solution)/shard_map/ppermute | solution.py:50
  44.5 0.4 collective-permute-done.3.refs_3_
  44.9 4.2 %collective-permute-done.2.refs_2_ = bf16[2,2,128,256]{3,2,1,0:T(8,128)(2,1)S(1)} collective-permute-done((bf16[2,2,128,256]{3,2,1,0:T(8,128)(2,1)S(1)}, bf16[2,2,128,256]{3,2,1,0:T(8,128)(2,1)S(1)}, u32[]{:S(2)}, u32[]{:S(2)}) %collective-permute-start.2) | collective-permute-done | bytes 262176 | tf_op jit(solution)/shard_map/ppermute | solution.py:50
  49.2 2.1 %collective-permute-done.1.refs_1_ = bf16[2,2,128,256]{3,2,1,0:T(8,128)(2,1)S(1)} collective-permute-done((bf16[2,2,128,256]{3,2,1,0:T(8,128)(2,1)S(1)}, bf16[2,2,128,256]{3,2,1,0:T(8,128)(2,1)S(1)}, u32[]{:S(2)}, u32[]{:S(2)}) %collective-permute-start.1) | collective-permute-done | bytes 262176 | tf_op jit(solution)/shard_map/ppermute | solution.py:50
  51.2 0.0 all-to-all-done.1.parts_ref
  51.2 0.1 shard_map.79
  51.3 0.0 copy-start
  51.3 11.1 %all_to_all.25.grads_ref = bf16[8,96,256]{2,1,0:T(8,128)(2,1)S(1)} all-to-all(bf16[8,96,256]{2,1,0:T(8,128)(2,1)S(1)} %shard_map.79), channel_id=1, replica_groups={{0,2,16,18,32,34,48,50},{1,3,17,19,33,35,49,51},{4,6,20,22,36,38,52,54}..., dimensions={0} | all-to-all | bytes 786432 | tf_op jit(solution)/shard_map/all_to_all | solution.py:54
  62.4 0.0 copy-done
  62.4 3.1 %shard_map.80 = (bf16[1,3,256,256]{3,2,1,0:T(8,128)(2,1)S(1)}, bf16[8,96,256]{2,1,0:T(8,128)(2,1)}) custom-call(bf16[8,96,256]{2,1,0:T(8,128)(2,1)S(1)} %all_to_all.25.grads_ref, bf16[1,3,256,256]{3,2,1,0:T(8,128)(2,1)S(1)} %copy-done, s32[1]{0:T(128)} %bitcast.place_ref, bf16[2,2,128,256]{3,2,1,0:T(8,128)(2,1)S(1)} %pad_maximum_fusion.refs_0_, ...), custom_call_target="tpu_custom_call" | custom-call | flops 900000000 | bytes 2621444 | tf_op jit(solution)/shard_map/pallas_call | solution.py:64
  65.5 0.0 copy-start.1
  65.5 11.6 %all-to-all-start.3 = ((bf16[8,96,256]{2,1,0:T(8,128)(2,1)}), bf16[8,96,256]{2,1,0:T(8,128)(2,1)S(1)}, u32[]{:S(2)}, u32[]{:S(2)}) async-start(bf16[8,96,256]{2,1,0:T(8,128)(2,1)} %get-tuple-element.33), calls=%async_computation.3 | async-start | bytes 786432 | tf_op jit(solution)/shard_map/all_to_all | solution.py:54
  77.2 0.0 copy-start.2
  77.2 0.0 copy-done.1
  77.2 0.7 copy-done.2
  77.8 0.6 shard_map.81
  78.4 3.4 %collective-permute-start.4 = (f32[2,128]{1,0:T(2,128)S(1)}, f32[2,128]{1,0:T(2,128)S(1)}, u32[]{:S(2)}, u32[]{:S(2)}) collective-permute-start(f32[2,128]{1,0:T(2,128)S(1)} %get-tuple-element.36), channel_id=1, source_target_pairs={{0,128},{64,192},{128,0},{192,64},{256,384},{320,448},{384,256},{4... | collective-permute-start | bytes 3080 | tf_op jit(solution)/shard_map/ppermute | solution.py:209
  81.8 2.8 %collective-permute-done.4 = f32[2,128]{1,0:T(2,128)S(1)} collective-permute-done((f32[2,128]{1,0:T(2,128)S(1)}, f32[2,128]{1,0:T(2,128)S(1)}, u32[]{:S(2)}, u32[]{:S(2)}) %collective-permute-start.4) | collective-permute-done | bytes 1056 | tf_op jit(solution)/shard_map/ppermute | solution.py:209
  84.6 3.6 %collective-permute-start.5 = (f32[2,128]{1,0:T(2,128)S(1)}, f32[2,128]{1,0:T(2,128)S(1)}, u32[]{:S(2)}, u32[]{:S(2)}) collective-permute-start(f32[2,128]{1,0:T(2,128)S(1)} %add.20), channel_id=1, source_target_pairs={{0,256},{64,320},{128,384},{192,448},{256,0},{320,64},{384,128},{4... | collective-permute-start | bytes 3080 | tf_op jit(solution)/shard_map/ppermute | solution.py:209
  88.3 2.7 %collective-permute-done.5 = f32[2,128]{1,0:T(2,128)S(1)} collective-permute-done((f32[2,128]{1,0:T(2,128)S(1)}, f32[2,128]{1,0:T(2,128)S(1)}, u32[]{:S(2)}, u32[]{:S(2)}) %collective-permute-start.5) | collective-permute-done | bytes 1056 | tf_op jit(solution)/shard_map/ppermute | solution.py:209
  91.0 0.2 all-to-all-done.3.parts_ref
  91.2 0.8 shard_map.83
  92.0 3.5 %all-to-all-start.4 = ((bf16[8,96,256]{2,1,0:T(8,128)(2,1)}), bf16[8,96,256]{2,1,0:T(8,128)(2,1)S(1)}, u32[]{:S(2)}, u32[]{:S(2)}) async-start(bf16[8,96,256]{2,1,0:T(8,128)(2,1)} %shard_map.83), calls=%async_computation.4 | async-start | bytes 786432 | tf_op jit(solution)/shard_map/all_to_all | solution.py:54
  95.5 1.9 %collective-permute-start.6 = (f32[2,128]{1,0:T(2,128)S(1)}, f32[2,128]{1,0:T(2,128)S(1)}, u32[]{:S(2)}, u32[]{:S(2)}) collective-permute-start(f32[2,128]{1,0:T(2,128)S(1)} %add.21), channel_id=1, source_target_pairs={{0,64},{64,0},{128,192},{192,128},{256,320},{320,256},{384,448},{4... | collective-permute-start | bytes 3080 | tf_op jit(solution)/shard_map/ppermute | solution.py:209
  97.4 1.1 %collective-permute-done.6 = f32[2,128]{1,0:T(2,128)S(1)} collective-permute-done((f32[2,128]{1,0:T(2,128)S(1)}, f32[2,128]{1,0:T(2,128)S(1)}, u32[]{:S(2)}, u32[]{:S(2)}) %collective-permute-start.6) | collective-permute-done | bytes 1056 | tf_op jit(solution)/shard_map/ppermute | solution.py:209
  98.5 0.8 shard_map.82
  99.3 4.1 %all-to-all-done.4.grads_ref = bf16[8,96,256]{2,1,0:T(8,128)(2,1)S(1)} async-done(((bf16[8,96,256]{2,1,0:T(8,128)(2,1)}), bf16[8,96,256]{2,1,0:T(8,128)(2,1)S(1)}, u32[]{:S(2)}, u32[]{:S(2)}) %all-to-all-start.4) | async-done | bytes 393248 | tf_op jit(solution)/shard_map/all_to_all | solution.py:54
  103.4 2.2 %shard_map.84 = bf16[1,3,256,256]{3,2,1,0:T(8,128)(2,1)} custom-call(bf16[8,96,256]{2,1,0:T(8,128)(2,1)S(1)} %all-to-all-done.4.grads_ref, bf16[1,3,256,256]{3,2,1,0:T(8,128)(2,1)S(1)} %get-tuple-element.34.w1_ref.w_ref), custom_call_target="tpu_custom_call" | custom-call | flops 600000000 | bytes 1179648 | tf_op jit(solution)/shard_map/pallas_call | solution.py:64
  (4 shorter events, 0.0 us)
Async XLA Ops:
  3.1 5.5 %copy-start.3 = (bf16[2,128,256]{2,1,0:T(8,128)(2,1)S(1)}, bf16[2,128,256]{2,1,0:T(8,128)(2,1)}, u32[]{:S(2)}) copy-start(bf16[2,128,256]{2,1,0:T(8,128)(2,1)} %get-tuple-element.23) | copy-start | bytes 393220
  3.1 15.6 %all-to-all-start = ((bf16[8,96,256]{2,1,0:T(8,128)(2,1)}), bf16[8,96,256]{2,1,0:T(8,128)(2,1)S(1)}, u32[]{:S(2)}, u32[]{:S(2)}) async-start(bf16[8,96,256]{2,1,0:T(8,128)(2,1)} %get-tuple-element.22), calls=%async_computation | async-start | bytes 786432 | tf_op jit(solution)/shard_map/all_to_all | solution.py:54
  8.6 9.4 %collective-permute-start = (bf16[2,128,256]{2,1,0:T(8,128)(2,1)S(1)}, bf16[2,128,256]{2,1,0:T(8,128)(2,1)S(1)}, u32[]{:S(2)}, u32[]{:S(2)}) collective-permute-start(bf16[2,128,256]{2,1,0:T(8,128)(2,1)S(1)} %copy-done.3), channel_id=1, source_target_pairs={{0,2},{1,3},{2,0},{3,1},{4,6},{5,7},{6,4},{7,5},{8,10},{9,11},{10,... | collective-permute-start | bytes 393224 | tf_op jit(solution)/shard_map/ppermute | solution.py:45
  19.5 31.7 %all-to-all-start.1 = ((bf16[8,96,256]{2,1,0:T(8,128)(2,1)}), bf16[8,96,256]{2,1,0:T(8,128)(2,1)S(1)}, u32[]{:S(2)}, u32[]{:S(2)}) async-start(bf16[8,96,256]{2,1,0:T(8,128)(2,1)} %shard_map.78), calls=%async_computation.1 | async-start | bytes 786432 | tf_op jit(solution)/shard_map/all_to_all | solution.py:54
  34.5 10.4 %collective-permute-start.3 = (bf16[2,2,128,256]{3,2,1,0:T(8,128)(2,1)S(1)}, bf16[2,2,128,256]{3,2,1,0:T(8,128)(2,1)S(1)}, u32[]{:S(2)}, u32[]{:S(2)}) collective-permute-start(bf16[2,2,128,256]{3,2,1,0:T(8,128)(2,1)S(1)} %pad_maximum_fusion.refs_0_), channel_id=1, source_target_pairs={{0,32},{1,33},{2,34},{3,35},{4,36},{5,37},{6,38},{7,39},{8,40},{9,... | collective-permute-start | bytes 786440 | tf_op jit(solution)/shard_map/ppermute | solution.py:50
  38.6 10.5 %collective-permute-start.2 = (bf16[2,2,128,256]{3,2,1,0:T(8,128)(2,1)S(1)}, bf16[2,2,128,256]{3,2,1,0:T(8,128)(2,1)S(1)}, u32[]{:S(2)}, u32[]{:S(2)}) collective-permute-start(bf16[2,2,128,256]{3,2,1,0:T(8,128)(2,1)S(1)} %pad_maximum_fusion.refs_0_), channel_id=1, source_target_pairs={{0,48},{1,49},{2,50},{3,51},{4,52},{5,53},{6,54},{7,55},{8,56},{9,... | collective-permute-start | bytes 786440 | tf_op jit(solution)/shard_map/ppermute | solution.py:50
  41.7 9.5 %collective-permute-start.1 = (bf16[2,2,128,256]{3,2,1,0:T(8,128)(2,1)S(1)}, bf16[2,2,128,256]{3,2,1,0:T(8,128)(2,1)S(1)}, u32[]{:S(2)}, u32[]{:S(2)}) collective-permute-start(bf16[2,2,128,256]{3,2,1,0:T(8,128)(2,1)S(1)} %pad_maximum_fusion.refs_0_), channel_id=1, source_target_pairs={{0,16},{1,17},{2,18},{3,19},{4,20},{5,21},{6,22},{7,23},{8,24},{9,... | collective-permute-start | bytes 786440 | tf_op jit(solution)/shard_map/ppermute | solution.py:50
  51.3 11.2 %copy-start = (bf16[1,3,256,256]{3,2,1,0:T(8,128)(2,1)S(1)}, bf16[1,3,256,256]{3,2,1,0:T(8,128)(2,1)}, u32[]{:S(2)}) copy-start(bf16[1,3,256,256]{3,2,1,0:T(8,128)(2,1)} %w0_ref.1) | copy-start | bytes 1179652
  65.5 11.6 %copy-start.1 = (bf16[2,128,256]{2,1,0:T(8,128)(2,1)S(1)}, bf16[2,128,256]{2,1,0:T(8,128)(2,1)}, u32[]{:S(2)}) copy-start(bf16[2,128,256]{2,1,0:T(8,128)(2,1)} %q_ref.1) | copy-start | bytes 393220
  65.5 25.7 %all-to-all-start.3 = ((bf16[8,96,256]{2,1,0:T(8,128)(2,1)}), bf16[8,96,256]{2,1,0:T(8,128)(2,1)S(1)}, u32[]{:S(2)}, u32[]{:S(2)}) async-start(bf16[8,96,256]{2,1,0:T(8,128)(2,1)} %get-tuple-element.33), calls=%async_computation.3 | async-start | bytes 786432 | tf_op jit(solution)/shard_map/all_to_all | solution.py:54
  77.2 0.7 copy-start.2
  78.4 6.2 %collective-permute-start.4 = (f32[2,128]{1,0:T(2,128)S(1)}, f32[2,128]{1,0:T(2,128)S(1)}, u32[]{:S(2)}, u32[]{:S(2)}) collective-permute-start(f32[2,128]{1,0:T(2,128)S(1)} %get-tuple-element.36), channel_id=1, source_target_pairs={{0,128},{64,192},{128,0},{192,64},{256,384},{320,448},{384,256},{4... | collective-permute-start | bytes 3080 | tf_op jit(solution)/shard_map/ppermute | solution.py:209
  84.6 6.4 %collective-permute-start.5 = (f32[2,128]{1,0:T(2,128)S(1)}, f32[2,128]{1,0:T(2,128)S(1)}, u32[]{:S(2)}, u32[]{:S(2)}) collective-permute-start(f32[2,128]{1,0:T(2,128)S(1)} %add.20), channel_id=1, source_target_pairs={{0,256},{64,320},{128,384},{192,448},{256,0},{320,64},{384,128},{4... | collective-permute-start | bytes 3080 | tf_op jit(solution)/shard_map/ppermute | solution.py:209
  92.0 11.4 %all-to-all-start.4 = ((bf16[8,96,256]{2,1,0:T(8,128)(2,1)}), bf16[8,96,256]{2,1,0:T(8,128)(2,1)S(1)}, u32[]{:S(2)}, u32[]{:S(2)}) async-start(bf16[8,96,256]{2,1,0:T(8,128)(2,1)} %shard_map.83), calls=%async_computation.4 | async-start | bytes 786432 | tf_op jit(solution)/shard_map/all_to_all | solution.py:54
  95.5 3.0 %collective-permute-start.6 = (f32[2,128]{1,0:T(2,128)S(1)}, f32[2,128]{1,0:T(2,128)S(1)}, u32[]{:S(2)}, u32[]{:S(2)}) collective-permute-start(f32[2,128]{1,0:T(2,128)S(1)} %add.21), channel_id=1, source_target_pairs={{0,64},{64,0},{128,192},{192,128},{256,320},{320,256},{384,448},{4... | collective-permute-start | bytes 3080 | tf_op jit(solution)/shard_map/ppermute | solution.py:209

commit v9 on v8

--- a/solution.py
+++ b/solution.py
@@ -133,7 +133,7 @@
     for m in range(3):
         wide = stacked[m].astype(F32)
         square = jnp.sum(jnp.sum(wide * wide, axis=0, keepdims=True), axis=1, keepdims=True)
-        current.append((wide / (jnp.sqrt(square) + 1e-07)).astype(BF16))
+        current.append((wide * (1.0 / (jnp.sqrt(square) + 1e-07))).astype(BF16))
     for step in range(NS_STEPS):
         grams = [mm(x, x, 1, 1).astype(BF16) for x in current]
         squares = [mm(a, a) for a in grams]
@@ -156,17 +156,18 @@
     gate_ref[...] = jnp.transpose(fresh[0])
     up_ref[...] = jnp.transpose(fresh[1])
     units = pl.ds(pl.multiple_of(place_ref[0] * UNITS, UNITS), UNITS)
-    gate_w, up_w, down_w = gate_ref[units], up_ref[units], fresh_ref[0, 2, units]
-    sums = [jnp.zeros((UNITS, DH), F32)] * 3
+    pair_w = jnp.concatenate([gate_ref[units], up_ref[units]], axis=0)
+    down_w = fresh_ref[0, 2, units]
+    pair_sum, down_sum = jnp.zeros((2 * UNITS, DH), F32), jnp.zeros((UNITS, DH), F32)
     for token_ref in tokens:
         keys = token_ref[:, 0].reshape(256, DH)
         scaled = token_ref[:, 1].reshape(256, DH)
-        gate = mm(gate_w, keys, 1, 1)
-        up = mm(up_w, keys, 1, 1)
+        gate_up = mm(pair_w, keys, 1, 1)
         back = mm(down_w, scaled, 1, 1)
-        hidden, grad_gate, grad_up = elementwise(gate, up, back)
-        terms = mm(grad_gate, keys), mm(grad_up, keys), mm(hidden, scaled)
-        sums = [s + t for s, t in zip(sums, terms)]
+        hidden, grad_gate, grad_up = elementwise(gate_up[:UNITS], gate_up[UNITS:], back)
+        pair_sum = pair_sum + mm(jnp.concatenate([grad_gate, grad_up], axis=0), keys)
+        down_sum = down_sum + mm(hidden, scaled)
+    sums = pair_sum[:UNITS], pair_sum[UNITS:], down_sum
     for m in range(3):
         part = sums[m].astype(BF16)
         for peer in range(PEERS):

time: 106 us -> 106 us (level)
  no operation moved by 1% of the time
where the time goes in v9:
time: 106 us; the launch traced here: 105 us
  starting transfers between devices  58.3 us (55%)
  waiting for transfers between devices  23.9 us (23%)
  blocking collectives  11.1 us (10%)
  Pallas kernels  10.5 us (10%)
    all_to_all x4, starting transfers between devices, exchange(): lax.all_to_all(array, 'tokens', 0, 0, axis_index_groups=groups, tiled=True)  35.5 us
    all_to_all x1, blocking collectives, exchange(): lax.all_to_all(array, 'tokens', 0, 0, axis_index_groups=groups, tiled=True)  11.1 us
    pallas_call x8, Pallas kernels, call(): pl.pallas_call(body, out_shape=out_shape, in_specs=[pl.BlockSpec(memory_s...  10.5 us
    ppermute x3, starting transfers between devices, from_along(): return lax.ppermute(array, 'tokens', pairs)  9.99 us
    ppermute x3, starting transfers between devices, add_partner(): return squares + lax.ppermute(squares, 'heads', pairs)  8.92 us
    ppermute x3, waiting for transfers between devices, from_along(): return lax.ppermute(array, 'tokens', pairs)  6.72 us
    ppermute x3, waiting for transfers between devices, add_partner(): return squares + lax.ppermute(squares, 'heads', pairs)  6.64 us
    ppermute x1, waiting for transfers between devices, from_beside(): lax.ppermute(array, 'tokens', token_pairs(lambda x, h, l, z: (x, h, 1 - l...  5.44 us
  transfers between devices with their start and end apart: 11, of which 10 were waited for; matrix products, arithmetic and copies ran while one was open for 0% of the time, Pallas kernels for 1%

profile of v9, /device:TPU:16, one launch (start us, length us, event | category | flops | bytes accessed | tf_op | source)
XLA Modules:
  0.0 105.4 jit_solution(3841092907879197309)
XLA Ops:
  0.7 2.4 %shard_map.77 = (bf16[8,96,256]{2,1,0:T(8,128)(2,1)}, bf16[2,128,256]{2,1,0:T(8,128)(2,1)}) custom-call(bf16[2,128,256]{2,1,0:T(8,128)(2,1)} %k_hbm.1, bf16[2,128,256]{2,1,0:T(8,128)(2,1)} %v_hbm.1, f32[2,1,128]{2,1,0:T(1,128)} %r_hbm.1, bf16[1,3,256,256]{3,2,1,0:T(8,128)(2,1)} %w0_ref.1), custom_call_target="tpu_custom_call" | custom-call | flops 100000000 | bytes 1180672 | tf_op jit(solution)/shard_map/pallas_call | solution.py:64
  3.1 0.0 copy-start.3
  3.1 5.5 %all-to-all-start = ((bf16[8,96,256]{2,1,0:T(8,128)(2,1)}), bf16[8,96,256]{2,1,0:T(8,128)(2,1)S(1)}, u32[]{:S(2)}, u32[]{:S(2)}) async-start(bf16[8,96,256]{2,1,0:T(8,128)(2,1)} %get-tuple-element.22), calls=%async_computation | async-start | bytes 786432 | tf_op jit(solution)/shard_map/all_to_all | solution.py:54
  8.6 0.0 copy-done.3
  8.6 3.9 %collective-permute-start = (bf16[2,128,256]{2,1,0:T(8,128)(2,1)S(1)}, bf16[2,128,256]{2,1,0:T(8,128)(2,1)S(1)}, u32[]{:S(2)}, u32[]{:S(2)}) collective-permute-start(bf16[2,128,256]{2,1,0:T(8,128)(2,1)S(1)} %copy-done.3), channel_id=1, source_target_pairs={{0,2},{1,3},{2,0},{3,1},{4,6},{5,7},{6,4},{7,5},{8,10},{9,11},{10,... | collective-permute-start | bytes 393224 | tf_op jit(solution)/shard_map/ppermute | solution.py:45
  12.5 5.4 %collective-permute-done = bf16[2,128,256]{2,1,0:T(8,128)(2,1)S(1)} collective-permute-done((bf16[2,128,256]{2,1,0:T(8,128)(2,1)S(1)}, bf16[2,128,256]{2,1,0:T(8,128)(2,1)S(1)}, u32[]{:S(2)}, u32[]{:S(2)}) %collective-permute-start) | collective-permute-done | bytes 131104 | tf_op jit(solution)/shard_map/ppermute | solution.py:45
  17.9 0.7 all-to-all-done.parts_ref
  18.7 0.8 shard_map.78
  19.5 15.0 %all-to-all-start.1 = ((bf16[8,96,256]{2,1,0:T(8,128)(2,1)}), bf16[8,96,256]{2,1,0:T(8,128)(2,1)S(1)}, u32[]{:S(2)}, u32[]{:S(2)}) async-start(bf16[8,96,256]{2,1,0:T(8,128)(2,1)} %shard_map.78), calls=%async_computation.1 | async-start | bytes 786432 | tf_op jit(solution)/shard_map/all_to_all | solution.py:54
  34.5 4.1 %collective-permute-start.3 = (bf16[2,2,128,256]{3,2,1,0:T(8,128)(2,1)S(1)}, bf16[2,2,128,256]{3,2,1,0:T(8,128)(2,1)S(1)}, u32[]{:S(2)}, u32[]{:S(2)}) collective-permute-start(bf16[2,2,128,256]{3,2,1,0:T(8,128)(2,1)S(1)} %pad_maximum_fusion.refs_0_), channel_id=1, source_target_pairs={{0,32},{1,33},{2,34},{3,35},{4,36},{5,37},{6,38},{7,39},{8,40},{9,... | collective-permute-start | bytes 786440 | tf_op jit(solution)/shard_map/ppermute | solution.py:50
  38.6 3.1 %collective-permute-start.2 = (bf16[2,2,128,256]{3,2,1,0:T(8,128)(2,1)S(1)}, bf16[2,2,128,256]{3,2,1,0:T(8,128)(2,1)S(1)}, u32[]{:S(2)}, u32[]{:S(2)}) collective-permute-start(bf16[2,2,128,256]{3,2,1,0:T(8,128)(2,1)S(1)} %pad_maximum_fusion.refs_0_), channel_id=1, source_target_pairs={{0,48},{1,49},{2,50},{3,51},{4,52},{5,53},{6,54},{7,55},{8,56},{9,... | collective-permute-start | bytes 786440 | tf_op jit(solution)/shard_map/ppermute | solution.py:50
  41.7 2.8 %collective-permute-start.1 = (bf16[2,2,128,256]{3,2,1,0:T(8,128)(2,1)S(1)}, bf16[2,2,128,256]{3,2,1,0:T(8,128)(2,1)S(1)}, u32[]{:S(2)}, u32[]{:S(2)}) collective-permute-start(bf16[2,2,128,256]{3,2,1,0:T(8,128)(2,1)S(1)} %pad_maximum_fusion.refs_0_), channel_id=1, source_target_pairs={{0,16},{1,17},{2,18},{3,19},{4,20},{5,21},{6,22},{7,23},{8,24},{9,... | collective-permute-start | bytes 786440 | tf_op jit(solution)/shard_map/ppermute | solution.py:50
  44.5 0.4 collective-permute-done.3.refs_3_
  44.9 4.2 %collective-permute-done.2.refs_2_ = bf16[2,2,128,256]{3,2,1,0:T(8,128)(2,1)S(1)} collective-permute-done((bf16[2,2,128,256]{3,2,1,0:T(8,128)(2,1)S(1)}, bf16[2,2,128,256]{3,2,1,0:T(8,128)(2,1)S(1)}, u32[]{:S(2)}, u32[]{:S(2)}) %collective-permute-start.2) | collective-permute-done | bytes 262176 | tf_op jit(solution)/shard_map/ppermute | solution.py:50
  49.2 2.1 %collective-permute-done.1.refs_1_ = bf16[2,2,128,256]{3,2,1,0:T(8,128)(2,1)S(1)} collective-permute-done((bf16[2,2,128,256]{3,2,1,0:T(8,128)(2,1)S(1)}, bf16[2,2,128,256]{3,2,1,0:T(8,128)(2,1)S(1)}, u32[]{:S(2)}, u32[]{:S(2)}) %collective-permute-start.1) | collective-permute-done | bytes 262176 | tf_op jit(solution)/shard_map/ppermute | solution.py:50
  51.2 0.0 all-to-all-done.1.parts_ref
  51.2 0.1 shard_map.79
  51.3 0.0 copy-start
  51.3 11.1 %all_to_all.25.grads_ref = bf16[8,96,256]{2,1,0:T(8,128)(2,1)S(1)} all-to-all(bf16[8,96,256]{2,1,0:T(8,128)(2,1)S(1)} %shard_map.79), channel_id=1, replica_groups={{0,2,16,18,32,34,48,50},{1,3,17,19,33,35,49,51},{4,6,20,22,36,38,52,54}..., dimensions={0} | all-to-all | bytes 786432 | tf_op jit(solution)/shard_map/all_to_all | solution.py:54
  62.4 0.0 copy-done
  62.4 2.9 %shard_map.80 = (bf16[1,3,256,256]{3,2,1,0:T(8,128)(2,1)S(1)}, bf16[8,96,256]{2,1,0:T(8,128)(2,1)}) custom-call(bf16[8,96,256]{2,1,0:T(8,128)(2,1)S(1)} %all_to_all.25.grads_ref, bf16[1,3,256,256]{3,2,1,0:T(8,128)(2,1)S(1)} %copy-done, s32[1]{0:T(128)} %bitcast.place_ref, bf16[2,2,128,256]{3,2,1,0:T(8,128)(2,1)S(1)} %pad_maximum_fusion.refs_0_, ...), custom_call_target="tpu_custom_call" | custom-call | flops 900000000 | bytes 2621444 | tf_op jit(solution)/shard_map/pallas_call | solution.py:64
  65.3 0.0 copy-start.1
  65.3 11.6 %all-to-all-start.3 = ((bf16[8,96,256]{2,1,0:T(8,128)(2,1)}), bf16[8,96,256]{2,1,0:T(8,128)(2,1)S(1)}, u32[]{:S(2)}, u32[]{:S(2)}) async-start(bf16[8,96,256]{2,1,0:T(8,128)(2,1)} %get-tuple-element.33), calls=%async_computation.3 | async-start | bytes 786432 | tf_op jit(solution)/shard_map/all_to_all | solution.py:54
  77.0 0.0 copy-start.2
  77.0 0.0 copy-done.1
  77.0 0.7 copy-done.2
  77.7 0.6 shard_map.81
  78.2 3.4 %collective-permute-start.4 = (f32[2,128]{1,0:T(2,128)S(1)}, f32[2,128]{1,0:T(2,128)S(1)}, u32[]{:S(2)}, u32[]{:S(2)}) collective-permute-start(f32[2,128]{1,0:T(2,128)S(1)} %get-tuple-element.36), channel_id=1, source_target_pairs={{0,128},{64,192},{128,0},{192,64},{256,384},{320,448},{384,256},{4... | collective-permute-start | bytes 3080 | tf_op jit(solution)/shard_map/ppermute | solution.py:210
  81.6 2.8 %collective-permute-done.4 = f32[2,128]{1,0:T(2,128)S(1)} collective-permute-done((f32[2,128]{1,0:T(2,128)S(1)}, f32[2,128]{1,0:T(2,128)S(1)}, u32[]{:S(2)}, u32[]{:S(2)}) %collective-permute-start.4) | collective-permute-done | bytes 1056 | tf_op jit(solution)/shard_map/ppermute | solution.py:210
  84.4 3.6 %collective-permute-start.5 = (f32[2,128]{1,0:T(2,128)S(1)}, f32[2,128]{1,0:T(2,128)S(1)}, u32[]{:S(2)}, u32[]{:S(2)}) collective-permute-start(f32[2,128]{1,0:T(2,128)S(1)} %add.20), channel_id=1, source_target_pairs={{0,256},{64,320},{128,384},{192,448},{256,0},{320,64},{384,128},{4... | collective-permute-start | bytes 3080 | tf_op jit(solution)/shard_map/ppermute | solution.py:210
  88.1 2.7 %collective-permute-done.5 = f32[2,128]{1,0:T(2,128)S(1)} collective-permute-done((f32[2,128]{1,0:T(2,128)S(1)}, f32[2,128]{1,0:T(2,128)S(1)}, u32[]{:S(2)}, u32[]{:S(2)}) %collective-permute-start.5) | collective-permute-done | bytes 1056 | tf_op jit(solution)/shard_map/ppermute | solution.py:210
  90.8 0.2 all-to-all-done.3.parts_ref
  91.0 0.8 shard_map.83
  91.8 3.5 %all-to-all-start.4 = ((bf16[8,96,256]{2,1,0:T(8,128)(2,1)}), bf16[8,96,256]{2,1,0:T(8,128)(2,1)S(1)}, u32[]{:S(2)}, u32[]{:S(2)}) async-start(bf16[8,96,256]{2,1,0:T(8,128)(2,1)} %shard_map.83), calls=%async_computation.4 | async-start | bytes 786432 | tf_op jit(solution)/shard_map/all_to_all | solution.py:54
  95.3 1.9 %collective-permute-start.6 = (f32[2,128]{1,0:T(2,128)S(1)}, f32[2,128]{1,0:T(2,128)S(1)}, u32[]{:S(2)}, u32[]{:S(2)}) collective-permute-start(f32[2,128]{1,0:T(2,128)S(1)} %add.21), channel_id=1, source_target_pairs={{0,64},{64,0},{128,192},{192,128},{256,320},{320,256},{384,448},{4... | collective-permute-start | bytes 3080 | tf_op jit(solution)/shard_map/ppermute | solution.py:210
  97.2 1.1 %collective-permute-done.6 = f32[2,128]{1,0:T(2,128)S(1)} collective-permute-done((f32[2,128]{1,0:T(2,128)S(1)}, f32[2,128]{1,0:T(2,128)S(1)}, u32[]{:S(2)}, u32[]{:S(2)}) %collective-permute-start.6) | collective-permute-done | bytes 1056 | tf_op jit(solution)/shard_map/ppermute | solution.py:210
  98.3 0.8 shard_map.82
  99.1 4.1 %all-to-all-done.4.grads_ref = bf16[8,96,256]{2,1,0:T(8,128)(2,1)S(1)} async-done(((bf16[8,96,256]{2,1,0:T(8,128)(2,1)}), bf16[8,96,256]{2,1,0:T(8,128)(2,1)S(1)}, u32[]{:S(2)}, u32[]{:S(2)}) %all-to-all-start.4) | async-done | bytes 393248 | tf_op jit(solution)/shard_map/all_to_all | solution.py:54
  103.2 2.2 %shard_map.84 = bf16[1,3,256,256]{3,2,1,0:T(8,128)(2,1)} custom-call(bf16[8,96,256]{2,1,0:T(8,128)(2,1)S(1)} %all-to-all-done.4.grads_ref, bf16[1,3,256,256]{3,2,1,0:T(8,128)(2,1)S(1)} %get-tuple-element.34.w1_ref.w_ref), custom_call_target="tpu_custom_call" | custom-call | flops 600000000 | bytes 1179648 | tf_op jit(solution)/shard_map/pallas_call | solution.py:64
  (4 shorter events, 0.0 us)
Async XLA Ops:
  3.1 5.5 %copy-start.3 = (bf16[2,128,256]{2,1,0:T(8,128)(2,1)S(1)}, bf16[2,128,256]{2,1,0:T(8,128)(2,1)}, u32[]{:S(2)}) copy-start(bf16[2,128,256]{2,1,0:T(8,128)(2,1)} %get-tuple-element.23) | copy-start | bytes 393220
  3.1 15.6 %all-to-all-start = ((bf16[8,96,256]{2,1,0:T(8,128)(2,1)}), bf16[8,96,256]{2,1,0:T(8,128)(2,1)S(1)}, u32[]{:S(2)}, u32[]{:S(2)}) async-start(bf16[8,96,256]{2,1,0:T(8,128)(2,1)} %get-tuple-element.22), calls=%async_computation | async-start | bytes 786432 | tf_op jit(solution)/shard_map/all_to_all | solution.py:54
  8.6 9.4 %collective-permute-start = (bf16[2,128,256]{2,1,0:T(8,128)(2,1)S(1)}, bf16[2,128,256]{2,1,0:T(8,128)(2,1)S(1)}, u32[]{:S(2)}, u32[]{:S(2)}) collective-permute-start(bf16[2,128,256]{2,1,0:T(8,128)(2,1)S(1)} %copy-done.3), channel_id=1, source_target_pairs={{0,2},{1,3},{2,0},{3,1},{4,6},{5,7},{6,4},{7,5},{8,10},{9,11},{10,... | collective-permute-start | bytes 393224 | tf_op jit(solution)/shard_map/ppermute | solution.py:45
  19.5 31.7 %all-to-all-start.1 = ((bf16[8,96,256]{2,1,0:T(8,128)(2,1)}), bf16[8,96,256]{2,1,0:T(8,128)(2,1)S(1)}, u32[]{:S(2)}, u32[]{:S(2)}) async-start(bf16[8,96,256]{2,1,0:T(8,128)(2,1)} %shard_map.78), calls=%async_computation.1 | async-start | bytes 786432 | tf_op jit(solution)/shard_map/all_to_all | solution.py:54
  34.5 10.4 %collective-permute-start.3 = (bf16[2,2,128,256]{3,2,1,0:T(8,128)(2,1)S(1)}, bf16[2,2,128,256]{3,2,1,0:T(8,128)(2,1)S(1)}, u32[]{:S(2)}, u32[]{:S(2)}) collective-permute-start(bf16[2,2,128,256]{3,2,1,0:T(8,128)(2,1)S(1)} %pad_maximum_fusion.refs_0_), channel_id=1, source_target_pairs={{0,32},{1,33},{2,34},{3,35},{4,36},{5,37},{6,38},{7,39},{8,40},{9,... | collective-permute-start | bytes 786440 | tf_op jit(solution)/shard_map/ppermute | solution.py:50
  38.6 10.5 %collective-permute-start.2 = (bf16[2,2,128,256]{3,2,1,0:T(8,128)(2,1)S(1)}, bf16[2,2,128,256]{3,2,1,0:T(8,128)(2,1)S(1)}, u32[]{:S(2)}, u32[]{:S(2)}) collective-permute-start(bf16[2,2,128,256]{3,2,1,0:T(8,128)(2,1)S(1)} %pad_maximum_fusion.refs_0_), channel_id=1, source_target_pairs={{0,48},{1,49},{2,50},{3,51},{4,52},{5,53},{6,54},{7,55},{8,56},{9,... | collective-permute-start | bytes 786440 | tf_op jit(solution)/shard_map/ppermute | solution.py:50
  41.7 9.5 %collective-permute-start.1 = (bf16[2,2,128,256]{3,2,1,0:T(8,128)(2,1)S(1)}, bf16[2,2,128,256]{3,2,1,0:T(8,128)(2,1)S(1)}, u32[]{:S(2)}, u32[]{:S(2)}) collective-permute-start(bf16[2,2,128,256]{3,2,1,0:T(8,128)(2,1)S(1)} %pad_maximum_fusion.refs_0_), channel_id=1, source_target_pairs={{0,16},{1,17},{2,18},{3,19},{4,20},{5,21},{6,22},{7,23},{8,24},{9,... | collective-permute-start | bytes 786440 | tf_op jit(solution)/shard_map/ppermute | solution.py:50
  51.3 11.2 %copy-start = (bf16[1,3,256,256]{3,2,1,0:T(8,128)(2,1)S(1)}, bf16[1,3,256,256]{3,2,1,0:T(8,128)(2,1)}, u32[]{:S(2)}) copy-start(bf16[1,3,256,256]{3,2,1,0:T(8,128)(2,1)} %w0_ref.1) | copy-start | bytes 1179652
  65.3 11.6 %copy-start.1 = (bf16[2,128,256]{2,1,0:T(8,128)(2,1)S(1)}, bf16[2,128,256]{2,1,0:T(8,128)(2,1)}, u32[]{:S(2)}) copy-start(bf16[2,128,256]{2,1,0:T(8,128)(2,1)} %q_ref.1) | copy-start | bytes 393220
  65.3 25.7 %all-to-all-start.3 = ((bf16[8,96,256]{2,1,0:T(8,128)(2,1)}), bf16[8,96,256]{2,1,0:T(8,128)(2,1)S(1)}, u32[]{:S(2)}, u32[]{:S(2)}) async-start(bf16[8,96,256]{2,1,0:T(8,128)(2,1)} %get-tuple-element.33), calls=%async_computation.3 | async-start | bytes 786432 | tf_op jit(solution)/shard_map/all_to_all | solution.py:54
  77.0 0.7 copy-start.2
  78.2 6.2 %collective-permute-start.4 = (f32[2,128]{1,0:T(2,128)S(1)}, f32[2,128]{1,0:T(2,128)S(1)}, u32[]{:S(2)}, u32[]{:S(2)}) collective-permute-start(f32[2,128]{1,0:T(2,128)S(1)} %get-tuple-element.36), channel_id=1, source_target_pairs={{0,128},{64,192},{128,0},{192,64},{256,384},{320,448},{384,256},{4... | collective-permute-start | bytes 3080 | tf_op jit(solution)/shard_map/ppermute | solution.py:210
  84.4 6.4 %collective-permute-start.5 = (f32[2,128]{1,0:T(2,128)S(1)}, f32[2,128]{1,0:T(2,128)S(1)}, u32[]{:S(2)}, u32[]{:S(2)}) collective-permute-start(f32[2,128]{1,0:T(2,128)S(1)} %add.20), channel_id=1, source_target_pairs={{0,256},{64,320},{128,384},{192,448},{256,0},{320,64},{384,128},{4... | collective-permute-start | bytes 3080 | tf_op jit(solution)/shard_map/ppermute | solution.py:210
  91.8 11.4 %all-to-all-start.4 = ((bf16[8,96,256]{2,1,0:T(8,128)(2,1)}), bf16[8,96,256]{2,1,0:T(8,128)(2,1)S(1)}, u32[]{:S(2)}, u32[]{:S(2)}) async-start(bf16[8,96,256]{2,1,0:T(8,128)(2,1)} %shard_map.83), calls=%async_computation.4 | async-start | bytes 786432 | tf_op jit(solution)/shard_map/all_to_all | solution.py:54
  95.3 3.0 %collective-permute-start.6 = (f32[2,128]{1,0:T(2,128)S(1)}, f32[2,128]{1,0:T(2,128)S(1)}, u32[]{:S(2)}, u32[]{:S(2)}) collective-permute-start(f32[2,128]{1,0:T(2,128)S(1)} %add.21), channel_id=1, source_target_pairs={{0,64},{64,0},{128,192},{192,128},{256,320},{320,256},{384,448},{4... | collective-permute-start | bytes 3080 | tf_op jit(solution)/shard_map/ppermute | solution.py:210

commit v10 on v9

--- a/solution.py
+++ b/solution.py
@@ -35,6 +35,13 @@
     for x in range(4)
     for y_lo in range(2)
 ]
+LOOP = [
+    [token_index(x, y_hi, y_lo, 0) for y_hi in range(4)]
+    + [token_index(x, y_hi, y_lo, 1) for y_hi in reversed(range(4))]
+    for x in range(4)
+    for y_lo in range(2)
+]
+
 
 def token_pairs(move):
     places = [(x, h, l, z) for x in range(4) for h in range(4) for l in range(2) for z in range(2)]
@@ -243,7 +250,7 @@
         queries, fast_init, fresh, out_gain.reshape(1, DH), flops=10**8,
     )
     squares = add_partner(add_partner(squares, 2), 4)
-    parts, y, squares = together(exchange(shares, FAR), y, squares)
+    parts, y, squares = together(exchange(shares, LOOP), y, squares)
     whole = exchange(call(share_kernel, pieces, parts), NEAR)
     final = call(last_kernel, weights, whole, fresh, flops=6 * 10**8)
     squares = add_partner(squares, 1)

time: 106 us -> 107 us (level)
  the two profiles are of different devices: /device:TPU:16 before, /device:TPU:6 now
where the time goes in v10:
time: 107 us; the launch traced here: 105 us
  starting transfers between devices  61.9 us (58%)
  waiting for transfers between devices  20.3 us (19%)
  Pallas kernels  10.5 us (10%)
  blocking collectives  10.5 us (10%)
    all_to_all x4, starting transfers between devices, exchange(): lax.all_to_all(array, 'tokens', 0, 0, axis_index_groups=groups, tiled=True)  38.6 us
    pallas_call x8, Pallas kernels, call(): pl.pallas_call(body, out_shape=out_shape, in_specs=[pl.BlockSpec(memory_s...  10.5 us
    all_to_all x1, blocking collectives, exchange(): lax.all_to_all(array, 'tokens', 0, 0, axis_index_groups=groups, tiled=True)  10.5 us
    ppermute x3, starting transfers between devices, from_along(): return lax.ppermute(array, 'tokens', pairs)  10.4 us
    ppermute x3, starting transfers between devices, add_partner(): return squares + lax.ppermute(squares, 'heads', pairs)  9.57 us
    all_to_all x4, waiting for transfers between devices, exchange(): lax.all_to_all(array, 'tokens', 0, 0, axis_index_groups=groups, tiled=True)  6.29 us
    ppermute x3, waiting for transfers between devices, add_partner(): return squares + lax.ppermute(squares, 'heads', pairs)  5.35 us
    ppermute x3, waiting for transfers between devices, from_along(): return lax.ppermute(array, 'tokens', pairs)  5.15 us
  transfers between devices with their start and end apart: 11, of which 9 were waited for; matrix products, arithmetic and copies ran while one was open for 0% of the time, Pallas kernels for 1%

profile of v10, /device:TPU:6, one launch (start us, length us, event | category | flops | bytes accessed | tf_op | source)
XLA Modules:
  0.0 104.7 jit_solution(17894597147132356205)
XLA Ops:
  0.7 2.4 %shard_map.77 = (bf16[8,96,256]{2,1,0:T(8,128)(2,1)}, bf16[2,128,256]{2,1,0:T(8,128)(2,1)}) custom-call(bf16[2,128,256]{2,1,0:T(8,128)(2,1)} %k_hbm.1, bf16[2,128,256]{2,1,0:T(8,128)(2,1)} %v_hbm.1, f32[2,1,128]{2,1,0:T(1,128)} %r_hbm.1, bf16[1,3,256,256]{3,2,1,0:T(8,128)(2,1)} %w0_ref.1), custom_call_target="tpu_custom_call" | custom-call | flops 100000000 | bytes 1180672 | tf_op jit(solution)/shard_map/pallas_call | solution.py:71
  3.1 0.0 copy-start.3
  3.1 9.4 %all-to-all-start = ((bf16[8,96,256]{2,1,0:T(8,128)(2,1)}), bf16[8,96,256]{2,1,0:T(8,128)(2,1)S(1)}, u32[]{:S(2)}, u32[]{:S(2)}) async-start(bf16[8,96,256]{2,1,0:T(8,128)(2,1)} %get-tuple-element.22), calls=%async_computation | async-start | bytes 786432 | tf_op jit(solution)/shard_map/all_to_all | solution.py:61
  12.5 0.0 copy-done.3
  12.5 3.4 %collective-permute-start = (bf16[2,128,256]{2,1,0:T(8,128)(2,1)S(1)}, bf16[2,128,256]{2,1,0:T(8,128)(2,1)S(1)}, u32[]{:S(2)}, u32[]{:S(2)}) collective-permute-start(bf16[2,128,256]{2,1,0:T(8,128)(2,1)S(1)} %copy-done.3), channel_id=1, source_target_pairs={{0,2},{1,3},{2,0},{3,1},{4,6},{5,7},{6,4},{7,5},{8,10},{9,11},{10,... | collective-permute-start | bytes 393224 | tf_op jit(solution)/shard_map/ppermute | solution.py:52
  15.9 3.5 %collective-permute-done = bf16[2,128,256]{2,1,0:T(8,128)(2,1)S(1)} collective-permute-done((bf16[2,128,256]{2,1,0:T(8,128)(2,1)S(1)}, bf16[2,128,256]{2,1,0:T(8,128)(2,1)S(1)}, u32[]{:S(2)}, u32[]{:S(2)}) %collective-permute-start) | collective-permute-done | bytes 131104 | tf_op jit(solution)/shard_map/ppermute | solution.py:52
  19.3 0.0 all-to-all-done.parts_ref
  19.3 0.8 shard_map.78
  20.2 13.2 %all-to-all-start.1 = ((bf16[8,96,256]{2,1,0:T(8,128)(2,1)}), bf16[8,96,256]{2,1,0:T(8,128)(2,1)S(1)}, u32[]{:S(2)}, u32[]{:S(2)}) async-start(bf16[8,96,256]{2,1,0:T(8,128)(2,1)} %shard_map.78), calls=%async_computation.1 | async-start | bytes 786432 | tf_op jit(solution)/shard_map/all_to_all | solution.py:61
  33.4 3.4 %collective-permute-start.3 = (bf16[2,2,128,256]{3,2,1,0:T(8,128)(2,1)S(1)}, bf16[2,2,128,256]{3,2,1,0:T(8,128)(2,1)S(1)}, u32[]{:S(2)}, u32[]{:S(2)}) collective-permute-start(bf16[2,2,128,256]{3,2,1,0:T(8,128)(2,1)S(1)} %pad_maximum_fusion.refs_0_), channel_id=1, source_target_pairs={{0,32},{1,33},{2,34},{3,35},{4,36},{5,37},{6,38},{7,39},{8,40},{9,... | collective-permute-start | bytes 786440 | tf_op jit(solution)/shard_map/ppermute | solution.py:57
  36.7 2.6 %collective-permute-start.2 = (bf16[2,2,128,256]{3,2,1,0:T(8,128)(2,1)S(1)}, bf16[2,2,128,256]{3,2,1,0:T(8,128)(2,1)S(1)}, u32[]{:S(2)}, u32[]{:S(2)}) collective-permute-start(bf16[2,2,128,256]{3,2,1,0:T(8,128)(2,1)S(1)} %pad_maximum_fusion.refs_0_), channel_id=1, source_target_pairs={{0,48},{1,49},{2,50},{3,51},{4,52},{5,53},{6,54},{7,55},{8,56},{9,... | collective-permute-start | bytes 786440 | tf_op jit(solution)/shard_map/ppermute | solution.py:57
  39.3 4.5 %collective-permute-start.1 = (bf16[2,2,128,256]{3,2,1,0:T(8,128)(2,1)S(1)}, bf16[2,2,128,256]{3,2,1,0:T(8,128)(2,1)S(1)}, u32[]{:S(2)}, u32[]{:S(2)}) collective-permute-start(bf16[2,2,128,256]{3,2,1,0:T(8,128)(2,1)S(1)} %pad_maximum_fusion.refs_0_), channel_id=1, source_target_pairs={{0,16},{1,17},{2,18},{3,19},{4,20},{5,21},{6,22},{7,23},{8,24},{9,... | collective-permute-start | bytes 786440 | tf_op jit(solution)/shard_map/ppermute | solution.py:57
  43.8 2.1 %collective-permute-done.3.refs_3_ = bf16[2,2,128,256]{3,2,1,0:T(8,128)(2,1)S(1)} collective-permute-done((bf16[2,2,128,256]{3,2,1,0:T(8,128)(2,1)S(1)}, bf16[2,2,128,256]{3,2,1,0:T(8,128)(2,1)S(1)}, u32[]{:S(2)}, u32[]{:S(2)}) %collective-permute-start.3) | collective-permute-done | bytes 262176 | tf_op jit(solution)/shard_map/ppermute | solution.py:57
  45.9 3.1 %collective-permute-done.2.refs_2_ = bf16[2,2,128,256]{3,2,1,0:T(8,128)(2,1)S(1)} collective-permute-done((bf16[2,2,128,256]{3,2,1,0:T(8,128)(2,1)S(1)}, bf16[2,2,128,256]{3,2,1,0:T(8,128)(2,1)S(1)}, u32[]{:S(2)}, u32[]{:S(2)}) %collective-permute-start.2) | collective-permute-done | bytes 262176 | tf_op jit(solution)/shard_map/ppermute | solution.py:57
  48.9 0.0 collective-permute-done.1.refs_1_
  48.9 1.7 %all-to-all-done.1.parts_ref = bf16[8,96,256]{2,1,0:T(8,128)(2,1)S(1)} async-done(((bf16[8,96,256]{2,1,0:T(8,128)(2,1)}), bf16[8,96,256]{2,1,0:T(8,128)(2,1)S(1)}, u32[]{:S(2)}, u32[]{:S(2)}) %all-to-all-start.1) | async-done | bytes 393248 | tf_op jit(solution)/shard_map/all_to_all | solution.py:61
  50.7 0.1 shard_map.79
  50.7 0.0 copy-start
  50.7 10.5 %all_to_all.25.grads_ref = bf16[8,96,256]{2,1,0:T(8,128)(2,1)S(1)} all-to-all(bf16[8,96,256]{2,1,0:T(8,128)(2,1)S(1)} %shard_map.79), channel_id=1, replica_groups={{0,2,16,18,32,34,48,50},{1,3,17,19,33,35,49,51},{4,6,20,22,36,38,52,54}..., dimensions={0} | all-to-all | bytes 786432 | tf_op jit(solution)/shard_map/all_to_all | solution.py:61
  61.3 0.0 copy-done
  61.3 2.9 %shard_map.80 = (bf16[1,3,256,256]{3,2,1,0:T(8,128)(2,1)S(1)}, bf16[8,96,256]{2,1,0:T(8,128)(2,1)}) custom-call(bf16[8,96,256]{2,1,0:T(8,128)(2,1)S(1)} %all_to_all.25.grads_ref, bf16[1,3,256,256]{3,2,1,0:T(8,128)(2,1)S(1)} %copy-done, s32[1]{0:T(128)} %bitcast.place_ref, bf16[2,2,128,256]{3,2,1,0:T(8,128)(2,1)S(1)} %pad_maximum_fusion.refs_0_, ...), custom_call_target="tpu_custom_call" | custom-call | flops 900000000 | bytes 2621444 | tf_op jit(solution)/shard_map/pallas_call | solution.py:71
  64.2 0.0 copy-start.1
  64.2 10.7 %all-to-all-start.3 = ((bf16[8,96,256]{2,1,0:T(8,128)(2,1)}), bf16[8,96,256]{2,1,0:T(8,128)(2,1)S(1)}, u32[]{:S(2)}, u32[]{:S(2)}) async-start(bf16[8,96,256]{2,1,0:T(8,128)(2,1)} %get-tuple-element.33), calls=%async_computation.3 | async-start | bytes 786432 | tf_op jit(solution)/shard_map/all_to_all | solution.py:61
  74.9 0.0 copy-start.2
  74.9 0.0 copy-done.1
  74.9 0.7 copy-done.2
  75.5 0.6 shard_map.81
  76.1 3.4 %collective-permute-start.4 = (f32[2,128]{1,0:T(2,128)S(1)}, f32[2,128]{1,0:T(2,128)S(1)}, u32[]{:S(2)}, u32[]{:S(2)}) collective-permute-start(f32[2,128]{1,0:T(2,128)S(1)} %get-tuple-element.36), channel_id=1, source_target_pairs={{0,128},{64,192},{128,0},{192,64},{256,384},{320,448},{384,256},{4... | collective-permute-start | bytes 3080 | tf_op jit(solution)/shard_map/ppermute | solution.py:217
  79.5 2.1 %collective-permute-done.4 = f32[2,128]{1,0:T(2,128)S(1)} collective-permute-done((f32[2,128]{1,0:T(2,128)S(1)}, f32[2,128]{1,0:T(2,128)S(1)}, u32[]{:S(2)}, u32[]{:S(2)}) %collective-permute-start.4) | collective-permute-done | bytes 1056 | tf_op jit(solution)/shard_map/ppermute | solution.py:217
  81.6 4.3 %collective-permute-start.5 = (f32[2,128]{1,0:T(2,128)S(1)}, f32[2,128]{1,0:T(2,128)S(1)}, u32[]{:S(2)}, u32[]{:S(2)}) collective-permute-start(f32[2,128]{1,0:T(2,128)S(1)} %add.20), channel_id=1, source_target_pairs={{0,256},{64,320},{128,384},{192,448},{256,0},{320,64},{384,128},{4... | collective-permute-start | bytes 3080 | tf_op jit(solution)/shard_map/ppermute | solution.py:217
  85.9 2.2 %collective-permute-done.5 = f32[2,128]{1,0:T(2,128)S(1)} collective-permute-done((f32[2,128]{1,0:T(2,128)S(1)}, f32[2,128]{1,0:T(2,128)S(1)}, u32[]{:S(2)}, u32[]{:S(2)}) %collective-permute-start.5) | collective-permute-done | bytes 1056 | tf_op jit(solution)/shard_map/ppermute | solution.py:217
  88.1 2.8 %all-to-all-done.3.parts_ref = bf16[8,96,256]{2,1,0:T(8,128)(2,1)S(1)} async-done(((bf16[8,96,256]{2,1,0:T(8,128)(2,1)}), bf16[8,96,256]{2,1,0:T(8,128)(2,1)S(1)}, u32[]{:S(2)}, u32[]{:S(2)}) %all-to-all-start.3) | async-done | bytes 393248 | tf_op jit(solution)/shard_map/all_to_all | solution.py:61
  90.8 0.8 shard_map.83
  91.6 5.3 %all-to-all-start.4 = ((bf16[8,96,256]{2,1,0:T(8,128)(2,1)}), bf16[8,96,256]{2,1,0:T(8,128)(2,1)S(1)}, u32[]{:S(2)}, u32[]{:S(2)}) async-start(bf16[8,96,256]{2,1,0:T(8,128)(2,1)} %shard_map.83), calls=%async_computation.4 | async-start | bytes 786432 | tf_op jit(solution)/shard_map/all_to_all | solution.py:61
  96.9 1.9 %collective-permute-start.6 = (f32[2,128]{1,0:T(2,128)S(1)}, f32[2,128]{1,0:T(2,128)S(1)}, u32[]{:S(2)}, u32[]{:S(2)}) collective-permute-start(f32[2,128]{1,0:T(2,128)S(1)} %add.21), channel_id=1, source_target_pairs={{0,64},{64,0},{128,192},{192,128},{256,320},{320,256},{384,448},{4... | collective-permute-start | bytes 3080 | tf_op jit(solution)/shard_map/ppermute | solution.py:217
  98.9 1.1 %collective-permute-done.6 = f32[2,128]{1,0:T(2,128)S(1)} collective-permute-done((f32[2,128]{1,0:T(2,128)S(1)}, f32[2,128]{1,0:T(2,128)S(1)}, u32[]{:S(2)}, u32[]{:S(2)}) %collective-permute-start.6) | collective-permute-done | bytes 1056 | tf_op jit(solution)/shard_map/ppermute | solution.py:217
  100.0 0.8 shard_map.82
  100.7 1.8 %all-to-all-done.4.grads_ref = bf16[8,96,256]{2,1,0:T(8,128)(2,1)S(1)} async-done(((bf16[8,96,256]{2,1,0:T(8,128)(2,1)}), bf16[8,96,256]{2,1,0:T(8,128)(2,1)S(1)}, u32[]{:S(2)}, u32[]{:S(2)}) %all-to-all-start.4) | async-done | bytes 393248 | tf_op jit(solution)/shard_map/all_to_all | solution.py:61
  102.5 2.2 %shard_map.84 = bf16[1,3,256,256]{3,2,1,0:T(8,128)(2,1)} custom-call(bf16[8,96,256]{2,1,0:T(8,128)(2,1)S(1)} %all-to-all-done.4.grads_ref, bf16[1,3,256,256]{3,2,1,0:T(8,128)(2,1)S(1)} %get-tuple-element.34.w1_ref.w_ref), custom_call_target="tpu_custom_call" | custom-call | flops 600000000 | bytes 1179648 | tf_op jit(solution)/shard_map/pallas_call | solution.py:71
  (4 shorter events, 0.0 us)
Async XLA Ops:
  3.1 9.4 %copy-start.3 = (bf16[2,128,256]{2,1,0:T(8,128)(2,1)S(1)}, bf16[2,128,256]{2,1,0:T(8,128)(2,1)}, u32[]{:S(2)}) copy-start(bf16[2,128,256]{2,1,0:T(8,128)(2,1)} %get-tuple-element.23) | copy-start | bytes 393220
  3.1 16.2 %all-to-all-start = ((bf16[8,96,256]{2,1,0:T(8,128)(2,1)}), bf16[8,96,256]{2,1,0:T(8,128)(2,1)S(1)}, u32[]{:S(2)}, u32[]{:S(2)}) async-start(bf16[8,96,256]{2,1,0:T(8,128)(2,1)} %get-tuple-element.22), calls=%async_computation | async-start | bytes 786432 | tf_op jit(solution)/shard_map/all_to_all | solution.py:61
  12.5 6.8 %collective-permute-start = (bf16[2,128,256]{2,1,0:T(8,128)(2,1)S(1)}, bf16[2,128,256]{2,1,0:T(8,128)(2,1)S(1)}, u32[]{:S(2)}, u32[]{:S(2)}) collective-permute-start(bf16[2,128,256]{2,1,0:T(8,128)(2,1)S(1)} %copy-done.3), channel_id=1, source_target_pairs={{0,2},{1,3},{2,0},{3,1},{4,6},{5,7},{6,4},{7,5},{8,10},{9,11},{10,... | collective-permute-start | bytes 393224 | tf_op jit(solution)/shard_map/ppermute | solution.py:52
  20.2 30.5 %all-to-all-start.1 = ((bf16[8,96,256]{2,1,0:T(8,128)(2,1)}), bf16[8,96,256]{2,1,0:T(8,128)(2,1)S(1)}, u32[]{:S(2)}, u32[]{:S(2)}) async-start(bf16[8,96,256]{2,1,0:T(8,128)(2,1)} %shard_map.78), calls=%async_computation.1 | async-start | bytes 786432 | tf_op jit(solution)/shard_map/all_to_all | solution.py:61
  33.4 12.5 %collective-permute-start.3 = (bf16[2,2,128,256]{3,2,1,0:T(8,128)(2,1)S(1)}, bf16[2,2,128,256]{3,2,1,0:T(8,128)(2,1)S(1)}, u32[]{:S(2)}, u32[]{:S(2)}) collective-permute-start(bf16[2,2,128,256]{3,2,1,0:T(8,128)(2,1)S(1)} %pad_maximum_fusion.refs_0_), channel_id=1, source_target_pairs={{0,32},{1,33},{2,34},{3,35},{4,36},{5,37},{6,38},{7,39},{8,40},{9,... | collective-permute-start | bytes 786440 | tf_op jit(solution)/shard_map/ppermute | solution.py:57
  36.7 12.2 %collective-permute-start.2 = (bf16[2,2,128,256]{3,2,1,0:T(8,128)(2,1)S(1)}, bf16[2,2,128,256]{3,2,1,0:T(8,128)(2,1)S(1)}, u32[]{:S(2)}, u32[]{:S(2)}) collective-permute-start(bf16[2,2,128,256]{3,2,1,0:T(8,128)(2,1)S(1)} %pad_maximum_fusion.refs_0_), channel_id=1, source_target_pairs={{0,48},{1,49},{2,50},{3,51},{4,52},{5,53},{6,54},{7,55},{8,56},{9,... | collective-permute-start | bytes 786440 | tf_op jit(solution)/shard_map/ppermute | solution.py:57
  39.3 9.6 %collective-permute-start.1 = (bf16[2,2,128,256]{3,2,1,0:T(8,128)(2,1)S(1)}, bf16[2,2,128,256]{3,2,1,0:T(8,128)(2,1)S(1)}, u32[]{:S(2)}, u32[]{:S(2)}) collective-permute-start(bf16[2,2,128,256]{3,2,1,0:T(8,128)(2,1)S(1)} %pad_maximum_fusion.refs_0_), channel_id=1, source_target_pairs={{0,16},{1,17},{2,18},{3,19},{4,20},{5,21},{6,22},{7,23},{8,24},{9,... | collective-permute-start | bytes 786440 | tf_op jit(solution)/shard_map/ppermute | solution.py:57
  50.7 10.5 %copy-start = (bf16[1,3,256,256]{3,2,1,0:T(8,128)(2,1)S(1)}, bf16[1,3,256,256]{3,2,1,0:T(8,128)(2,1)}, u32[]{:S(2)}) copy-start(bf16[1,3,256,256]{3,2,1,0:T(8,128)(2,1)} %w0_ref.1) | copy-start | bytes 1179652
  64.2 10.7 %copy-start.1 = (bf16[2,128,256]{2,1,0:T(8,128)(2,1)S(1)}, bf16[2,128,256]{2,1,0:T(8,128)(2,1)}, u32[]{:S(2)}) copy-start(bf16[2,128,256]{2,1,0:T(8,128)(2,1)} %q_ref.1) | copy-start | bytes 393220
  64.2 26.7 %all-to-all-start.3 = ((bf16[8,96,256]{2,1,0:T(8,128)(2,1)}), bf16[8,96,256]{2,1,0:T(8,128)(2,1)S(1)}, u32[]{:S(2)}, u32[]{:S(2)}) async-start(bf16[8,96,256]{2,1,0:T(8,128)(2,1)} %get-tuple-element.33), calls=%async_computation.3 | async-start | bytes 786432 | tf_op jit(solution)/shard_map/all_to_all | solution.py:61
  74.9 0.7 copy-start.2
  76.1 5.5 %collective-permute-start.4 = (f32[2,128]{1,0:T(2,128)S(1)}, f32[2,128]{1,0:T(2,128)S(1)}, u32[]{:S(2)}, u32[]{:S(2)}) collective-permute-start(f32[2,128]{1,0:T(2,128)S(1)} %get-tuple-element.36), channel_id=1, source_target_pairs={{0,128},{64,192},{128,0},{192,64},{256,384},{320,448},{384,256},{4... | collective-permute-start | bytes 3080 | tf_op jit(solution)/shard_map/ppermute | solution.py:217
  81.6 6.5 %collective-permute-start.5 = (f32[2,128]{1,0:T(2,128)S(1)}, f32[2,128]{1,0:T(2,128)S(1)}, u32[]{:S(2)}, u32[]{:S(2)}) collective-permute-start(f32[2,128]{1,0:T(2,128)S(1)} %add.20), channel_id=1, source_target_pairs={{0,256},{64,320},{128,384},{192,448},{256,0},{320,64},{384,128},{4... | collective-permute-start | bytes 3080 | tf_op jit(solution)/shard_map/ppermute | solution.py:217
  91.6 10.9 %all-to-all-start.4 = ((bf16[8,96,256]{2,1,0:T(8,128)(2,1)}), bf16[8,96,256]{2,1,0:T(8,128)(2,1)S(1)}, u32[]{:S(2)}, u32[]{:S(2)}) async-start(bf16[8,96,256]{2,1,0:T(8,128)(2,1)} %shard_map.83), calls=%async_computation.4 | async-start | bytes 786432 | tf_op jit(solution)/shard_map/all_to_all | solution.py:61
  96.9 3.0 %collective-permute-start.6 = (f32[2,128]{1,0:T(2,128)S(1)}, f32[2,128]{1,0:T(2,128)S(1)}, u32[]{:S(2)}, u32[]{:S(2)}) collective-permute-start(f32[2,128]{1,0:T(2,128)S(1)} %add.21), channel_id=1, source_target_pairs={{0,64},{64,0},{128,192},{192,128},{256,320},{320,256},{384,448},{4... | collective-permute-start | bytes 3080 | tf_op jit(solution)/shard_map/ppermute | solution.py:217

commit v11 on v9

--- a/solution.py
+++ b/solution.py
@@ -228,7 +228,7 @@
     grads, place = together(grads, place)
     parts, beside = together(exchange(grads, NEAR), from_beside(ahead))
     shares = call(share_kernel, pieces, parts)
-    shares, pair = together(shares, jnp.stack([ahead, beside]))
+    pair = jnp.stack([ahead, beside])
     parts, *others = together(
         exchange(shares, FAR), *(from_along(pair, steps) for steps in (1, 3, 2))
     )

time: 106 us -> 106 us (level)
  no operation moved by 1% of the time
where the time goes in v11:
time: 106 us; the launch traced here: 105 us
  starting transfers between devices  58.4 us (55%)
  waiting for transfers between devices  23.9 us (23%)
  blocking collectives  11.1 us (10%)
  Pallas kernels  10.5 us (10%)
    all_to_all x4, starting transfers between devices, exchange(): lax.all_to_all(array, 'tokens', 0, 0, axis_index_groups=groups, tiled=True)  35.6 us
    all_to_all x1, blocking collectives, exchange(): lax.all_to_all(array, 'tokens', 0, 0, axis_index_groups=groups, tiled=True)  11.1 us
    pallas_call x8, Pallas kernels, call(): pl.pallas_call(body, out_shape=out_shape, in_specs=[pl.BlockSpec(memory_s...  10.5 us
    ppermute x3, starting transfers between devices, from_along(): return lax.ppermute(array, 'tokens', pairs)  10 us
    ppermute x3, starting transfers between devices, add_partner(): return squares + lax.ppermute(squares, 'heads', pairs)  8.92 us
    ppermute x3, waiting for transfers between devices, from_along(): return lax.ppermute(array, 'tokens', pairs)  6.72 us
    ppermute x3, waiting for transfers between devices, add_partner(): return squares + lax.ppermute(squares, 'heads', pairs)  6.64 us
    ppermute x1, waiting for transfers between devices, from_beside(): lax.ppermute(array, 'tokens', token_pairs(lambda x, h, l, z: (x, h, 1 - l...  5.44 us
  transfers between devices with their start and end apart: 11, of which 10 were waited for; matrix products, arithmetic and copies ran while one was open for 0% of the time, Pallas kernels for 1%

profile of v11, /device:TPU:16, one launch (start us, length us, event | category | flops | bytes accessed | tf_op | source)
XLA Modules:
  0.0 105.4 jit_solution(9525855605907979241)
XLA Ops:
  0.7 2.4 %shard_map.77 = (bf16[8,96,256]{2,1,0:T(8,128)(2,1)}, bf16[2,128,256]{2,1,0:T(8,128)(2,1)}) custom-call(bf16[2,128,256]{2,1,0:T(8,128)(2,1)} %k_hbm.1, bf16[2,128,256]{2,1,0:T(8,128)(2,1)} %v_hbm.1, f32[2,1,128]{2,1,0:T(1,128)} %r_hbm.1, bf16[1,3,256,256]{3,2,1,0:T(8,128)(2,1)} %w0_ref.1), custom_call_target="tpu_custom_call" | custom-call | flops 100000000 | bytes 1180672 | tf_op jit(solution)/shard_map/pallas_call | solution.py:64
  3.1 0.0 copy-start.3
  3.1 5.5 %all-to-all-start = ((bf16[8,96,256]{2,1,0:T(8,128)(2,1)}), bf16[8,96,256]{2,1,0:T(8,128)(2,1)S(1)}, u32[]{:S(2)}, u32[]{:S(2)}) async-start(bf16[8,96,256]{2,1,0:T(8,128)(2,1)} %get-tuple-element.20), calls=%async_computation | async-start | bytes 786432 | tf_op jit(solution)/shard_map/all_to_all | solution.py:54
  8.6 0.0 copy-done.3
  8.6 3.9 %collective-permute-start = (bf16[2,128,256]{2,1,0:T(8,128)(2,1)S(1)}, bf16[2,128,256]{2,1,0:T(8,128)(2,1)S(1)}, u32[]{:S(2)}, u32[]{:S(2)}) collective-permute-start(bf16[2,128,256]{2,1,0:T(8,128)(2,1)S(1)} %copy-done.3), channel_id=1, source_target_pairs={{0,2},{1,3},{2,0},{3,1},{4,6},{5,7},{6,4},{7,5},{8,10},{9,11},{10,... | collective-permute-start | bytes 393224 | tf_op jit(solution)/shard_map/ppermute | solution.py:45
  12.5 5.4 %collective-permute-done = bf16[2,128,256]{2,1,0:T(8,128)(2,1)S(1)} collective-permute-done((bf16[2,128,256]{2,1,0:T(8,128)(2,1)S(1)}, bf16[2,128,256]{2,1,0:T(8,128)(2,1)S(1)}, u32[]{:S(2)}, u32[]{:S(2)}) %collective-permute-start) | collective-permute-done | bytes 131104 | tf_op jit(solution)/shard_map/ppermute | solution.py:45
  17.9 0.7 all-to-all-done.parts_ref
  18.7 0.8 shard_map.78
  19.5 15.0 %all-to-all-start.1 = ((bf16[8,96,256]{2,1,0:T(8,128)(2,1)}), bf16[8,96,256]{2,1,0:T(8,128)(2,1)S(1)}, u32[]{:S(2)}, u32[]{:S(2)}) async-start(bf16[8,96,256]{2,1,0:T(8,128)(2,1)} %shard_map.78), calls=%async_computation.1 | async-start | bytes 786432 | tf_op jit(solution)/shard_map/all_to_all | solution.py:54
  34.5 4.2 %collective-permute-start.3 = (bf16[2,2,128,256]{3,2,1,0:T(8,128)(2,1)S(1)}, bf16[2,2,128,256]{3,2,1,0:T(8,128)(2,1)S(1)}, u32[]{:S(2)}, u32[]{:S(2)}) collective-permute-start(bf16[2,2,128,256]{3,2,1,0:T(8,128)(2,1)S(1)} %pad_maximum_fusion.refs_0_), channel_id=1, source_target_pairs={{0,32},{1,33},{2,34},{3,35},{4,36},{5,37},{6,38},{7,39},{8,40},{9,... | collective-permute-start | bytes 786440 | tf_op jit(solution)/shard_map/ppermute | solution.py:50
  38.6 3.1 %collective-permute-start.2 = (bf16[2,2,128,256]{3,2,1,0:T(8,128)(2,1)S(1)}, bf16[2,2,128,256]{3,2,1,0:T(8,128)(2,1)S(1)}, u32[]{:S(2)}, u32[]{:S(2)}) collective-permute-start(bf16[2,2,128,256]{3,2,1,0:T(8,128)(2,1)S(1)} %pad_maximum_fusion.refs_0_), channel_id=1, source_target_pairs={{0,48},{1,49},{2,50},{3,51},{4,52},{5,53},{6,54},{7,55},{8,56},{9,... | collective-permute-start | bytes 786440 | tf_op jit(solution)/shard_map/ppermute | solution.py:50
  41.7 2.8 %collective-permute-start.1 = (bf16[2,2,128,256]{3,2,1,0:T(8,128)(2,1)S(1)}, bf16[2,2,128,256]{3,2,1,0:T(8,128)(2,1)S(1)}, u32[]{:S(2)}, u32[]{:S(2)}) collective-permute-start(bf16[2,2,128,256]{3,2,1,0:T(8,128)(2,1)S(1)} %pad_maximum_fusion.refs_0_), channel_id=1, source_target_pairs={{0,16},{1,17},{2,18},{3,19},{4,20},{5,21},{6,22},{7,23},{8,24},{9,... | collective-permute-start | bytes 786440 | tf_op jit(solution)/shard_map/ppermute | solution.py:50
  44.5 0.4 collective-permute-done.3.refs_3_
  44.9 4.2 %collective-permute-done.2.refs_2_ = bf16[2,2,128,256]{3,2,1,0:T(8,128)(2,1)S(1)} collective-permute-done((bf16[2,2,128,256]{3,2,1,0:T(8,128)(2,1)S(1)}, bf16[2,2,128,256]{3,2,1,0:T(8,128)(2,1)S(1)}, u32[]{:S(2)}, u32[]{:S(2)}) %collective-permute-start.2) | collective-permute-done | bytes 262176 | tf_op jit(solution)/shard_map/ppermute | solution.py:50
  49.2 2.1 %collective-permute-done.1.refs_1_ = bf16[2,2,128,256]{3,2,1,0:T(8,128)(2,1)S(1)} collective-permute-done((bf16[2,2,128,256]{3,2,1,0:T(8,128)(2,1)S(1)}, bf16[2,2,128,256]{3,2,1,0:T(8,128)(2,1)S(1)}, u32[]{:S(2)}, u32[]{:S(2)}) %collective-permute-start.1) | collective-permute-done | bytes 262176 | tf_op jit(solution)/shard_map/ppermute | solution.py:50
  51.2 0.0 all-to-all-done.1.parts_ref
  51.2 0.1 shard_map.79
  51.3 0.0 copy-start
  51.3 11.1 %all_to_all.25.grads_ref = bf16[8,96,256]{2,1,0:T(8,128)(2,1)S(1)} all-to-all(bf16[8,96,256]{2,1,0:T(8,128)(2,1)S(1)} %shard_map.79), channel_id=1, replica_groups={{0,2,16,18,32,34,48,50},{1,3,17,19,33,35,49,51},{4,6,20,22,36,38,52,54}..., dimensions={0} | all-to-all | bytes 786432 | tf_op jit(solution)/shard_map/all_to_all | solution.py:54
  62.4 0.0 copy-done
  62.4 2.9 %shard_map.80 = (bf16[1,3,256,256]{3,2,1,0:T(8,128)(2,1)S(1)}, bf16[8,96,256]{2,1,0:T(8,128)(2,1)}) custom-call(bf16[8,96,256]{2,1,0:T(8,128)(2,1)S(1)} %all_to_all.25.grads_ref, bf16[1,3,256,256]{3,2,1,0:T(8,128)(2,1)S(1)} %copy-done, s32[1]{0:T(128)} %bitcast.place_ref, bf16[2,2,128,256]{3,2,1,0:T(8,128)(2,1)S(1)} %pad_maximum_fusion.refs_0_, ...), custom_call_target="tpu_custom_call" | custom-call | flops 900000000 | bytes 2621444 | tf_op jit(solution)/shard_map/pallas_call | solution.py:64
  65.3 0.0 copy-start.1
  65.3 11.7 %all-to-all-start.3 = ((bf16[8,96,256]{2,1,0:T(8,128)(2,1)}), bf16[8,96,256]{2,1,0:T(8,128)(2,1)S(1)}, u32[]{:S(2)}, u32[]{:S(2)}) async-start(bf16[8,96,256]{2,1,0:T(8,128)(2,1)} %get-tuple-element.29), calls=%async_computation.3 | async-start | bytes 786432 | tf_op jit(solution)/shard_map/all_to_all | solution.py:54
  77.0 0.0 copy-start.2
  77.0 0.0 copy-done.1
  77.0 0.7 copy-done.2
  77.7 0.6 shard_map.81
  78.2 3.4 %collective-permute-start.4 = (f32[2,128]{1,0:T(2,128)S(1)}, f32[2,128]{1,0:T(2,128)S(1)}, u32[]{:S(2)}, u32[]{:S(2)}) collective-permute-start(f32[2,128]{1,0:T(2,128)S(1)} %get-tuple-element.32), channel_id=1, source_target_pairs={{0,128},{64,192},{128,0},{192,64},{256,384},{320,448},{384,256},{4... | collective-permute-start | bytes 3080 | tf_op jit(solution)/shard_map/ppermute | solution.py:210
  81.6 2.8 %collective-permute-done.4 = f32[2,128]{1,0:T(2,128)S(1)} collective-permute-done((f32[2,128]{1,0:T(2,128)S(1)}, f32[2,128]{1,0:T(2,128)S(1)}, u32[]{:S(2)}, u32[]{:S(2)}) %collective-permute-start.4) | collective-permute-done | bytes 1056 | tf_op jit(solution)/shard_map/ppermute | solution.py:210
  84.4 3.6 %collective-permute-start.5 = (f32[2,128]{1,0:T(2,128)S(1)}, f32[2,128]{1,0:T(2,128)S(1)}, u32[]{:S(2)}, u32[]{:S(2)}) collective-permute-start(f32[2,128]{1,0:T(2,128)S(1)} %add.20), channel_id=1, source_target_pairs={{0,256},{64,320},{128,384},{192,448},{256,0},{320,64},{384,128},{4... | collective-permute-start | bytes 3080 | tf_op jit(solution)/shard_map/ppermute | solution.py:210
  88.1 2.7 %collective-permute-done.5 = f32[2,128]{1,0:T(2,128)S(1)} collective-permute-done((f32[2,128]{1,0:T(2,128)S(1)}, f32[2,128]{1,0:T(2,128)S(1)}, u32[]{:S(2)}, u32[]{:S(2)}) %collective-permute-start.5) | collective-permute-done | bytes 1056 | tf_op jit(solution)/shard_map/ppermute | solution.py:210
  90.8 0.2 all-to-all-done.3.parts_ref
  91.0 0.8 shard_map.83
  91.8 3.5 %all-to-all-start.4 = ((bf16[8,96,256]{2,1,0:T(8,128)(2,1)}), bf16[8,96,256]{2,1,0:T(8,128)(2,1)S(1)}, u32[]{:S(2)}, u32[]{:S(2)}) async-start(bf16[8,96,256]{2,1,0:T(8,128)(2,1)} %shard_map.83), calls=%async_computation.4 | async-start | bytes 786432 | tf_op jit(solution)/shard_map/all_to_all | solution.py:54
  95.3 1.9 %collective-permute-start.6 = (f32[2,128]{1,0:T(2,128)S(1)}, f32[2,128]{1,0:T(2,128)S(1)}, u32[]{:S(2)}, u32[]{:S(2)}) collective-permute-start(f32[2,128]{1,0:T(2,128)S(1)} %add.21), channel_id=1, source_target_pairs={{0,64},{64,0},{128,192},{192,128},{256,320},{320,256},{384,448},{4... | collective-permute-start | bytes 3080 | tf_op jit(solution)/shard_map/ppermute | solution.py:210
  97.2 1.1 %collective-permute-done.6 = f32[2,128]{1,0:T(2,128)S(1)} collective-permute-done((f32[2,128]{1,0:T(2,128)S(1)}, f32[2,128]{1,0:T(2,128)S(1)}, u32[]{:S(2)}, u32[]{:S(2)}) %collective-permute-start.6) | collective-permute-done | bytes 1056 | tf_op jit(solution)/shard_map/ppermute | solution.py:210
  98.3 0.8 shard_map.82
  99.1 4.1 %all-to-all-done.4.grads_ref = bf16[8,96,256]{2,1,0:T(8,128)(2,1)S(1)} async-done(((bf16[8,96,256]{2,1,0:T(8,128)(2,1)}), bf16[8,96,256]{2,1,0:T(8,128)(2,1)S(1)}, u32[]{:S(2)}, u32[]{:S(2)}) %all-to-all-start.4) | async-done | bytes 393248 | tf_op jit(solution)/shard_map/all_to_all | solution.py:54
  103.2 2.2 %shard_map.84 = bf16[1,3,256,256]{3,2,1,0:T(8,128)(2,1)} custom-call(bf16[8,96,256]{2,1,0:T(8,128)(2,1)S(1)} %all-to-all-done.4.grads_ref, bf16[1,3,256,256]{3,2,1,0:T(8,128)(2,1)S(1)} %get-tuple-element.30.w1_ref.w_ref), custom_call_target="tpu_custom_call" | custom-call | flops 600000000 | bytes 1179648 | tf_op jit(solution)/shard_map/pallas_call | solution.py:64
  (4 shorter events, 0.0 us)
Async XLA Ops:
  3.1 5.5 %copy-start.3 = (bf16[2,128,256]{2,1,0:T(8,128)(2,1)S(1)}, bf16[2,128,256]{2,1,0:T(8,128)(2,1)}, u32[]{:S(2)}) copy-start(bf16[2,128,256]{2,1,0:T(8,128)(2,1)} %get-tuple-element.21) | copy-start | bytes 393220
  3.1 15.6 %all-to-all-start = ((bf16[8,96,256]{2,1,0:T(8,128)(2,1)}), bf16[8,96,256]{2,1,0:T(8,128)(2,1)S(1)}, u32[]{:S(2)}, u32[]{:S(2)}) async-start(bf16[8,96,256]{2,1,0:T(8,128)(2,1)} %get-tuple-element.20), calls=%async_computation | async-start | bytes 786432 | tf_op jit(solution)/shard_map/all_to_all | solution.py:54
  8.6 9.4 %collective-permute-start = (bf16[2,128,256]{2,1,0:T(8,128)(2,1)S(1)}, bf16[2,128,256]{2,1,0:T(8,128)(2,1)S(1)}, u32[]{:S(2)}, u32[]{:S(2)}) collective-permute-start(bf16[2,128,256]{2,1,0:T(8,128)(2,1)S(1)} %copy-done.3), channel_id=1, source_target_pairs={{0,2},{1,3},{2,0},{3,1},{4,6},{5,7},{6,4},{7,5},{8,10},{9,11},{10,... | collective-permute-start | bytes 393224 | tf_op jit(solution)/shard_map/ppermute | solution.py:45
  19.5 31.7 %all-to-all-start.1 = ((bf16[8,96,256]{2,1,0:T(8,128)(2,1)}), bf16[8,96,256]{2,1,0:T(8,128)(2,1)S(1)}, u32[]{:S(2)}, u32[]{:S(2)}) async-start(bf16[8,96,256]{2,1,0:T(8,128)(2,1)} %shard_map.78), calls=%async_computation.1 | async-start | bytes 786432 | tf_op jit(solution)/shard_map/all_to_all | solution.py:54
  34.5 10.5 %collective-permute-start.3 = (bf16[2,2,128,256]{3,2,1,0:T(8,128)(2,1)S(1)}, bf16[2,2,128,256]{3,2,1,0:T(8,128)(2,1)S(1)}, u32[]{:S(2)}, u32[]{:S(2)}) collective-permute-start(bf16[2,2,128,256]{3,2,1,0:T(8,128)(2,1)S(1)} %pad_maximum_fusion.refs_0_), channel_id=1, source_target_pairs={{0,32},{1,33},{2,34},{3,35},{4,36},{5,37},{6,38},{7,39},{8,40},{9,... | collective-permute-start | bytes 786440 | tf_op jit(solution)/shard_map/ppermute | solution.py:50
  38.6 10.5 %collective-permute-start.2 = (bf16[2,2,128,256]{3,2,1,0:T(8,128)(2,1)S(1)}, bf16[2,2,128,256]{3,2,1,0:T(8,128)(2,1)S(1)}, u32[]{:S(2)}, u32[]{:S(2)}) collective-permute-start(bf16[2,2,128,256]{3,2,1,0:T(8,128)(2,1)S(1)} %pad_maximum_fusion.refs_0_), channel_id=1, source_target_pairs={{0,48},{1,49},{2,50},{3,51},{4,52},{5,53},{6,54},{7,55},{8,56},{9,... | collective-permute-start | bytes 786440 | tf_op jit(solution)/shard_map/ppermute | solution.py:50
  41.7 9.5 %collective-permute-start.1 = (bf16[2,2,128,256]{3,2,1,0:T(8,128)(2,1)S(1)}, bf16[2,2,128,256]{3,2,1,0:T(8,128)(2,1)S(1)}, u32[]{:S(2)}, u32[]{:S(2)}) collective-permute-start(bf16[2,2,128,256]{3,2,1,0:T(8,128)(2,1)S(1)} %pad_maximum_fusion.refs_0_), channel_id=1, source_target_pairs={{0,16},{1,17},{2,18},{3,19},{4,20},{5,21},{6,22},{7,23},{8,24},{9,... | collective-permute-start | bytes 786440 | tf_op jit(solution)/shard_map/ppermute | solution.py:50
  51.3 11.1 %copy-start = (bf16[1,3,256,256]{3,2,1,0:T(8,128)(2,1)S(1)}, bf16[1,3,256,256]{3,2,1,0:T(8,128)(2,1)}, u32[]{:S(2)}) copy-start(bf16[1,3,256,256]{3,2,1,0:T(8,128)(2,1)} %w0_ref.1) | copy-start | bytes 1179652
  65.3 11.7 %copy-start.1 = (bf16[2,128,256]{2,1,0:T(8,128)(2,1)S(1)}, bf16[2,128,256]{2,1,0:T(8,128)(2,1)}, u32[]{:S(2)}) copy-start(bf16[2,128,256]{2,1,0:T(8,128)(2,1)} %q_ref.1) | copy-start | bytes 393220
  65.3 25.7 %all-to-all-start.3 = ((bf16[8,96,256]{2,1,0:T(8,128)(2,1)}), bf16[8,96,256]{2,1,0:T(8,128)(2,1)S(1)}, u32[]{:S(2)}, u32[]{:S(2)}) async-start(bf16[8,96,256]{2,1,0:T(8,128)(2,1)} %get-tuple-element.29), calls=%async_computation.3 | async-start | bytes 786432 | tf_op jit(solution)/shard_map/all_to_all | solution.py:54
  77.0 0.7 copy-start.2
  78.2 6.2 %collective-permute-start.4 = (f32[2,128]{1,0:T(2,128)S(1)}, f32[2,128]{1,0:T(2,128)S(1)}, u32[]{:S(2)}, u32[]{:S(2)}) collective-permute-start(f32[2,128]{1,0:T(2,128)S(1)} %get-tuple-element.32), channel_id=1, source_target_pairs={{0,128},{64,192},{128,0},{192,64},{256,384},{320,448},{384,256},{4... | collective-permute-start | bytes 3080 | tf_op jit(solution)/shard_map/ppermute | solution.py:210
  84.4 6.4 %collective-permute-start.5 = (f32[2,128]{1,0:T(2,128)S(1)}, f32[2,128]{1,0:T(2,128)S(1)}, u32[]{:S(2)}, u32[]{:S(2)}) collective-permute-start(f32[2,128]{1,0:T(2,128)S(1)} %add.20), channel_id=1, source_target_pairs={{0,256},{64,320},{128,384},{192,448},{256,0},{320,64},{384,128},{4... | collective-permute-start | bytes 3080 | tf_op jit(solution)/shard_map/ppermute | solution.py:210
  91.8 11.4 %all-to-all-start.4 = ((bf16[8,96,256]{2,1,0:T(8,128)(2,1)}), bf16[8,96,256]{2,1,0:T(8,128)(2,1)S(1)}, u32[]{:S(2)}, u32[]{:S(2)}) async-start(bf16[8,96,256]{2,1,0:T(8,128)(2,1)} %shard_map.83), calls=%async_computation.4 | async-start | bytes 786432 | tf_op jit(solution)/shard_map/all_to_all | solution.py:54
  95.3 3.0 %collective-permute-start.6 = (f32[2,128]{1,0:T(2,128)S(1)}, f32[2,128]{1,0:T(2,128)S(1)}, u32[]{:S(2)}, u32[]{:S(2)}) collective-permute-start(f32[2,128]{1,0:T(2,128)S(1)} %add.21), channel_id=1, source_target_pairs={{0,64},{64,0},{128,192},{192,128},{256,320},{320,256},{384,448},{4... | collective-permute-start | bytes 3080 | tf_op jit(solution)/shard_map/ppermute | solution.py:210
